TPU v7x, 32 devices: a whole 2x2x4 slice. The times are simulated.
32 devices in a mesh: section: 4 (over y, x), dp: 8 (over z, core).
Axes of the slice: x: 2, y: 2, z: 4, core: 2. Of those that a mesh axis runs over, the one named last changes fastest.
Arguments:
- history: bfloat16 [12288, 3600], P('dp'), may hold values from -6 to 6
- targets: bfloat16 [12288, 720], P('dp'), may hold values from -6 to 6
- horizon: int32 [12288], P('dp'), may hold values from 96 to 720, as said below
- residual_cotangent: bfloat16 [12288, 3600], P('dp'), may hold values from -6 to 6
- coarse_entry: float32 [450, 512], P(None, 'dp'), may hold values from -0.25 to 0.25
- coarse_entry_bias: float32 [512], P('dp'), may hold values from -3 to 3
- coarse_middle: float32 [512, 512], P('dp'), may hold values from -0.25 to 0.25
- coarse_middle_bias: float32 [512], P('dp'), may hold values from -3 to 3
- coarse_upper: float32 [512, 512], P('dp'), may hold values from -0.25 to 0.25
- coarse_upper_bias: float32 [512], P('dp'), may hold values from -3 to 3
- coarse_head: float32 [512, 180], P('dp'), may hold values from -0.25 to 0.25
- coarse_head_bias: float32 [180], replicated, may hold values from -3 to 3
- fine_entry: float32 [3600, 512], P(None, 'dp'), may hold values from -0.09375 to 0.09375
- fine_entry_bias: float32 [512], P('dp'), may hold values from -3 to 3
- fine_middle: float32 [512, 512], P('dp'), may hold values from -0.25 to 0.25
- fine_middle_bias: float32 [512], P('dp'), may hold values from -3 to 3
- fine_upper: float32 [512, 512], P('dp'), may hold values from -0.25 to 0.25
- fine_upper_bias: float32 [512], P('dp'), may hold values from -3 to 3
- fine_head: float32 [512, 4320], P('dp'), may hold values from -0.25 to 0.25
- fine_head_bias: float32 [4320], replicated, may hold values from -3 to 3
Outputs:
- summed_prediction: float32 [12288, 720], P('dp')
- residual: bfloat16 [12288, 3600], P('dp')
- history_grad: bfloat16 [12288, 3600], P('dp')
- coarse_entry_grad: float32 [450, 512], P(None, 'dp')
- coarse_entry_bias_grad: float32 [512], P('dp')
- coarse_middle_grad: float32 [512, 512], P('dp')
- coarse_middle_bias_grad: float32 [512], P('dp')
- coarse_upper_grad: float32 [512, 512], P('dp')
- coarse_upper_bias_grad: float32 [512], P('dp')
- coarse_head_grad: float32 [512, 180], P('dp')
- coarse_head_bias_grad: float32 [180], replicated
- fine_entry_grad: float32 [3600, 512], P(None, 'dp')
- fine_entry_bias_grad: float32 [512], P('dp')
- fine_middle_grad: float32 [512, 512], P('dp')
- fine_middle_bias_grad: float32 [512], P('dp')
- fine_upper_grad: float32 [512, 512], P('dp')
- fine_upper_bias_grad: float32 [512], P('dp')
- fine_head_grad: float32 [512, 4320], P('dp')
- fine_head_bias_grad: float32 [4320], replicated
Inputs may be any that keep to these rules, and one draw needn't show every extreme that they name: Each window's horizon is one of 96, 336 and 720.
All inputs are finite; a program needn't handle non-finite values.
Results may differ from a plain program's by a relative error of at most 0.0093.
Values may be sent and summed in bfloat16 or wider, within the bound.
A program may use at most 320 MiB of HBM per device.

v0:
```python
import jax
import jax.numpy as jnp
from jax import lax
from jax.sharding import PartitionSpec as P

KERNEL_EXTENT = 8
DETAIL_SHARE = 24
MICRO = 6


def from_behind(block, axis, distance):
    devices = range(lax.axis_size(axis))
    route = [(i - distance, i) for i in devices if i - distance in devices]
    return lax.ppermute(block, axis, route)


def matmul(left_side, right_side):
    return jnp.dot(left_side, right_side, preferred_element_type=jnp.float32)


def contract_rows(left_side, right_side):
    return lax.dot_general(
        left_side, right_side, (((0,), (0,)), ((), ())), preferred_element_type=jnp.float32
    )


def times_transpose(left_side, right_side):
    return lax.dot_general(
        left_side, right_side, (((1,), (1,)), ((), ())), preferred_element_type=jnp.float32
    )


def interpolate_knots(theta_values, knot_divisor):
    later_part = jnp.concatenate([theta_values[:, 1:], theta_values[:, -1:]], axis=1)
    fraction = jnp.arange(knot_divisor, dtype=jnp.float32) / knot_divisor
    spread = theta_values[:, :, None] * (1.0 - fraction) + later_part[:, :, None] * fraction
    return spread.reshape(theta_values.shape[0], theta_values.shape[1] * knot_divisor)


def interpolate_adjoint(gradient, knot_divisor):
    grouped = gradient.reshape(gradient.shape[0], gradient.shape[1] // knot_divisor, knot_divisor)
    fraction = jnp.arange(knot_divisor, dtype=jnp.float32) / knot_divisor
    own_part = jnp.sum(grouped * (1.0 - fraction), axis=2)
    later_part = jnp.sum(grouped * fraction, axis=2)
    shifted = jnp.concatenate(
        [
            jnp.zeros_like(later_part[:, :1]),
            later_part[:, :-2],
            later_part[:, -2:-1] + later_part[:, -1:],
        ],
        axis=1,
    )
    return own_part + shifted


def block_forward(module_arguments, weights, head_bias, pool_size, knot_divisor, history_extent):
    (
        entry_weight,
        entry_offset,
        middle_weight,
        middle_offset,
        upper_weight,
        upper_offset,
        head_weight,
    ) = weights
    pooled = module_arguments
    if pool_size > 1:
        pooled = jnp.mean(
            module_arguments.reshape(module_arguments.shape[0], -1, pool_size), axis=2
        )
    hidden = pooled.astype(jnp.bfloat16)
    for w_layer, b_layer in (
        (entry_weight, entry_offset),
        (middle_weight, middle_offset),
        (upper_weight, upper_offset),
    ):
        hidden = jax.nn.gelu(matmul(hidden, w_layer) + b_layer.astype(jnp.float32)).astype(
            jnp.bfloat16
        )
    theta_values = matmul(hidden, head_weight) + head_bias
    history_reconstruction = theta_values[:, :history_extent]
    summed_prediction = theta_values[:, history_extent:]
    if knot_divisor > 1:
        history_reconstruction = interpolate_knots(history_reconstruction, knot_divisor)
        summed_prediction = interpolate_knots(summed_prediction, knot_divisor)
    return (module_arguments - history_reconstruction, summed_prediction)


def block_backward(module_arguments, weights, resid_grad, fore_grad, pool_size, knot_divisor):
    (
        entry_weight,
        entry_offset,
        middle_weight,
        middle_offset,
        upper_weight,
        upper_offset,
        head_weight,
    ) = weights
    pooled = module_arguments
    if pool_size > 1:
        pooled = jnp.mean(
            module_arguments.reshape(module_arguments.shape[0], -1, pool_size), axis=2
        )
    activations = [pooled.astype(jnp.bfloat16)]
    pullbacks = []
    for w_layer, b_layer in (
        (entry_weight, entry_offset),
        (middle_weight, middle_offset),
        (upper_weight, upper_offset),
    ):
        activated, cotangent_map = jax.vjp(
            jax.nn.gelu, matmul(activations[-1], w_layer) + b_layer.astype(jnp.float32)
        )
        activations.append(activated.astype(jnp.bfloat16))
        pullbacks.append(cotangent_map)
    back_part = resid_grad
    fore_part = fore_grad
    if knot_divisor > 1:
        back_part = interpolate_adjoint(resid_grad, knot_divisor)
        fore_part = interpolate_adjoint(fore_grad, knot_divisor)
    upstream = jnp.concatenate([-back_part, fore_part], axis=1).astype(jnp.bfloat16)
    gradients = [
        contract_rows(activations[3], upstream),
        jnp.sum(upstream.astype(jnp.float32), axis=0),
    ]
    downstream = times_transpose(upstream, head_weight)
    for layer_index, w_layer in ((2, upper_weight), (1, middle_weight), (0, entry_weight)):
        local_grad = pullbacks[layer_index](downstream)[0].astype(jnp.bfloat16)
        gradients = [
            contract_rows(activations[layer_index], local_grad),
            jnp.sum(local_grad.astype(jnp.float32), axis=0),
        ] + gradients
        downstream = times_transpose(local_grad, w_layer)
    if pool_size > 1:
        downstream = jnp.repeat(downstream / pool_size, pool_size, axis=1)
    return (resid_grad + downstream, tuple(gradients))


def flatten_shards(shard_set):
    return jnp.concatenate([shard_part.reshape(-1) for shard_part in shard_set])


def slot_bounds(in_dim, per_device, width, out_dim):
    lengths = [
        in_dim * per_device,
        per_device,
        per_device * width,
        per_device,
        per_device * width,
        per_device,
        per_device * out_dim,
    ]
    bounds = [0]
    for length in lengths:
        bounds.append(bounds[-1] + length)
    return bounds


def unpack_rows(flat_rows, in_dim, width, out_dim):
    row_count = flat_rows.shape[0]
    per_device = width // row_count
    bounds = slot_bounds(in_dim, per_device, width, out_dim)
    pieces = [flat_rows[:, bounds[slot_index] : bounds[slot_index + 1]] for slot_index in range(7)]
    entry_full = (
        pieces[0].reshape(row_count, in_dim, per_device).transpose(1, 0, 2).reshape(in_dim, width)
    )
    return (
        entry_full,
        pieces[1].reshape(width),
        pieces[2].reshape(width, width),
        pieces[3].reshape(width),
        pieces[4].reshape(width, width),
        pieces[5].reshape(width),
        pieces[6].reshape(width, out_dim),
    )


def pack_rows(full_set, row_count, padded):
    entry_full = full_set[0]
    in_dim, width = entry_full.shape
    per_device = width // row_count
    columns = [
        entry_full.reshape(in_dim, row_count, per_device)
        .transpose(1, 0, 2)
        .reshape(row_count, in_dim * per_device)
    ]
    columns = columns + [gradient.reshape(row_count, -1) for gradient in full_set[1:7]]
    packed = jnp.concatenate(columns, axis=1)
    return jnp.pad(packed, ((0, 0), (0, padded - packed.shape[1]))).reshape(-1)


def unpack_shard(flat_shard, in_dim, per_device, width, out_dim):
    bounds = slot_bounds(in_dim, per_device, width, out_dim)
    pieces = [flat_shard[bounds[slot_index] : bounds[slot_index + 1]] for slot_index in range(7)]
    return (
        pieces[0].reshape(in_dim, per_device),
        pieces[1],
        pieces[2].reshape(per_device, width),
        pieces[3],
        pieces[4].reshape(per_device, width),
        pieces[5],
        pieces[6].reshape(per_device, out_dim),
    )


def body(
    history,
    targets,
    horizon,
    residual_cotangent,
    coarse_entry,
    coarse_entry_bias,
    coarse_middle,
    coarse_middle_bias,
    coarse_upper,
    coarse_upper_bias,
    coarse_head,
    coarse_head_bias,
    fine_entry,
    fine_entry_bias,
    fine_middle,
    fine_middle_bias,
    fine_upper,
    fine_upper_bias,
    fine_head,
    fine_head_bias,
):
    broad_params = (
        coarse_entry,
        coarse_entry_bias,
        coarse_middle,
        coarse_middle_bias,
        coarse_upper,
        coarse_upper_bias,
        coarse_head,
    )
    detailed_params = (
        fine_entry,
        fine_entry_bias,
        fine_middle,
        fine_middle_bias,
        fine_upper,
        fine_upper_bias,
        fine_head,
    )
    dp_count = lax.axis_size("dp")
    per_device = coarse_middle.shape[0]
    width = coarse_middle.shape[1]
    pooled_dim = coarse_entry.shape[0]
    coarse_out = coarse_head.shape[1]
    fine_out = fine_head.shape[1]
    length_in = fine_entry.shape[0]
    length_out = fine_out - length_in
    coarse_back = length_in // DETAIL_SHARE
    coarse_size = per_device * (pooled_dim + 3 + 2 * width + coarse_out)
    fine_size = per_device * (length_in + 3 + 2 * width + fine_out)
    micro_rows = history.shape[0] // (2 * MICRO)
    local_samples = history.shape[0]
    section_index = lax.axis_index("section")
    first_block = section_index // 2 == 0
    horizon_mask = (jnp.arange(length_out, dtype=jnp.int32)[None, :] < horizon[:, None]).astype(
        jnp.float32
    )
    zero_rows = jnp.zeros((micro_rows, length_in), jnp.float32)
    zero_fore = jnp.zeros((micro_rows, length_out), jnp.float32)
    half_index = section_index % 2

    def own_half(source):
        shaped = source.reshape((2, MICRO, micro_rows) + source.shape[1:])
        return lax.dynamic_index_in_dim(shaped, half_index, 0, keepdims=False)

    my_series = own_half(history)
    my_targets = own_half(targets)
    my_mask = own_half(horizon_mask)
    my_cotangent = own_half(residual_cotangent)
    own_flat = jnp.where(
        first_block,
        jnp.pad(flatten_shards(broad_params), (0, fine_size - coarse_size)),
        flatten_shards(detailed_params),
    ).astype(jnp.bfloat16)
    gathered = lax.all_gather(own_flat, "dp", axis=0, tiled=True).reshape(dp_count, fine_size)
    coarse_weights = unpack_rows(gathered[:, :coarse_size], pooled_dim, width, coarse_out)
    fine_weights = unpack_rows(gathered, length_in, width, fine_out)
    incoming = (zero_rows, zero_fore)
    fine_inputs, kept_rows, kept_fore, kept_grad = ([], [], [], [])
    for tick_index in range(MICRO + 1):

        def coarse_step(received):
            if tick_index == MICRO:
                return (zero_rows, zero_fore, zero_fore)
            out_rows, out_fore = block_forward(
                my_series[tick_index].astype(jnp.float32),
                coarse_weights,
                coarse_head_bias,
                KERNEL_EXTENT,
                DETAIL_SHARE,
                coarse_back,
            )
            return (out_rows, out_fore, zero_fore)

        def fine_step(received):
            if tick_index == 0:
                return (zero_rows, zero_fore, zero_fore)
            out_rows, out_fore = block_forward(
                received[0], fine_weights, fine_head_bias, 1, 1, length_in
            )
            prediction_error = (
                received[1] + out_fore - my_targets[tick_index - 1].astype(jnp.float32)
            )
            return (out_rows, out_fore, my_mask[tick_index - 1] * prediction_error)

        out_rows, out_fore, fore_grad = lax.cond(first_block, coarse_step, fine_step, incoming)
        fine_inputs.append(incoming[0])
        kept_rows.append(out_rows)
        kept_fore.append(out_fore)
        kept_grad.append(fore_grad)
        if tick_index < MICRO:
            incoming = from_behind((out_rows, out_fore), "section", 2)
    regathered = lax.all_gather(own_flat, "dp", axis=0, tiled=True).reshape(dp_count, fine_size)
    coarse_weights = unpack_rows(regathered[:, :coarse_size], pooled_dim, width, coarse_out)
    fine_weights = unpack_rows(regathered, length_in, width, fine_out)
    coarse_totals = tuple((jnp.zeros(weight.shape, jnp.float32) for weight in coarse_weights)) + (
        jnp.zeros((coarse_out,), jnp.float32),
    )
    fine_totals = tuple((jnp.zeros(weight.shape, jnp.float32) for weight in fine_weights)) + (
        jnp.zeros((fine_out,), jnp.float32),
    )
    incoming = (zero_rows, zero_fore)
    signal_samples = []
    for tick_index in range(MICRO + 1):

        def coarse_back_step(received, totals_coarse, totals_fine):
            if tick_index == 0:
                return (zero_rows, zero_fore, totals_coarse, totals_fine)
            input_grad, gradients = block_backward(
                my_series[tick_index - 1].astype(jnp.float32),
                coarse_weights,
                received[0],
                received[1],
                KERNEL_EXTENT,
                DETAIL_SHARE,
            )
            updated = tuple((total + term for total, term in zip(totals_coarse, gradients)))
            return (input_grad, zero_fore, updated, totals_fine)

        def fine_back_step(received, totals_coarse, totals_fine):
            if tick_index == MICRO:
                return (zero_rows, zero_fore, totals_coarse, totals_fine)
            input_grad, gradients = block_backward(
                fine_inputs[tick_index + 1],
                fine_weights,
                my_cotangent[tick_index].astype(jnp.float32),
                kept_grad[tick_index + 1],
                1,
                1,
            )
            updated = tuple((total + term for total, term in zip(totals_fine, gradients)))
            return (input_grad, kept_grad[tick_index + 1], totals_coarse, updated)

        sent_rows, sent_fore, coarse_totals, fine_totals = lax.cond(
            first_block, coarse_back_step, fine_back_step, incoming, coarse_totals, fine_totals
        )
        if tick_index >= 1:
            signal_samples.append(sent_rows)
        if tick_index < MICRO:
            incoming = from_behind((sent_rows, sent_fore), "section", -2)
    coarse_flat = pack_rows(coarse_totals[:7], dp_count, fine_size)
    fine_flat = pack_rows(fine_totals[:7], dp_count, fine_size)
    own_grads = lax.psum_scatter(
        jnp.where(first_block, coarse_flat, fine_flat), "dp", scatter_dimension=0, tiled=True
    )
    zero_flat = jnp.zeros_like(own_grads)
    coarse_shard, fine_shard = lax.psum(
        (
            jnp.where(first_block, own_grads, zero_flat),
            jnp.where(first_block, zero_flat, own_grads),
        ),
        "section",
    )
    head_terms = (
        jnp.where(first_block, coarse_totals[7], 0.0),
        jnp.where(first_block, 0.0, fine_totals[7]),
    )
    my_rows = jnp.where(
        first_block, jnp.concatenate(signal_samples, axis=0), jnp.concatenate(kept_rows[1:], axis=0)
    ).astype(jnp.bfloat16)
    my_fore = jnp.concatenate(
        [
            jnp.where(first_block, kept_fore[micro_index], kept_fore[micro_index + 1])
            for micro_index in range(MICRO)
        ],
        axis=0,
    ).astype(jnp.bfloat16)
    whole_samples, stacked_predictions = (
        lax.all_gather(my_rows, "section", axis=0, tiled=True),
        lax.all_gather(my_fore, "section", axis=0, tiled=True),
    )
    history_grad = whole_samples[:local_samples]
    residual = whole_samples[local_samples:]
    summed_prediction = stacked_predictions[:local_samples].astype(
        jnp.float32
    ) + stacked_predictions[local_samples:].astype(jnp.float32)
    head_coarse, head_fine = lax.psum((head_terms[0], head_terms[1]), ("section", "dp"))
    coarse_grads = unpack_shard(coarse_shard, pooled_dim, per_device, width, coarse_out)
    fine_grads = unpack_shard(fine_shard, length_in, per_device, width, fine_out)
    return (
        summed_prediction,
        residual,
        history_grad,
        coarse_grads[0],
        coarse_grads[1],
        coarse_grads[2],
        coarse_grads[3],
        coarse_grads[4],
        coarse_grads[5],
        coarse_grads[6],
        head_coarse,
        fine_grads[0],
        fine_grads[1],
        fine_grads[2],
        fine_grads[3],
        fine_grads[4],
        fine_grads[5],
        fine_grads[6],
        head_fine,
    )


def solution(mesh):
    in_specs = (
        P("dp", None),
        P("dp", None),
        P("dp"),
        P("dp", None),
        P(None, "dp"),
        P("dp"),
        P("dp", None),
        P("dp"),
        P("dp", None),
        P("dp"),
        P("dp", None),
        P(),
        P(None, "dp"),
        P("dp"),
        P("dp", None),
        P("dp"),
        P("dp", None),
        P("dp"),
        P("dp", None),
        P(),
    )
    out_specs = (
        P("dp", None),
        P("dp", None),
        P("dp", None),
        P(None, "dp"),
        P("dp"),
        P("dp", None),
        P("dp"),
        P("dp", None),
        P("dp"),
        P("dp", None),
        P(),
        P(None, "dp"),
        P("dp"),
        P("dp", None),
        P("dp"),
        P("dp", None),
        P("dp"),
        P("dp", None),
        P(),
    )
    return jax.shard_map(body, mesh=mesh, in_specs=in_specs, out_specs=out_specs, check_vma=False)
```

profile of v0, /device:TPU:8, one launch (start us, length us, event | category | flops | bytes accessed | tf_op | source)
XLA Modules:
  0.0 1884.3 jit_solution(7527564626247275246)
XLA Ops:
  12.5 7.4 concatenate.143
  21.7 4.0 broadcast.853
  25.7 18.4 dynamic-update-slice
  44.5 14.8 copy.323
  59.4 14.7 copy.343
  74.1 9.7 constant_dynamic-slice_fusion
  83.8 8.3 copy.324
  92.1 143.6 %all-reduce.10.cloned.1.call-done = bf16[4580864]{0:T(1024)(128)(2,1)} async-done(((bf16[4580864]{0:T(1024)(128)(2,1)}), bf16[4580864]{0:T(1024)(128)(2,1)}) %all-reduce.10.cloned.1.call-update) | async-done | bytes 9161744
  235.7 14.2 reshape.664
  258.6 8.7 conditional.14
  281.8 5.9 slice.630
  289.7 5.7 reshape.741
  295.4 10.1 reshape.673
  305.5 8.2 copy.329
  313.8 6.3 reshape.743
  320.1 9.9 reshape.680
  330.0 10.8 conditional.15
  340.8 4.1 constant_dynamic-update-slice_fusion.11
  345.0 4.9 collective-permute-start.2
  349.8 8.2 copy.344
  358.1 12.4 conditional.21
  358.3 4.7 broadcast_in_dim.81
  371.8 22.4 %collective-permute-start.3 = (f32[128,720]{0,1:T(8,128)S(1)}, f32[128,720]{0,1:T(8,128)S(1)}, u32[]{:S(2)}, u32[]{:S(2)}) collective-permute-start(f32[128,720]{0,1:T(8,128)S(1)} %get-tuple-element.1479), channel_id=1, source_target_pairs={{0,16},{8,24},{1,17},{9,25},{2,18},{10,26},{3,19},{11,27},{4,20},{... | collective-permute-start | bytes 1105928 | tf_op jit(solution)/shard_map/ppermute | solution.py:14
  395.5 6.3 collective-permute-done.3
  401.8 12.5 conditional.16
  418.2 13.1 collective-permute-start.4
  431.3 7.9 collective-permute-done.13
  439.3 36.7 %conditional.22 = (f32[128,720]{1,0:T(8,128)}, f32[450,512]{1,0:T(8,128)S(1)}, f32[512]{0:T(512)}, f32[512,512]{1,0:T(8,128)}, f32[512]{0:T(512)}, /*index=5*/f3...) conditional(s32[]{:T(128)} %convert_element_type.1039, ...), branch_computations={%region_26.31_spmd, %region_31.41_spmd} | conditional | flops 2971315712 | bytes 122844944 | solution.py:360
  466.0 9.2 copy.351
  476.0 4.0 constant_dynamic-update-slice_fusion.5
  481.2 23.8 %collective-permute-start.5 = (f32[128,720]{0,1:T(8,128)}, f32[128,720]{0,1:T(8,128)}, u32[]{:S(2)}, u32[]{:S(2)}) collective-permute-start(f32[128,720]{0,1:T(8,128)} %get-tuple-element.1482), channel_id=1, source_target_pairs={{0,16},{8,24},{1,17},{9,25},{2,18},{10,26},{3,19},{11,27},{4,20},{... | collective-permute-start | bytes 1105928 | tf_op jit(solution)/shard_map/ppermute | solution.py:14
  511.7 37.7 %conditional.17 = (f32[128,720]{0,1:T(8,128)}, f32[128,720]{1,0:T(8,128)}, f32[128,3600]{0,1:T(8,128)}, f32[128,3600]{0,1:T(8,128)}) conditional(s32[]{:T(128)} %convert_element_type.1039, (f32[128,3600]{0,1:T(8,128)}, bf16[3600,512]{0,1:T(8,128)(2,1)}, bf16[512]{0:T(512)(128)(2,1)}, bf16[512,512]{1,0:T(8,128)(2,1)}, bf16[512]{0:T(512)(128)(2,1)}, ...), branch_computations={%region_9.10_spmd, %region_10.12_spmd} | conditional | flops 1175657984 | bytes 23646112 | solution.py:312
  549.5 3.9 constant_dynamic-update-slice_fusion.9
  555.9 26.7 %conditional.23 = (f32[128,720]{1,0:T(8,128)}, f32[450,512]{1,0:T(8,128)S(1)}, f32[512]{0:T(512)}, f32[512,512]{1,0:T(8,128)}, f32[512]{0:T(512)}, /*index=5*/f3...) conditional(s32[]{:T(128)} %convert_element_type.1039, ...), branch_computations={%region_41.46_spmd, %region_46.56_spmd} | conditional | flops 2971315712 | bytes 135138336 | solution.py:360
  582.7 3.9 constant_dynamic-update-slice_fusion.4
  587.9 32.8 %collective-permute-start.7 = (f32[128,720]{0,1:T(8,128)}, f32[128,720]{0,1:T(8,128)}, u32[]{:S(2)}, u32[]{:S(2)}) collective-permute-start(f32[128,720]{0,1:T(8,128)} %get-tuple-element.1485), channel_id=1, source_target_pairs={{0,16},{8,24},{1,17},{9,25},{2,18},{10,26},{3,19},{11,27},{4,20},{... | collective-permute-start | bytes 1105928 | tf_op jit(solution)/shard_map/ppermute | solution.py:14
  626.6 37.5 %conditional.18 = (f32[128,720]{0,1:T(8,128)}, f32[128,720]{1,0:T(8,128)}, f32[128,3600]{0,1:T(8,128)}, f32[128,3600]{0,1:T(8,128)}) conditional(s32[]{:T(128)} %convert_element_type.1039, (f32[128,3600]{0,1:T(8,128)}, bf16[3600,512]{0,1:T(8,128)(2,1)}, bf16[512]{0:T(512)(128)(2,1)}, bf16[512,512]{1,0:T(8,128)(2,1)}, bf16[512]{0:T(512)(128)(2,1)}, ...), branch_computations={%region_12.13_spmd, %region_13.15_spmd} | conditional | flops 1175657984 | bytes 23646112 | solution.py:312
  664.2 3.9 constant_dynamic-update-slice_fusion.8
  670.6 35.4 %conditional.24 = (f32[128,720]{1,0:T(8,128)}, f32[450,512]{1,0:T(8,128)S(1)}, f32[512]{0:T(512)}, f32[512,512]{1,0:T(8,128)}, f32[512]{0:T(512)}, /*index=5*/f3...) conditional(s32[]{:T(128)} %convert_element_type.1039, ...), branch_computations={%region_56.61_spmd, %region_61.71_spmd} | conditional | flops 2971315712 | bytes 135138336 | solution.py:360
  711.2 24.3 %collective-permute-start.9 = (f32[128,720]{0,1:T(8,128)}, f32[128,720]{0,1:T(8,128)}, u32[]{:S(2)}, u32[]{:S(2)}) collective-permute-start(f32[128,720]{0,1:T(8,128)} %get-tuple-element.1488), channel_id=1, source_target_pairs={{0,16},{8,24},{1,17},{9,25},{2,18},{10,26},{3,19},{11,27},{4,20},{... | collective-permute-start | bytes 1105928 | tf_op jit(solution)/shard_map/ppermute | solution.py:14
  740.9 37.6 %conditional.19 = (f32[128,720]{0,1:T(8,128)}, f32[128,720]{1,0:T(8,128)}, f32[128,3600]{0,1:T(8,128)}, f32[128,3600]{0,1:T(8,128)}) conditional(s32[]{:T(128)} %convert_element_type.1039, (f32[128,3600]{0,1:T(8,128)}, bf16[3600,512]{0,1:T(8,128)(2,1)}, bf16[512]{0:T(512)(128)(2,1)}, bf16[512,512]{1,0:T(8,128)(2,1)}, bf16[512]{0:T(512)(128)(2,1)}, ...), branch_computations={%region_15.16_spmd, %region_16.18_spmd} | conditional | flops 1175657984 | bytes 23646112 | solution.py:312
  784.9 33.4 %conditional.25 = (f32[128,720]{1,0:T(8,128)}, f32[450,512]{1,0:T(8,128)S(1)}, f32[512]{0:T(512)}, f32[512,512]{1,0:T(8,128)}, f32[512]{0:T(512)}, /*index=5*/f3...) conditional(s32[]{:T(128)} %convert_element_type.1039, ...), branch_computations={%region_71.76_spmd, %region_76.86_spmd} | conditional | flops 2971315712 | bytes 135138336 | solution.py:360
  823.5 26.4 %collective-permute-start.11 = (f32[128,720]{0,1:T(8,128)}, f32[128,720]{0,1:T(8,128)}, u32[]{:S(2)}, u32[]{:S(2)}) collective-permute-start(f32[128,720]{0,1:T(8,128)} %get-tuple-element.1491), channel_id=1, source_target_pairs={{0,16},{8,24},{1,17},{9,25},{2,18},{10,26},{3,19},{11,27},{4,20},{... | collective-permute-start | bytes 1105928 | tf_op jit(solution)/shard_map/ppermute | solution.py:14
  855.5 36.2 %collective-permute-done.21 = f32[128,720]{0,1:T(8,128)} collective-permute-done((f32[128,720]{0,1:T(8,128)}, f32[128,720]{0,1:T(8,128)}, u32[]{:S(2)}, u32[]{:S(2)}) %collective-permute-start.21) | collective-permute-done | bytes 368672 | tf_op jit(solution)/shard_map/ppermute | solution.py:14
  891.7 57.2 %conditional.26 = (f32[128,3600]{0,1:T(8,128)}, f32[450,512]{1,0:T(8,128)S(1)}, f32[512]{0:T(512)}, f32[512,512]{1,0:T(8,128)}, f32[512]{0:T(512)}, /*index=5*/f...) conditional(s32[]{:T(128)} %convert_element_type.1039, ...), branch_computations={%region_86.91_spmd, %region_91.101_spmd} | conditional | flops 2972329472 | bytes 193001680 | solution.py:360
  922.2 11.9 reshape.739
  934.1 8.3 reshape.605
  952.3 8.5 copy.377
  960.8 11.3 copy.378
  972.1 11.6 reshape.692
  983.7 5.3 constant_dynamic-update-slice_fusion.15
  990.4 4.6 dynamic-update-slice.3
  1000.0 24.4 %dynamic-update-slice.7 = f32[8,572608]{1,0:T(8,128)} dynamic-update-slice(f32[8,572608]{1,0:T(8,128)} %dynamic-update-slice.6, f32[8,276480]{1,0:T(8,128)} %get-tuple-element.1612, s32[]{} %constant.525, s32[]{} %constant.531) | dynamic-update-slice | bytes 17694724 | tf_op jit(solution)/shard_map/concatenate | solution.py:188
  1025.4 20.8 %conditional.27 = (bf16[128,3600]{0,1:T(8,128)(2,1)}, f32[450,512]{1,0:T(8,128)S(1)}, f32[512]{0:T(512)}, f32[512,512]{1,0:T(8,128)}, f32[512]{0:T(512)}, /*inde...) conditional(s32[]{:T(128)} %convert_element_type.1039, (f32[450,512]{1,0:T(8,128)S(1)}, ...), branch_computations={%region_101.102_spmd, %region_102.112_spmd} | conditional | flops 639756352 | bytes 25885700 | solution.py:360
  1070.4 9.4 pad_select_fusion
  1079.8 19.3 %select_n.115 = f32[4580864]{0:T(1024)} reshape(f32[8,572608]{1,0:T(8,128)} %pad_select_fusion) | data formatting | bytes 36646912 | tf_op jit(solution)/shard_map/jit(_where)/select_n | solution.py:370
  1105.8 378.1 %all-reduce.12.cloned.1.call-done = f32[4580864]{0:T(1024)} async-done(((f32[4580864]{0:T(1024)}), f32[4580864]{0:T(1024)}) %all-reduce.12.cloned.1.call-update) | async-done | bytes 18323472
  1483.9 4.5 dynamic-slice_select_fusion
  1495.0 5.9 select_convert_fusion
  1502.3 39.3 %all-reduce.4 = (f32[180]{0:T(256)}, f32[4320]{0:T(1024)}) all-reduce(f32[180]{0:T(256)S(1)} %broadcast_select_fusion.1, f32[4320]{0:T(1024)S(1)} %broadcast_select_fusion), channel_id=1, replica_groups=mesh['section'=4,'dp'=8] {'section','dp'}, use_global_device_ids=true, to_apply=%region_114.115 | all-reduce | flops 4500 | bytes 36000 | tf_op jit(solution)/shard_map/psum | solution.py:403
  1542.3 5.0 convert_add_fusion
  1547.3 109.7 %all-reduce.14.cloned.1.call-done = (f32[572608]{0:T(1024)}, f32[572608]{0:T(1024)}) async-done(((f32[572608]{0:T(1024)}, f32[572608]{0:T(1024)}), (f32[572608]{0:T(1024)}, f32[572608]{0:T(1024)})) %all-reduce.14.cloned.1.call-update) | async-done | bytes 4580880 | tf_op jit(solution)/shard_map/psum | solution.py:373
  1676.7 185.3 %all-gather.5.cloned.1.call-done = bf16[3072,3600]{0,1:T(8,128)(2,1)} async-done(((bf16[768,3600]{0,1:T(8,128)(2,1)}), bf16[3072,3600]{0,1:T(8,128)(2,1)}) %all-gather.5.cloned.1.call-update) | async-done | bytes 22118416 | tf_op jit(solution)/shard_map/all_gather | solution.py:395
  1862.0 15.5 fusion.1090
  (670 shorter events, 456.1 us)
Async XLA Ops:
  7.2 228.5 %all-reduce.10.cloned.1.call-start = ((), (), s32[]{:S(2)}) async-start(), calls=%async_computation.2 | async-start | bytes 18325504
  10.5 9.4 copy-start.157
  10.5 9.4 copy-start.158
  10.5 9.4 copy-start.159
  44.2 1439.7 %all-reduce.12.cloned.1.call-start = ((), (), s32[]{:S(2)}) async-start(), calls=%async_computation.3 | async-start | bytes 36651008
  254.8 184.5 %copy-start.98 = (bf16[512]{0:T(512)(128)(2,1)}, bf16[512]{0:T(512)(128)(2,1)S(1)}, u32[]{:S(2)}) copy-start(bf16[512]{0:T(512)(128)(2,1)S(1)} %reshape.667) | copy-start | bytes 3076
  254.9 184.4 %copy-start.104 = (bf16[512]{0:T(512)(128)(2,1)}, bf16[512]{0:T(512)(128)(2,1)S(1)}, u32[]{:S(2)}) copy-start(bf16[512]{0:T(512)(128)(2,1)S(1)} %reshape.669) | copy-start | bytes 3076
  254.9 184.3 %copy-start.110 = (bf16[512]{0:T(512)(128)(2,1)}, bf16[512]{0:T(512)(128)(2,1)S(1)}, u32[]{:S(2)}) copy-start(bf16[512]{0:T(512)(128)(2,1)S(1)} %reshape.671) | copy-start | bytes 3076
  267.3 8.2 copy-start.48
  267.3 62.7 %collective-permute-start = (f32[128,3600]{0,1:T(8,128)}, f32[128,3600]{0,1:T(8,128)}, u32[]{:S(2)}, u32[]{:S(2)}) collective-permute-start(f32[128,3600]{0,1:T(8,128)} %get-tuple-element.1478), channel_id=1, source_target_pairs={{0,16},{8,24},{1,17},{9,25},{2,18},{10,26},{3,19},{11,27},{4,20},{... | collective-permute-start | bytes 5529608 | tf_op jit(solution)/shard_map/ppermute | solution.py:14
  275.5 54.6 %copy-start.35 = (bf16[1,6,128,720]{2,3,1,0:T(8,128)(2,1)}, bf16[1,6,128,720]{2,3,1,0:T(8,128)(2,1)S(1)}, u32[]{:S(2)}) copy-start(bf16[1,6,128,720]{2,3,1,0:T(8,128)(2,1)S(1)} %copy.331) | copy-start | bytes 3317764
  275.5 54.5 %collective-permute-start.1 = (f32[128,720]{0,1:T(8,128)S(1)}, f32[128,720]{0,1:T(8,128)S(1)}, u32[]{:S(2)}, u32[]{:S(2)}) collective-permute-start(f32[128,720]{0,1:T(8,128)S(1)} %get-tuple-element.1477), channel_id=1, source_target_pairs={{0,16},{8,24},{1,17},{9,25},{2,18},{10,26},{3,19},{11,27},{4,20},{... | collective-permute-start | bytes 1105928 | tf_op jit(solution)/shard_map/ppermute | solution.py:14
  281.8 6.2 copy-start.40
  287.8 151.5 %copy-start.116 = (bf16[512]{0:T(512)(128)(2,1)}, bf16[512]{0:T(512)(128)(2,1)S(1)}, u32[]{:S(2)}) copy-start(bf16[512]{0:T(512)(128)(2,1)S(1)} %reshape.675) | copy-start | bytes 3076
  287.9 151.4 %copy-start.117 = (bf16[512]{0:T(512)(128)(2,1)}, bf16[512]{0:T(512)(128)(2,1)S(1)}, u32[]{:S(2)}) copy-start(bf16[512]{0:T(512)(128)(2,1)S(1)} %reshape.677) | copy-start | bytes 3076
  287.9 70.2 %copy-start.121 = (bf16[512]{0:T(512)(128)(2,1)}, bf16[512]{0:T(512)(128)(2,1)S(1)}, u32[]{:S(2)}) copy-start(bf16[512]{0:T(512)(128)(2,1)S(1)} %reshape.679) | copy-start | bytes 3076
  288.2 151.1 %copy-start.6 = (bf16[512,512]{1,0:T(8,128)(2,1)}, bf16[512,512]{1,0:T(8,128)(2,1)S(1)}, u32[]{:S(2)}) copy-start(bf16[512,512]{1,0:T(8,128)(2,1)S(1)} %reshape.676) | copy-start | bytes 1572868
  289.7 68.4 %copy-start.14 = (bf16[512,512]{1,0:T(8,128)(2,1)}, bf16[512,512]{1,0:T(8,128)(2,1)S(1)}, u32[]{:S(2)}) copy-start(bf16[512,512]{1,0:T(8,128)(2,1)S(1)} %reshape.678) | copy-start | bytes 1572868
  320.1 9.9 copy-start.66
  320.1 9.9 copy-start.164
  340.8 30.9 %copy-start.38 = (f32[128,720]{0,1:T(8,128)}, f32[128,720]{0,1:T(8,128)S(1)}, u32[]{:S(2)}) copy-start(f32[128,720]{0,1:T(8,128)S(1)} %get-tuple-element.1479) | copy-start | bytes 1105924
  345.0 56.9 %collective-permute-start.2 = (f32[128,3600]{0,1:T(8,128)}, f32[128,3600]{0,1:T(8,128)}, u32[]{:S(2)}, u32[]{:S(2)}) collective-permute-start(f32[128,3600]{0,1:T(8,128)} %get-tuple-element.3730), channel_id=1, source_target_pairs={{0,16},{8,24},{1,17},{9,25},{2,18},{10,26},{3,19},{11,27},{4,20},{... | collective-permute-start | bytes 5529608 | tf_op jit(solution)/shard_map/ppermute | solution.py:14
  370.5 31.3 %copy-start.62 = (f32[4320]{0:T(1024)}, f32[4320]{0:T(1024)S(1)}, u32[]{:S(2)}) copy-start(f32[4320]{0:T(1024)S(1)} %get-tuple-element.1504) | copy-start | bytes 51844
  370.5 31.3 %copy-start.135 = (f32[512]{0:T(512)}, f32[512]{0:T(512)S(1)}, u32[]{:S(2)}) copy-start(f32[512]{0:T(512)S(1)} %get-tuple-element.1500) | copy-start | bytes 6148
  370.5 68.7 %collective-permute-start.12 = (f32[128,3600]{0,1:T(8,128)}, f32[128,3600]{0,1:T(8,128)}, u32[]{:S(2)}, u32[]{:S(2)}) collective-permute-start(f32[128,3600]{0,1:T(8,128)} %get-tuple-element.1505), channel_id=1, source_target_pairs={{16,0},{24,8},{17,1},{25,9},{18,2},{26,10},{19,3},{27,11},{20,4},{... | collective-permute-start | bytes 5529608 | tf_op jit(solution)/shard_map/ppermute | solution.py:14
  371.8 30.0 %collective-permute-start.3 = (f32[128,720]{0,1:T(8,128)S(1)}, f32[128,720]{0,1:T(8,128)S(1)}, u32[]{:S(2)}, u32[]{:S(2)}) collective-permute-start(f32[128,720]{0,1:T(8,128)S(1)} %get-tuple-element.1479), channel_id=1, source_target_pairs={{0,16},{8,24},{1,17},{9,25},{2,18},{10,26},{3,19},{11,27},{4,20},{... | collective-permute-start | bytes 1105928 | tf_op jit(solution)/shard_map/ppermute | solution.py:14
  394.2 45.0 %collective-permute-start.13 = (f32[128,720]{0,1:T(8,128)}, f32[128,720]{0,1:T(8,128)}, u32[]{:S(2)}, u32[]{:S(2)}) collective-permute-start(f32[128,720]{0,1:T(8,128)} %get-tuple-element.1506), channel_id=1, source_target_pairs={{16,0},{24,8},{17,1},{25,9},{18,2},{26,10},{19,3},{27,11},{20,4},{... | collective-permute-start | bytes 1105928 | tf_op jit(solution)/shard_map/ppermute | solution.py:14
  414.3 24.9 %copy-start.122 = (bf16[512]{0:T(512)(128)(2,1)S(1)}, bf16[512]{0:T(512)(128)(2,1)}, u32[]{:S(2)}) copy-start(bf16[512]{0:T(512)(128)(2,1)} %copy-done.121) | copy-start | bytes 3076
  418.2 93.5 %collective-permute-start.4 = (f32[128,3600]{0,1:T(8,128)}, f32[128,3600]{0,1:T(8,128)}, u32[]{:S(2)}, u32[]{:S(2)}) collective-permute-start(f32[128,3600]{0,1:T(8,128)} %get-tuple-element.3728), channel_id=1, source_target_pairs={{0,16},{8,24},{1,17},{9,25},{2,18},{10,26},{3,19},{11,27},{4,20},{... | collective-permute-start | bytes 5529608 | tf_op jit(solution)/shard_map/ppermute | solution.py:14
  479.9 76.0 %collective-permute-start.14 = (f32[128,3600]{0,1:T(8,128)}, f32[128,3600]{0,1:T(8,128)}, u32[]{:S(2)}, u32[]{:S(2)}) collective-permute-start(f32[128,3600]{0,1:T(8,128)} %get-tuple-element.3738), channel_id=1, source_target_pairs={{16,0},{24,8},{17,1},{25,9},{18,2},{26,10},{19,3},{27,11},{20,4},{... | collective-permute-start | bytes 5529608 | tf_op jit(solution)/shard_map/ppermute | solution.py:14
  481.2 30.5 %collective-permute-start.5 = (f32[128,720]{0,1:T(8,128)}, f32[128,720]{0,1:T(8,128)}, u32[]{:S(2)}, u32[]{:S(2)}) collective-permute-start(f32[128,720]{0,1:T(8,128)} %get-tuple-element.1482), channel_id=1, source_target_pairs={{0,16},{8,24},{1,17},{9,25},{2,18},{10,26},{3,19},{11,27},{4,20},{... | collective-permute-start | bytes 1105928 | tf_op jit(solution)/shard_map/ppermute | solution.py:14
  507.0 48.9 %collective-permute-start.15 = (f32[128,720]{0,1:T(8,128)}, f32[128,720]{0,1:T(8,128)}, u32[]{:S(2)}, u32[]{:S(2)}) collective-permute-start(f32[128,720]{0,1:T(8,128)} %copy.352), channel_id=1, source_target_pairs={{16,0},{24,8},{17,1},{25,9},{18,2},{26,10},{19,3},{27,11},{20,4},{... | collective-permute-start | bytes 1105928 | tf_op jit(solution)/shard_map/ppermute | solution.py:14
  553.4 73.2 %collective-permute-start.6 = (f32[128,3600]{0,1:T(8,128)}, f32[128,3600]{0,1:T(8,128)}, u32[]{:S(2)}, u32[]{:S(2)}) collective-permute-start(f32[128,3600]{0,1:T(8,128)} %get-tuple-element.3726), channel_id=1, source_target_pairs={{0,16},{8,24},{1,17},{9,25},{2,18},{10,26},{3,19},{11,27},{4,20},{... | collective-permute-start | bytes 5529608 | tf_op jit(solution)/shard_map/ppermute | solution.py:14
  556.3 5.8 copy-start.106
  556.3 5.9 copy-start.69
  586.6 84.0 %collective-permute-start.16 = (f32[128,3600]{0,1:T(8,128)}, f32[128,3600]{0,1:T(8,128)}, u32[]{:S(2)}, u32[]{:S(2)}) collective-permute-start(f32[128,3600]{0,1:T(8,128)} %get-tuple-element.3736), channel_id=1, source_target_pairs={{16,0},{24,8},{17,1},{25,9},{18,2},{26,10},{19,3},{27,11},{20,4},{... | collective-permute-start | bytes 5529608 | tf_op jit(solution)/shard_map/ppermute | solution.py:14
  587.9 38.7 %collective-permute-start.7 = (f32[128,720]{0,1:T(8,128)}, f32[128,720]{0,1:T(8,128)}, u32[]{:S(2)}, u32[]{:S(2)}) collective-permute-start(f32[128,720]{0,1:T(8,128)} %get-tuple-element.1485), channel_id=1, source_target_pairs={{0,16},{8,24},{1,17},{9,25},{2,18},{10,26},{3,19},{11,27},{4,20},{... | collective-permute-start | bytes 1105928 | tf_op jit(solution)/shard_map/ppermute | solution.py:14
  622.5 48.1 %collective-permute-start.17 = (f32[128,720]{0,1:T(8,128)}, f32[128,720]{0,1:T(8,128)}, u32[]{:S(2)}, u32[]{:S(2)}) collective-permute-start(f32[128,720]{0,1:T(8,128)} %copy.357), channel_id=1, source_target_pairs={{16,0},{24,8},{17,1},{25,9},{18,2},{26,10},{19,3},{27,11},{20,4},{... | collective-permute-start | bytes 1105928 | tf_op jit(solution)/shard_map/ppermute | solution.py:14
  668.1 72.8 %collective-permute-start.8 = (f32[128,3600]{0,1:T(8,128)}, f32[128,3600]{0,1:T(8,128)}, u32[]{:S(2)}, u32[]{:S(2)}) collective-permute-start(f32[128,3600]{0,1:T(8,128)} %get-tuple-element.3724), channel_id=1, source_target_pairs={{0,16},{8,24},{1,17},{9,25},{2,18},{10,26},{3,19},{11,27},{4,20},{... | collective-permute-start | bytes 5529608 | tf_op jit(solution)/shard_map/ppermute | solution.py:14
  679.7 5.8 copy-start.107
  679.7 5.8 copy-start.70
  709.9 75.0 %collective-permute-start.18 = (f32[128,3600]{0,1:T(8,128)}, f32[128,3600]{0,1:T(8,128)}, u32[]{:S(2)}, u32[]{:S(2)}) collective-permute-start(f32[128,3600]{0,1:T(8,128)} %get-tuple-element.3734), channel_id=1, source_target_pairs={{16,0},{24,8},{17,1},{25,9},{18,2},{26,10},{19,3},{27,11},{20,4},{... | collective-permute-start | bytes 5529608 | tf_op jit(solution)/shard_map/ppermute | solution.py:14
  711.2 29.7 %collective-permute-start.9 = (f32[128,720]{0,1:T(8,128)}, f32[128,720]{0,1:T(8,128)}, u32[]{:S(2)}, u32[]{:S(2)}) collective-permute-start(f32[128,720]{0,1:T(8,128)} %get-tuple-element.1488), channel_id=1, source_target_pairs={{0,16},{8,24},{1,17},{9,25},{2,18},{10,26},{3,19},{11,27},{4,20},{... | collective-permute-start | bytes 1105928 | tf_op jit(solution)/shard_map/ppermute | solution.py:14
  737.4 47.5 %collective-permute-start.19 = (f32[128,720]{0,1:T(8,128)}, f32[128,720]{0,1:T(8,128)}, u32[]{:S(2)}, u32[]{:S(2)}) collective-permute-start(f32[128,720]{0,1:T(8,128)} %copy.362), channel_id=1, source_target_pairs={{16,0},{24,8},{17,1},{25,9},{18,2},{26,10},{19,3},{27,11},{20,4},{... | collective-permute-start | bytes 1105928 | tf_op jit(solution)/shard_map/ppermute | solution.py:14
  782.3 72.3 %collective-permute-start.10 = (f32[128,3600]{0,1:T(8,128)}, f32[128,3600]{0,1:T(8,128)}, u32[]{:S(2)}, u32[]{:S(2)}) collective-permute-start(f32[128,3600]{0,1:T(8,128)} %get-tuple-element.3722), channel_id=1, source_target_pairs={{0,16},{8,24},{1,17},{9,25},{2,18},{10,26},{3,19},{11,27},{4,20},{... | collective-permute-start | bytes 5529608 | tf_op jit(solution)/shard_map/ppermute | solution.py:14
  792.0 5.8 copy-start.108
  792.0 5.9 copy-start.71
  822.2 69.5 %collective-permute-start.20 = (f32[128,3600]{0,1:T(8,128)}, f32[128,3600]{0,1:T(8,128)}, u32[]{:S(2)}, u32[]{:S(2)}) collective-permute-start(f32[128,3600]{0,1:T(8,128)} %get-tuple-element.3732), channel_id=1, source_target_pairs={{16,0},{24,8},{17,1},{25,9},{18,2},{26,10},{19,3},{27,11},{20,4},{... | collective-permute-start | bytes 5529608 | tf_op jit(solution)/shard_map/ppermute | solution.py:14
  823.5 31.1 %collective-permute-start.11 = (f32[128,720]{0,1:T(8,128)}, f32[128,720]{0,1:T(8,128)}, u32[]{:S(2)}, u32[]{:S(2)}) collective-permute-start(f32[128,720]{0,1:T(8,128)} %get-tuple-element.1491), channel_id=1, source_target_pairs={{0,16},{8,24},{1,17},{9,25},{2,18},{10,26},{3,19},{11,27},{4,20},{... | collective-permute-start | bytes 1105928 | tf_op jit(solution)/shard_map/ppermute | solution.py:14
  851.8 39.9 %collective-permute-start.21 = (f32[128,720]{0,1:T(8,128)}, f32[128,720]{0,1:T(8,128)}, u32[]{:S(2)}, u32[]{:S(2)}) collective-permute-start(f32[128,720]{0,1:T(8,128)} %copy.367), channel_id=1, source_target_pairs={{16,0},{24,8},{17,1},{25,9},{18,2},{26,10},{19,3},{27,11},{20,4},{... | collective-permute-start | bytes 1105928 | tf_op jit(solution)/shard_map/ppermute | solution.py:14
  855.5 36.2 %copy-start.36 = (bf16[128,3600]{0,1:T(8,128)(2,1)}, bf16[128,3600]{0,1:T(8,128)(2,1)S(1)}, u32[]{:S(2)}) copy-start(bf16[128,3600]{0,1:T(8,128)(2,1)S(1)} %get-tuple-element.1598) | copy-start | bytes 2764804
  855.5 36.2 %copy-start.46 = (f32[128,720]{0,1:T(8,128)}, f32[128,720]{0,1:T(8,128)S(1)}, u32[]{:S(2)}) copy-start(f32[128,720]{0,1:T(8,128)S(1)} %get-tuple-element.1494) | copy-start | bytes 1105924
  898.0 5.8 copy-start.109
  898.0 5.9 copy-start.72
  949.5 75.9 %collective-permute-start.22 = (f32[128,3600]{0,1:T(8,128)}, f32[128,3600]{0,1:T(8,128)S(1)}, u32[]{:S(2)}, u32[]{:S(2)}) collective-permute-start(f32[128,3600]{0,1:T(8,128)} %get-tuple-element.1587), channel_id=1, source_target_pairs={{16,0},{24,8},{17,1},{25,9},{18,2},{26,10},{19,3},{27,11},{20,4},{... | collective-permute-start | bytes 5529608 | tf_op jit(solution)/shard_map/ppermute | solution.py:14
  950.8 74.6 %collective-permute-start.23 = (f32[128,720]{0,1:T(8,128)}, f32[128,720]{0,1:T(8,128)}, u32[]{:S(2)}, u32[]{:S(2)}) collective-permute-start(f32[128,720]{0,1:T(8,128)} %get-tuple-element.3624), channel_id=1, source_target_pairs={{16,0},{24,8},{17,1},{25,9},{18,2},{26,10},{19,3},{27,11},{20,4},{... | collective-permute-start | bytes 1105928 | tf_op jit(solution)/shard_map/ppermute | solution.py:14
  983.7 11.3 copy-start.146
  989.1 9.6 copy-start.148
  1000.0 25.4 %copy-start.99 = (bf16[512]{0:T(512)(128)(2,1)S(1)}, bf16[512]{0:T(512)(128)(2,1)}, u32[]{:S(2)}) copy-start(bf16[512]{0:T(512)(128)(2,1)} %copy-done.98) | copy-start | bytes 3076
  1000.0 25.4 %copy-start.105 = (bf16[512]{0:T(512)(128)(2,1)S(1)}, bf16[512]{0:T(512)(128)(2,1)}, u32[]{:S(2)}) copy-start(bf16[512]{0:T(512)(128)(2,1)} %copy-done.104) | copy-start | bytes 3076
  1000.0 25.4 %copy-start.111 = (bf16[512]{0:T(512)(128)(2,1)S(1)}, bf16[512]{0:T(512)(128)(2,1)}, u32[]{:S(2)}) copy-start(bf16[512]{0:T(512)(128)(2,1)} %copy-done.110) | copy-start | bytes 3076
  1099.2 443.2 %all-gather.3.cloned.1.call-start = ((), (), s32[]{:S(2)}) async-start(), calls=%async_computation | async-start | bytes 5529600 | tf_op jit(solution)/shard_map/all_gather | solution.py:396
  1105.7 551.3 %all-reduce.14.cloned.1.call-start = ((), (), s32[]{:S(2)}) async-start(), calls=%async_computation.4 | async-start | bytes 9175040 | tf_op jit(solution)/shard_map/psum | solution.py:373
  1488.4 373.6 %all-gather.5.cloned.1.call-start = ((), (), s32[]{:S(2)}) async-start(), calls=%async_computation.1 | async-start | bytes 27648000 | tf_op jit(solution)/shard_map/all_gather | solution.py:395
  (50 other events, 145.6 us)
Sparse Core Ops, SparseCore 0:
  44.3 191.3 all-reduce.9
  1099.3 384.5 all-reduce.11
  1486.3 55.9 all-gather.2
  1546.4 110.6 all-reduce.13
  1659.3 202.6 all-gather.4
where the time goes:
time: 1900 us; the launch traced here: 1880 us
  waiting for transfers between devices  879 us (46%)
  local copies, waits for them, and re-layouts  462 us (24%)
  other arithmetic  195 us (10%)
  starting transfers between devices  175 us (9%)
  matrix products  84.6 us (4%)
  blocking collectives  39.3 us (2%)
  loops' own time  33.1 us (2%)
    unnamed x7, waiting for transfers between devices  522 us
    all_gather x1, waiting for transfers between devices, body(): lax.all_gather(my_rows, 'section', axis=0, tiled=True)  185 us
    ppermute x24, starting transfers between devices, from_behind(): return lax.ppermute(block, axis, route)  175 us
    psum x1, waiting for transfers between devices, body(): lax.psum((jnp.where(first_block, own_grads, zero_flat), jnp.where(first_b...  110 us
    unnamed x131, local copies, waits for them, and re-layouts  99.8 us
    ppermute x24, waiting for transfers between devices, from_behind(): return lax.ppermute(block, axis, route)  61.4 us
    dot_general x24, matrix products, contract_rows(): lax.dot_general(left_side, right_side, (((0,), (0,)), ((), ())), preferre...  40.7 us
    psum x1, blocking collectives, body(): lax.psum((head_terms[0], head_terms[1]), ('section', 'dp'))  39.3 us
  transfers between devices with their start and end apart: 29, of which 13 were waited for; matrix products, arithmetic and copies ran while one was open for 27% of the time, Pallas kernels for 0%

commit v1 on v0

v1 whole, which is shorter than its diff:
```python
import functools

import jax
import jax.numpy as jnp
from jax import lax
from jax.experimental import pallas as pl
from jax.experimental.pallas import tpu as pltpu
from jax.sharding import PartitionSpec as P

POOL = 8
KNOT = 24
LANES = 128
ONES = 16
GELU_A = 0.7978845608028654
GELU_B = GELU_A * 0.044715
F32 = jnp.float32
BF16 = jnp.bfloat16
MIB = 1 << 20


def up(size, unit):
    return -(-size // unit) * unit


class Plan:
    def __init__(self, length, horizon, hidden, pooled, coarse_out, sections, windows):
        self.length, self.horizon, self.hidden = length, horizon, hidden
        self.pooled, self.coarse_out = pooled, coarse_out
        self.fine_out = length + horizon
        self.sections, self.windows = sections, windows
        self.back, self.fore = length // KNOT, horizon // KNOT
        self.wide_in, self.wide_out = up(length + 1, LANES), up(self.fine_out + 1, LANES)
        self.pool_wide, self.theta_wide = up(pooled + 1, LANES), up(coarse_out + 1, LANES)
        widths = [
            ("coarse_entry", self.pool_wide),
            ("coarse_middle", hidden),
            ("coarse_upper", hidden),
            ("coarse_head", self.theta_wide),
            ("bias", LANES),
            ("fine_entry", self.wide_in),
            ("fine_middle", hidden),
            ("fine_upper", hidden),
            ("fine_head", self.wide_out),
        ]
        self.at, place = {}, 0
        for name, width in widths:
            self.at[name] = place
            place += width
        self.columns = place
        self.knots_wide = up(self.back, ONES)
        self.low = length // LANES * LANES
        self.skip = length - self.low
        self.square = hidden // sections
        self.slice_at, self.part, place = {}, {}, 0
        for name, width in (
            ("fine_head", self.wide_out),
            ("fine_entry", self.wide_in),
            ("fine_middle", hidden),
            ("fine_upper", hidden),
            ("coarse_middle", hidden),
            ("coarse_upper", hidden),
            ("coarse_head", self.theta_wide),
            ("coarse_entry", self.pool_wide),
        ):
            self.slice_at[name] = place
            total = width // LANES
            share = -(-total // sections)
            self.part[name] = share, total
            place += share * LANES
        self.slice_columns = place
        self.bias_at, place = {}, 0
        for name in ("fine_head", "coarse_head", "coarse_middle", "coarse_upper", "fine_middle", "fine_upper"):
            self.bias_at[name] = place
            place += self.part[name][0]
        self.bias_rows = up(place, 8)
        self.knot_rows = up(coarse_out, ONES)
        self.pair = 2 * KNOT
        self.r1_pairs = -(-(self.rows("fine_entry") + self.pair - ONES) // self.pair)

    def rows(self, name):
        return self.part[name][0] * LANES

    def start(self, name, section):
        low = min if isinstance(section, int) else jnp.minimum
        share, total = self.part[name]
        return low(section * share, total - share) * LANES


def gelu_both(a):
    square = a * a
    t = jnp.tanh(a * (GELU_A + GELU_B * square))
    half = 0.5 * a
    slope = 0.5 + 0.5 * t + half * (1.0 - t * t) * (GELU_A + (3.0 * GELU_B) * square)
    return half + half * t, slope


def dot(a, b):
    return jnp.dot(a, b, preferred_element_type=F32)


def dot_rows(a, b):
    return lax.dot_general(a, b, (((1,), (1,)), ((), ())), preferred_element_type=F32)


def aligned(start, size, unit):
    return pl.ds(pl.multiple_of(start, unit), size)


def column_of(row_ref, first, count):
    size = row_ref.shape[1]
    columns = []
    for at in range(first, first + count, LANES):
        width = max(0, min(LANES, size - at))
        row = jnp.zeros((1, LANES), F32) if width == 0 else row_ref[:, at : at + width]
        if 0 < width < LANES:
            row = jnp.concatenate([row, jnp.zeros((1, LANES - width), F32)], axis=1)
        columns.append(jnp.broadcast_to(row, (LANES, LANES)).T[:, :1])
    return jnp.concatenate(columns, axis=0)


def hat_weights(first, count, plan, turned=False):
    shape = (plan.knots_wide, count) if turned else (count, plan.theta_wide)
    row = lax.broadcasted_iota(jnp.int32, shape, 1 if turned else 0) + first
    knot = lax.broadcasted_iota(jnp.int32, shape, 0 if turned else 1)
    away = row - KNOT * knot
    weight = jnp.maximum(KNOT - jnp.abs(away), 0)
    weight = jnp.where((knot == plan.back - 1) & (away > 0), KNOT, weight)
    return jnp.where((knot < plan.back) & (row < plan.length), weight, 0).astype(F32).astype(BF16)


def fractions(width):
    later = lax.broadcasted_iota(jnp.int32, (KNOT, width), 0).astype(F32) * (1.0 / KNOT)
    return 1.0 - later, later


NAMES = (
    "coarse_entry",
    "coarse_middle",
    "coarse_upper",
    "coarse_head",
    "fine_entry",
    "fine_middle",
    "fine_upper",
    "fine_head",
)
KEPT = ("fine_entry", "fine_head")


def remote(source, target, send_sem, recv_sem, place):
    return pltpu.make_async_remote_copy(
        src_ref=source,
        dst_ref=target,
        send_sem=send_sem,
        recv_sem=recv_sem,
        device_id=place,
        device_id_type=pl.DeviceIdType.MESH,
    )


def signal(semaphore, places):
    for place in places:
        pl.semaphore_signal(semaphore, inc=1, device_id=place, device_id_type=pl.DeviceIdType.MESH)


class Ways:
    def __init__(self, groups):
        self.section, self.dp = lax.axis_index("section"), lax.axis_index("dp")
        self.group, self.core = self.dp // 2, self.dp % 2
        self.groups = groups
        self.partner = (self.section, self.group * 2 + 1 - self.core)
        s = self.section
        self.side = [s + 1 - 2 * (s % 2), (s + 2) % 4]
        self.sides = [(t, self.dp) for t in self.side]
        self.across = 3 - s

    def far(self, j):
        group = (self.group + j) % self.groups
        return group, (self.section, group * 2 + self.core)

    def from_far(self, j):
        return (self.group + self.groups - j) % self.groups

    def all(self):
        return [self.partner] + self.sides + [self.far(j)[1] for j in range(1, self.groups)]


class Gather:
    def __init__(self, plan, way, per, cuts, w_ref, shards, biases, send, recv, partner_recv):
        self.p, self.way, self.per, self.cuts, self.w_ref = plan, way, per, cuts, w_ref
        self.shards, self.biases = shards, biases
        self.send, self.recv, self.partner_recv = send, recv, partner_recv
        self.near = range(1, way.groups)
        self.chunks, self.ahead = len(cuts) - 1, 3

    def at(self, k, owner, s=None):
        quarter = self.per // 4
        rows = aligned(owner * self.per, self.per, self.per)
        if s is not None:
            rows = aligned(owner * self.per + s * quarter, quarter, quarter)
        return self.w_ref.at[rows, self.cuts[k] : self.cuts[k + 1]]

    def source(self, j):
        return self.way.from_far(j) * 2 + self.way.core

    def copy(self, here, k, j, kind, place):
        return remote(here, here, self.send.at[k, j - 1, kind], self.recv.at[k, j - 1, kind], place)

    def to_far(self, k, j):
        return self.copy(self.at(k, self.way.dp, self.way.section), k, j, 0, self.way.far(j)[1])

    def to_side(self, k, j, i):
        return self.copy(self.at(k, self.source(j), self.way.section), k, j, 1 + i, self.way.sides[i])

    def to_across(self, k, j):
        i = (k + j) % 2
        return self.copy(self.at(k, self.source(j), self.way.side[i]), k, j, 3, self.way.sides[1 - i])

    def to_partner(self, k, j):
        here = self.at(k, self.source(j) if j else self.way.dp)
        return remote(here, here, self.send.at[k, max(j - 1, 0), 4 if j else 5], self.partner_recv.at[k, j], self.way.partner)

    def arrived(self, k, j, kind):
        s = [self.way.section, self.way.side[0], self.way.side[1], self.way.across][kind]
        self.copy(self.at(k, self.source(j), s), k, j, kind, self.way.partner).wait_recv()

    def cast(self, k):
        p, own = self.p, aligned(self.way.dp * self.per, self.per, self.per)
        low, high = self.cuts[k], self.cuts[k + 1]
        for ref, name in zip(self.shards, NAMES):
            at, size = p.at[name], ref.shape[1]
            wide = up(size + 1, LANES) if name.endswith(("entry", "head")) else size
            first, last = max(at, low), min(at + wide, high)
            full = min(last, at + size // LANES * LANES)
            if first < full:
                self.w_ref[own, first:full] = ref[:, first - at : full - at].astype(BF16)
            if first < last and last > full:
                rest = ref[:, full - at : size].astype(BF16)
                pad = jnp.zeros((self.per, last - at - size), BF16)
                self.w_ref[own, full:last] = jnp.concatenate([rest, pad], axis=1)
        at = p.at["bias"]
        if low <= at < high:
            count = len(self.biases)
            rows = jnp.concatenate([ref[...] for ref in self.biases] + [jnp.zeros((8 - count, self.per), F32)], axis=0)
            wide = jnp.concatenate([rows, jnp.zeros((8, LANES - self.per), F32)], axis=1)
            wide = jnp.concatenate([wide, jnp.zeros((LANES - 8, LANES), F32)], axis=0)
            self.w_ref[own, at : at + LANES] = wide.T[: self.per].astype(BF16)

    def first(self, k):
        self.cast(k)
        for j in self.near:
            self.to_far(k, j).start()
        self.to_partner(k, 0).start()

    def second(self, k):
        for j in self.near:
            self.arrived(k, j, 0)
            for i in range(2):
                self.to_side(k, j, i).start()

    def third(self, k):
        for j in self.near:
            self.arrived(k, j, 1)
            self.arrived(k, j, 2)
            self.to_across(k, j).start()

    def fourth(self, k):
        for j in self.near:
            self.arrived(k, j, 3)
            self.to_partner(k, j).start()

    def turn(self, t):
        for depth, stage in enumerate((self.second, self.third, self.fourth)):
            if 0 <= t - depth < self.chunks:
                stage(t - depth)
            if depth == 0 and t + self.ahead < self.chunks:
                self.first(t + self.ahead)

    def complete(self, k):
        for j in range(self.way.groups):
            there = (self.way.from_far(j) * 2 + 1 - self.way.core) if j else self.way.partner[1]
            here = self.at(k, there)
            remote(here, here, self.send.at[k, 0, 5], self.partner_recv.at[k, j], self.way.partner).wait_recv()

    def sent(self):
        for k in range(self.chunks):
            for j in self.near:
                for copy in (self.to_far(k, j), self.to_side(k, j, 0), self.to_side(k, j, 1), self.to_across(k, j)):
                    copy.wait_send()
                self.to_partner(k, j).wait_send()
            self.to_partner(k, 0).wait_send()


class Reduce:
    def __init__(self, plan, way, per, cuts, part_ref, core_in, far_in, far_out, out_ref, send, recv):
        self.p, self.way, self.per, self.cuts = plan, way, per, cuts
        self.part_ref, self.core_in, self.far_in, self.far_out = part_ref, core_in, far_in, far_out
        self.out_ref, self.send, self.recv = out_ref, send, recv
        self.near = range(1, way.groups)
        self.chunks = len(cuts) - 1

    def columns(self, k):
        return slice(self.cuts[k], self.cuts[k + 1])

    def to_partner(self, k, g):
        return remote(
            self.part_ref(g * 2 + 1 - self.way.core, k),
            self.core_in(g, k),
            self.send.at[k, g, 0],
            self.recv.at[k, g, 0],
            self.way.partner,
        )

    def to_far(self, k, j):
        here, there = self.far_out(j - 1, k), self.far_in(j - 1, k)
        return remote(here, there, self.send.at[k, j - 1, 1], self.recv.at[k, j - 1, 1], self.way.far(j)[1])

    def side(self, k, source, i, to):
        here = self.out_ref.at[source, :, self.columns(k)]
        return remote(here, here, self.send.at[k, i, 2], self.recv.at[k, i, 2], to)

    def to_side(self, k, i):
        return self.side(k, self.way.section, i, self.way.sides[i])

    def to_across(self, k):
        i = k % 2
        return self.side(k, self.way.side[i], 2, self.way.sides[1 - i])

    def summed(self, k, group):
        own = self.part_ref(group * 2 + self.way.core, k)[...].astype(F32)
        return own + self.core_in(group, k)[...].astype(F32)

    def first(self, k):
        for g in range(self.way.groups):
            self.to_partner(k, g).start()

    def second(self, k):
        for g in range(self.way.groups):
            self.to_partner(k, g).wait_recv()
        for j in self.near:
            self.far_out(j - 1, k)[...] = self.summed(k, self.way.far(j)[0]).astype(BF16)
            self.to_far(k, j).start()

    def third(self, k):
        total = self.summed(k, self.way.group)
        for j in self.near:
            self.to_far(k, j).wait_recv()
            total += self.far_in(j - 1, k)[...].astype(F32)
        self.out_ref[self.way.section, :, self.columns(k)] = total.astype(BF16)
        for i in range(2):
            self.to_side(k, i).start()

    def fourth(self, k):
        i = k % 2
        for turn in (i, 1 - i):
            self.side(k, self.way.side[turn], turn, self.way.sides[turn]).wait_recv()
            if turn == i:
                self.to_across(k).start()

    def complete(self, k):
        self.side(k, self.way.across, 2, self.way.partner).wait_recv()

    def sent(self, k):
        for g in range(self.way.groups):
            self.to_partner(k, g).wait_send()
        for j in self.near:
            self.to_far(k, j).wait_send()
        for i in range(2):
            self.to_side(k, i).wait_send()
        self.to_across(k).wait_send()


class ReduceBias:
    def __init__(self, way, own_ref, core_in, far_ref, out_ref, send, recv):
        self.way, self.own_ref, self.core_in, self.far_ref, self.out_ref = way, own_ref, core_in, far_ref, out_ref
        self.send, self.recv = send, recv
        self.near = range(1, way.groups)

    def copy(self, here, there, n, place):
        return remote(here, there, self.send.at[n], self.recv.at[n], place)

    def to_partner(self):
        return self.copy(self.own_ref, self.core_in, 0, self.way.partner)

    def to_far(self, j):
        here = self.far_ref.at[self.way.group]
        return self.copy(here, here, j, self.way.far(j)[1])

    def side(self, source, n, to):
        here = self.out_ref.at[source]
        return self.copy(here, here, self.way.groups + n, to)

    def to_across(self):
        return self.side(self.way.side[0], 2, self.way.sides[1])

    def second(self):
        self.to_partner().wait_recv()
        self.far_ref[self.way.group] = self.own_ref[...] + self.core_in[...]
        for j in self.near:
            self.to_far(j).start()

    def third(self):
        for j in self.near:
            here = self.far_ref.at[self.way.from_far(j)]
            self.copy(here, here, j, self.way.partner).wait_recv()
        total = self.far_ref[0]
        for g in range(1, self.way.groups):
            total += self.far_ref[g]
        self.out_ref[self.way.section] = total
        for i in range(2):
            self.side(self.way.section, i, self.way.sides[i]).start()

    def fourth(self):
        self.side(self.way.side[0], 0, self.way.partner).wait_recv()
        self.to_across().start()
        self.side(self.way.side[1], 1, self.way.partner).wait_recv()

    def complete(self):
        self.side(self.way.across, 2, self.way.partner).wait_recv()
        self.to_partner().wait_send()
        for j in self.near:
            self.to_far(j).wait_send()
        for i in range(2):
            self.side(self.way.section, i, self.way.sides[i]).wait_send()
        self.to_across().wait_send()


def core_kernel(plan, per, groups, *refs):
    p = plan
    refs = list(refs)
    take = lambda count: [refs.pop(0) for _ in range(count)]
    history_ref, cotangent_ref, target_ref, horizon_ref, coarse_bias_ref, fine_bias_ref = take(6)
    if groups:
        shards_in = take(14)
    else:
        (packed_ref,) = take(1)
    theta_out, h3_out, gfine_out, pool_out = take(4)
    if groups:
        kept_out, slices_out, bias_out = take(3)
    else:
        slice_out, bias_out = take(2)
    w_ref, big_ref, h_ref, g_ref, r1_ref, pooled_ref, split_ref, theta_ref, gtheta_ref, gknot_ref = take(10)
    pw_ref, pwt_ref, f32_ref, product_ref, bias_ref = take(5)
    fore_bias_ref, horizon_buf, coarse_bias_buf, fine_bias_buf, sems = take(5)
    if groups:
        shards = take(14)
        shard_sems, send, recv, partner_recv = take(4)
        head_bias_ref, bias_in, bias_far, far_first, ready, reduce_send, reduce_recv, bias_send, bias_recv = take(9)
    else:
        head_bias_ref = bias_out
    hid, windows = p.hidden, p.windows
    section = lax.axis_index("section")
    chunk = min(512, windows)
    chunks = windows // chunk
    H = slice(0, hid)
    lanes_of = lambda n: aligned(n * chunk, chunk, chunk)
    place = p.at["fine_entry"]
    head_at = p.at["fine_head"]

    load = lambda source, out, sem: pltpu.make_async_copy(source, out, sems.at[sem])
    history_in = load(history_ref, big_ref.at[: p.length], 1)
    cotangent_in = load(cotangent_ref, big_ref.at[: p.length], 2)
    target_in = load(target_ref, big_ref.at[p.length : p.fine_out], 0)
    rows_in = [
        load(horizon_ref, horizon_buf, 3),
        load(coarse_bias_ref, coarse_bias_buf, 4),
        load(fine_bias_ref, fine_bias_buf, 5),
    ]
    theta_copy = load(theta_ref, theta_out, 6)
    h3_copy = load(h_ref.at[5, H], h3_out, 7)
    gfine_copy = load(g_ref.at[3], gfine_out, 8)
    pool_copy = load(pooled_ref, pool_out, 9)

    if groups:
        shards_load = [
            pltpu.make_async_copy(source, out, shard_sems.at[n]) for n, (source, out) in enumerate(zip(shards_in, shards))
        ]
        order = [0, 1, 2, 3, 8, 9, 10, 11, 12, 13, 4, 5, 6, 7]
        for n in order:
            shards_load[n].start()
        way = Ways(groups)
        middle = p.at["fine_middle"]
        third = (p.columns - middle) // 3 // LANES * LANES
        entry_cut = place + up((middle - place) // 2, LANES)
        cuts = (0, 2 * hid, place, entry_cut, middle, middle + third, middle + 2 * third, p.columns)
        gather = Gather(p, way, per, cuts, w_ref, shards[:8], shards[8:], send, recv, partner_recv)
        history_in.start()
        for copy in rows_in:
            copy.start()
        barrier = pltpu.get_barrier_semaphore()
        signal(barrier, way.all())
        for n in order[:10]:
            shards_load[n].wait()
        pl.semaphore_wait(barrier, len(way.all()))
        gather.first(0)
        for n in order[10:]:
            shards_load[n].wait()
        for k in range(1, gather.ahead):
            gather.first(k)
    else:
        weights_in = load(packed_ref, w_ref, 10)
        weights_in.start()
        history_in.start()
        for copy in rows_in:
            copy.start()

    def turn(t):
        if groups:
            gather.turn(t)

    def complete(*ks):
        if groups:
            for k in ks:
                gather.complete(k)

    tail = p.wide_out - p.length
    mark = lax.broadcasted_iota(jnp.int32, (tail, windows), 0) < POOL
    big_ref[p.length :, :] = mark.astype(F32).astype(BF16)
    pooled_ref[...] = jnp.zeros_like(pooled_ref)
    for index in range(6):
        h_ref[index, hid:, :] = jnp.ones((ONES, windows), BF16)
    for copy in rows_in:
        copy.wait()
    fore_bias_ref[...] = column_of(fine_bias_buf, p.low, p.wide_out - p.low)
    history_in.wait()
    turn(0)

    pool_unit = LANES
    pool_count = p.wide_in // pool_unit

    def pool(i):
        rows = aligned(i * pool_unit, pool_unit, pool_unit)
        for c in range(windows // LANES):
            lanes = slice(c * LANES, (c + 1) * LANES)
            f32_ref[c] = big_ref[rows, lanes].astype(F32)
            total = f32_ref[c, pl.ds(0, pool_unit // POOL, stride=POOL), :]
            for j in range(1, POOL):
                total += f32_ref[c, pl.ds(j, pool_unit // POOL, stride=POOL), :]
            pooled_ref[aligned(i * (pool_unit // POOL), pool_unit // POOL, ONES), lanes] = (total * (1.0 / POOL)).astype(BF16)

    pieces = 4
    for piece in range(pieces):
        pl.loop(pool_count * piece // pieces, pool_count * (piece + 1) // pieces)(pool)
        if piece + 1 < pieces:
            turn(piece + 1)
    complete(0, 1)
    if not groups:
        weights_in.wait()
    bias_ref[...] = w_ref[:, p.at["bias"] : p.at["bias"] + LANES].astype(F32)

    strip = ONES

    def strips():
        for r in range(0, hid, strip):
            rows = slice(r, r + strip)
            yield product_ref[rows, :], rows

    def activate(a, index, lanes):
        product_ref[H, :] = a
        for value, rows in strips():
            h, slope = gelu_both(value + bias_ref[rows, index : index + 1])
            h_ref[index, rows, lanes] = h.astype(BF16)
            g_ref[index, rows, lanes] = slope.astype(BF16)

    def tiles(body):
        @pl.loop(0, chunks)
        def _(n):
            body(lanes_of(n))

    def hidden_layer(name, index):
        at = p.at[name]
        turned = w_ref[:, at : at + hid].T
        tiles(lambda lanes: activate(dot(turned, h_ref[index - 1, H, lanes]), index, lanes))

    at_entry = p.at["coarse_entry"]
    tiles(
        lambda lanes: activate(dot(w_ref[:, at_entry : at_entry + p.pool_wide], pooled_ref[:, lanes]), 0, lanes)
    )
    turn(4)
    hidden_layer("coarse_middle", 1)
    turn(5)
    hidden_layer("coarse_upper", 2)
    at_head = p.at["coarse_head"]
    turned_head = w_ref[:, at_head : at_head + p.theta_wide].T
    theta_bias = column_of(coarse_bias_buf, 0, p.theta_wide)
    used = lax.broadcasted_iota(jnp.int32, (p.theta_wide, chunk), 0) < p.back

    @pl.loop(0, chunks)
    def _(n):
        lanes = lanes_of(n)
        theta = dot(turned_head, h_ref[2, H, lanes]) + theta_bias
        theta_ref[:, lanes] = theta
        knots = jnp.where(used, theta, 0.0)
        high = knots.astype(BF16)
        split_ref[: p.theta_wide, lanes] = high
        split_ref[p.theta_wide :, lanes] = (knots - high.astype(F32)).astype(BF16)

    theta_copy.start()
    turn(6)
    complete(2, 3)

    total = jnp.zeros((hid, p.theta_wide), F32)
    step = 6 * LANES
    for first in range(0, p.wide_in, step):
        count = min(step, p.wide_in - first)
        total += dot(w_ref[:, place + first : place + first + count], hat_weights(first, count, p))
    product = (total * (1.0 / KNOT)).astype(BF16)
    pwt_ref[:, : p.theta_wide] = product
    pwt_ref[:, p.theta_wide :] = product
    pw_ref[...] = product.T

    def fine_entry(lanes):
        a = dot(w_ref[:, place : place + p.wide_in], big_ref[: p.wide_in, lanes])
        activate(a - dot(pwt_ref[...], split_ref[:, lanes]), 3, lanes)

    for n in range(chunks):
        fine_entry(slice(n * chunk, (n + 1) * chunk))
        if n < 2:
            turn(7 + n)
    if chunks < 2:
        turn(8)

    first_pair = p.start("fine_entry", section) // p.pair

    def interpolate(base, count, k, rest, later, lanes):
        own = theta_ref[pl.ds(base + jnp.minimum(k, count - 1), 1), lanes]
        after = theta_ref[pl.ds(base + jnp.minimum(k + 1, count - 1), 1), lanes]
        return own * rest + after * later

    everything = slice(0, windows)
    rest, later = fractions(windows)

    @pl.loop(0, p.r1_pairs)
    def _(i):
        pair = first_pair + i
        source = aligned(pair * p.pair, p.pair, ONES)
        made = jnp.concatenate(
            [interpolate(0, p.back, 2 * pair + j, rest, later, everything) for j in range(2)], axis=0
        )
        made = made * (pair < p.back // 2).astype(F32)
        r1_ref[aligned(i * p.pair, p.pair, ONES), :] = (big_ref[source, :].astype(F32) - made).astype(BF16)

    cotangent_in.start()
    target_in.start()
    big_ref[p.fine_out :, :] = jnp.zeros((p.wide_out - p.fine_out, windows), BF16)
    if groups:
        signal(ready.at[0], way.all())
    complete(4)
    hidden_layer("fine_middle", 4)
    hidden_layer("fine_upper", 5)
    h3_copy.start()
    complete(5, 6)
    if groups:
        kept = [
            load(w_ref.at[:, p.at[name] : p.at[name] + wide], kept_out.at[:, p.at[name] : p.at[name] + wide], 10 + n)
            for n, (name, wide) in enumerate(zip(KEPT, (p.wide_in, p.wide_out)))
        ]
        for copy in kept:
            copy.start()

    rest_c, later_c = fractions(chunk)
    turned_fore = w_ref[:, head_at + p.low : head_at + p.wide_out].T
    target_in.wait()

    @pl.loop(0, chunks)
    def _(n):
        lanes = lanes_of(n)
        before = jnp.zeros((1, chunk), F32)
        product_ref[: p.horizon, :] = dot(turned_fore[p.skip : p.skip + p.horizon], h_ref[5, H, lanes])
        for k in range(0, p.fore, 2):
            here = slice(k * KNOT, (k + 2) * KNOT)
            second = product_ref[here, :] + fore_bias_ref[p.skip + k * KNOT : p.skip + (k + 2) * KNOT, :]
            first = jnp.concatenate(
                [interpolate(p.back, p.fore, k + j, rest_c, later_c, lanes) for j in range(2)], axis=0
            )
            counts = (lax.broadcasted_iota(jnp.int32, (2 * KNOT, chunk), 0) + k * KNOT) < horizon_buf[:, lanes]
            there = slice(p.length + k * KNOT, p.length + (k + 2) * KNOT)
            error = first + second - big_ref[there, lanes].astype(F32)
            gradient = jnp.where(counts, error, 0.0)
            big_ref[there, lanes] = (-gradient).astype(BF16)
            for j in range(2):
                part = gradient[j * KNOT : (j + 1) * KNOT]
                own = jnp.sum(part * rest_c, axis=0, keepdims=True)
                after = jnp.sum(part * later_c, axis=0, keepdims=True)
                last = after if k + j == p.fore - 1 else 0.0
                gtheta_ref[p.back + k + j : p.back + k + j + 1, lanes] = own + before + last
                before = after

    cotangent_in.wait()

    def gradient_slice(name, left, right_ref, first, step=LANES, sign=1.0):
        left_side = left if name.endswith("entry") else h_ref[left]
        for b in range(0, p.rows(name), step):
            width = min(step, p.rows(name) - b)
            value = sign * dot_rows(left_side, right_ref[aligned(first + b, width, ONES), :])
            to = place + p.slice_at[name] + b
            w_ref[:, to : to + width] = value[:hid].astype(BF16)
            if name in p.bias_at:
                for c in range(0, width, LANES):
                    row = p.bias_at[name] + (b + c) // LANES
                    head_bias_ref[row : row + 1, :] = value[hid : hid + 1, c : c + LANES]

    def square_slice(name, index):
        gradient_slice(name, index - 1, g_ref.at[index], p.start(name, section))

    def back_layer(product, index):
        def body(lanes):
            product_ref[H, :] = product(lanes)
            for value, rows in strips():
                g_ref[index, rows, lanes] = (value * g_ref[index, rows, lanes].astype(F32)).astype(BF16)

        tiles(body)

    def times(name, index):
        at = p.at[name]
        return lambda lanes: dot(w_ref[:, at : at + hid], g_ref[index, :, lanes])

    if groups:
        for copy in kept:
            copy.wait()
        gather.sent()
        cuts = (0, p.slice_at["fine_entry"], p.slice_at["coarse_middle"], p.slice_columns)
        width = lambda k: cuts[k + 1] - cuts[k]

        def arrivals(row, k):
            rows = slice(row * per, (row + 1) * per) if isinstance(row, int) else aligned(row * per, per, per)
            if k == 0:
                return split_ref.at[rows, : width(0)]
            first = head_at + cuts[k] - cuts[1]
            return w_ref.at[rows, first : first + width(k)]

        def departures(j, k):
            if k == 0:
                return far_first.at[j * per : (j + 1) * per, :]
            first = (k * groups + j) * per
            return big_ref.at[first : first + per, : width(k)]

        reduce = Reduce(
            p,
            way,
            per,
            cuts,
            lambda owner, k: w_ref.at[aligned(owner * per, per, per), place + cuts[k] : place + cuts[k + 1]],
            arrivals,
            lambda j, k: arrivals(groups + j, k),
            departures,
            slices_out,
            reduce_send,
            reduce_recv,
        )
        reduce_bias = ReduceBias(way, head_bias_ref, bias_in, bias_far, bias_out, bias_send, bias_recv)

    gradient_slice("fine_head", 5, big_ref, p.start("fine_head", section), 3 * LANES, -1.0)
    if groups:
        pl.semaphore_wait(ready.at[0], len(way.all()))
        reduce.first(0)

    back_layer(lambda lanes: -dot(w_ref[:, head_at : head_at + p.wide_out], big_ref[:, lanes]), 5)
    if groups:
        signal(ready.at[1], way.all())
        reduce.second(0)

    for first in range(0, p.wide_in, step):
        count = min(step, p.wide_in - first)
        hats = hat_weights(first, count, p, True)

        @pl.loop(0, chunks)
        def _(n):
            lanes = lanes_of(n)
            part = dot(hats, big_ref[first : first + count, lanes])[: p.back] * (-1.0 / KNOT)
            if first == 0:
                gtheta_ref[: p.back, lanes] = part
            else:
                gtheta_ref[: p.back, lanes] += part

    back_layer(times("fine_upper", 5), 4)
    back_layer(times("fine_middle", 4), 3)
    gfine_copy.start()
    gradient_slice("fine_entry", g_ref[3], r1_ref, p.start("fine_entry", section) - first_pair * p.pair, 2 * LANES)
    square_slice("fine_middle", 4)
    square_slice("fine_upper", 5)
    if groups:
        pl.semaphore_wait(ready.at[1], len(way.all()))
        reduce.first(1)
        reduce.third(0)
    row = lax.broadcasted_iota(jnp.int32, (p.knot_rows, chunk), 0)
    gknot_ref[p.knot_rows :, :] = jnp.zeros((p.theta_wide - p.knot_rows, windows), BF16)

    @pl.loop(0, chunks)
    def _(n):
        lanes = lanes_of(n)
        knots = jnp.where(row < p.coarse_out, gtheta_ref[:, lanes], 0.0)
        gknot_ref[: p.knot_rows, lanes] = (knots - dot(pw_ref[: p.knot_rows, :], g_ref[3, :, lanes])).astype(BF16)

    back_layer(lambda lanes: dot(w_ref[:, at_head : at_head + p.theta_wide], gknot_ref[:, lanes]), 2)
    if groups:
        reduce.second(1)
    back_layer(times("coarse_upper", 2), 1)
    if groups:
        reduce.fourth(0)
    back_layer(times("coarse_middle", 1), 0)
    gradient_slice("coarse_head", 2, gknot_ref, p.start("coarse_head", section))
    gradient_slice("coarse_entry", g_ref[0], pooled_ref, p.start("coarse_entry", section))
    square_slice("coarse_middle", 1)
    square_slice("coarse_upper", 2)
    if groups:
        reduce.first(2)
        reduce_bias.to_partner().start()
        reduce.third(1)
        reduce.second(2)
        reduce_bias.second()

    turned_entry = w_ref[:, at_entry : at_entry + p.pool_wide].T

    def pool_gradient(lanes):
        product_ref[: p.pool_wide, :] = dot(turned_entry, g_ref[0, :, lanes])
        for r in range(0, p.pool_wide, strip):
            pooled_ref[r : r + strip, lanes] = (product_ref[r : r + strip, :] * (1.0 / POOL)).astype(BF16)

    tiles(pool_gradient)
    pool_copy.start()
    if groups:
        reduce.fourth(1)
        reduce_bias.third()
        reduce.third(2)
        reduce_bias.fourth()
        reduce.fourth(2)
        for k in range(reduce.chunks):
            reduce.complete(k)
            reduce.sent(k)
        reduce_bias.complete()
    else:
        out = load(w_ref.at[:, place : place + p.slice_columns], slice_out, 10)
        out.start()
        out.wait()
    theta_copy.wait()
    h3_copy.wait()
    gfine_copy.wait()
    pool_copy.wait()


ANY = pl.BlockSpec(memory_space=pl.ANY)
VMEM = pl.BlockSpec(memory_space=pltpu.VMEM)


def core(plan, per, groups, history, cotangent, targets, horizon, coarse_bias, fine_bias, weights):
    p = plan
    hid, windows = p.hidden, p.windows
    flops = 2 * windows * hid * (2 * p.length + 2 * p.wide_out // 3 + 12 * hid + p.slice_columns)
    out_shape = [
        jax.ShapeDtypeStruct((p.theta_wide, windows), F32),
        jax.ShapeDtypeStruct((hid, windows), BF16),
        jax.ShapeDtypeStruct((hid, windows), BF16),
        jax.ShapeDtypeStruct((p.pool_wide, windows), BF16),
    ]
    out_specs = [ANY] * 4
    scratch = [
        pltpu.VMEM((hid, p.columns), BF16),
        pltpu.VMEM((p.wide_out, windows), BF16),
        pltpu.VMEM((6, hid + ONES, windows), BF16),
        pltpu.VMEM((6, hid, windows), BF16),
        pltpu.VMEM((p.r1_pairs * p.pair, windows), BF16),
        pltpu.VMEM((p.pool_wide, windows), BF16),
        pltpu.VMEM((2 * p.theta_wide, windows), BF16),
        pltpu.VMEM((p.theta_wide, windows), F32),
        pltpu.VMEM((p.knot_rows, windows), F32),
        pltpu.VMEM((p.theta_wide, windows), BF16),
        pltpu.VMEM((p.theta_wide, hid), BF16),
        pltpu.VMEM((hid, 2 * p.theta_wide), BF16),
        pltpu.VMEM((windows // LANES, LANES, LANES), F32),
        pltpu.VMEM((max(hid, p.horizon), min(512, windows)), F32),
        pltpu.VMEM((hid, LANES), F32),
        pltpu.VMEM((p.wide_out - p.low, 1), F32),
        pltpu.VMEM(horizon.shape, jnp.int32),
        pltpu.VMEM(coarse_bias.shape, F32),
        pltpu.VMEM(fine_bias.shape, F32),
        pltpu.SemaphoreType.DMA((13,)),
    ]
    params = {}
    if groups:
        bias = (p.bias_rows, LANES)
        out_shape += [
            jax.ShapeDtypeStruct((hid, p.columns), BF16),
            jax.ShapeDtypeStruct((4, per, p.slice_columns), BF16),
            jax.ShapeDtypeStruct((4,) + bias, F32),
        ]
        out_specs += [ANY, VMEM, VMEM]
        chunks, reduce_chunks = 7, 3
        scratch += [pltpu.VMEM(piece.shape, F32) for piece in weights]
        scratch += [
            pltpu.SemaphoreType.DMA((len(weights),)),
            pltpu.SemaphoreType.DMA((chunks, groups - 1, 6)),
            pltpu.SemaphoreType.DMA((chunks, groups - 1, 4)),
            pltpu.SemaphoreType.DMA((chunks, groups)),
            pltpu.VMEM(bias, F32),
            pltpu.VMEM(bias, F32),
            pltpu.VMEM((groups,) + bias, F32),
            pltpu.VMEM(((groups - 1) * per, p.rows("fine_head")), BF16),
            pltpu.SemaphoreType.REGULAR((2,)),
            pltpu.SemaphoreType.DMA((reduce_chunks, max(groups, 3), 3)),
            pltpu.SemaphoreType.DMA((reduce_chunks, max(groups, 3), 3)),
            pltpu.SemaphoreType.DMA((groups + 3,)),
            pltpu.SemaphoreType.DMA((groups + 3,)),
        ]
        params = {"collective_id": 0, "has_side_effects": True}
    else:
        out_shape += [jax.ShapeDtypeStruct((hid, p.slice_columns), BF16), jax.ShapeDtypeStruct((p.bias_rows, LANES), F32)]
        out_specs += [ANY, VMEM]
    return pl.pallas_call(
        functools.partial(core_kernel, p, per, groups),
        out_shape=tuple(out_shape),
        in_specs=[ANY] * (6 + len(weights)),
        out_specs=tuple(out_specs),
        scratch_shapes=scratch,
        compiler_params=pltpu.CompilerParams(vmem_limit_bytes=63 * MIB, **params),
        cost_estimate=pl.CostEstimate(flops=flops, bytes_accessed=windows * p.length * 4, transcendentals=0),
    )(history, cotangent, targets, horizon, coarse_bias, fine_bias, *weights)


def outputs_kernel(
    plan,
    block,
    steps,
    packed_ref,
    history_ref,
    cotangent_ref,
    theta_ref,
    h3_ref,
    gfine_ref,
    pool_ref,
    fine_bias_ref,
    slices_ref,
    bias_rows_ref,
    residual_ref,
    history_grad_ref,
    prediction_ref,
    *refs,
):
    grads = refs[:16]
    head_ref, entry_ref, side_ref, pool_grad, fore_ref, back_ref, fine_ref, bias_ref, sems = refs[16:]
    p = plan
    step = pl.program_id(0)
    windows = p.windows
    chunk = min(512, p.windows)
    chunks = windows // chunk
    lanes_of = lambda n: aligned(n * chunk, chunk, chunk)
    knots = block // KNOT
    pooled = block // POOL
    rest, later = fractions(chunk)

    def fetch(name, out, at, slot, sem):
        first = aligned(p.at[name] + at * block, block, LANES)
        return pltpu.make_async_copy(packed_ref.at[:, first], out.at[slot], sems.at[sem, slot])

    def interpolate(k, count, base, lanes):
        low = jnp.minimum if not isinstance(k, int) else min
        own = theta_ref[pl.ds(base + low(k, count - 1), 1), lanes]
        after = theta_ref[pl.ds(base + low(k + 1, count - 1), 1), lanes]
        return own * rest + after * later

    fore_out = pltpu.make_async_copy(fore_ref, prediction_ref, sems.at[3, 0])
    wide = p.wide_out - p.low
    first_fore = p.at["fine_head"] + p.low
    side = pltpu.make_async_copy(packed_ref.at[:, first_fore : first_fore + wide], side_ref, sems.at[2, 0])

    @pl.when(step == 0)
    def _():
        fetch("fine_head", head_ref, 0, 0, 0).start()
        fetch("fine_entry", entry_ref, 0, 0, 1).start()
        side.start()
        pool_grad[...] = pool_ref[...].astype(F32)

    @pl.when(step == 2)
    def _():
        side.wait()
        turned_fore = side_ref[...].T
        fore_bias = column_of(fine_bias_ref, p.low, wide)

        @pl.loop(0, chunks)
        def _(n):
            lanes = lanes_of(n)
            back_ref[: p.horizon, :] = dot(turned_fore[p.skip : p.skip + p.horizon], h3_ref[:, lanes])
            for k in range(0, p.fore, 2):
                rows = slice(k * KNOT, (k + 2) * KNOT)
                second = back_ref[rows, :] + fore_bias[p.skip + k * KNOT : p.skip + (k + 2) * KNOT]
                first = jnp.concatenate([interpolate(k + j, p.fore, p.back, lanes) for j in range(2)], axis=0)
                fore_ref[rows, lanes] = first.astype(BF16).astype(F32) + second.astype(BF16).astype(F32)

        fore_out.start()

    @pl.when(step == 1)
    def _():
        unpack(p, slices_ref, bias_rows_ref, grads)

    slot = step % 2

    @pl.when(step + 1 < steps)
    def _():
        fetch("fine_head", head_ref, step + 1, 1 - slot, 0).start()
        fetch("fine_entry", entry_ref, step + 1, 1 - slot, 1).start()

    fetch("fine_head", head_ref, step, slot, 0).wait()
    fetch("fine_entry", entry_ref, step, slot, 1).wait()
    turned_head = head_ref[slot].T
    turned_entry = entry_ref[slot].T
    row = jnp.broadcast_to(fine_bias_ref[:, aligned(step * block, block, LANES)], (8, block))
    bias_ref[...] = row.T[:, :1]
    pair = 2 * KNOT

    @pl.loop(0, chunks)
    def _(n):
        lanes = lanes_of(n)
        back_ref[...] = dot(turned_head, h3_ref[:, lanes])
        fine_ref[...] = dot(turned_entry, gfine_ref[:, lanes])
        for at in range(0, block, pair):
            rows = slice(at, at + pair)
            k = step * knots + at // KNOT
            made = jnp.concatenate([interpolate(k + j, p.back, 0, lanes) for j in range(2)], axis=0)
            back = back_ref[rows, :] + bias_ref[rows, :]
            residual_ref[rows, lanes] = (history_ref[rows, lanes].astype(F32) - made - back).astype(BF16)
        for at in range(0, block, pair):
            rows = slice(at, at + pair)
            first = step * pooled + at // POOL
            spread = jnp.concatenate(
                [jnp.broadcast_to(pool_grad[pl.ds(first + j, 1), lanes], (POOL, chunk)) for j in range(pair // POOL)],
                axis=0,
            )
            history_grad_ref[rows, lanes] = (cotangent_ref[rows, lanes].astype(F32) + fine_ref[rows, :] + spread).astype(BF16)

    @pl.when(step == steps - 1)
    def _():
        fore_out.wait()


def outputs(plan, packed, history, cotangent, theta, h3, gfine, pool, fine_bias, slices, bias_rows):
    p = plan
    hid, windows = p.hidden, p.windows
    block = 6 * LANES
    steps = -(-p.length // block)
    rows = pl.BlockSpec((block, windows), lambda i: (i, 0))
    wide = p.wide_out - p.low
    per = slices.shape[1]
    square, vector = (per, hid), (1, per)
    grads = []
    for entry, out in ((p.pooled, p.coarse_out), (p.length, p.fine_out)):
        grads += [(per, entry), vector, square, vector, square, vector, (per, out), (1, out)]
    return pl.pallas_call(
        functools.partial(outputs_kernel, p, block, steps),
        grid=(steps,),
        out_shape=(
            jax.ShapeDtypeStruct((p.length, windows), BF16),
            jax.ShapeDtypeStruct((p.length, windows), BF16),
            jax.ShapeDtypeStruct((p.horizon, windows), F32),
        )
        + tuple(jax.ShapeDtypeStruct(shape, F32) for shape in grads),
        in_specs=[ANY, rows, rows, VMEM, VMEM, VMEM, VMEM, VMEM, VMEM, VMEM],
        out_specs=(rows, rows, ANY) + (VMEM,) * len(grads),
        scratch_shapes=[
            pltpu.VMEM((2, hid, block), BF16),
            pltpu.VMEM((2, hid, block), BF16),
            pltpu.VMEM((hid, wide), BF16),
            pltpu.VMEM((p.pool_wide, windows), F32),
            pltpu.VMEM((p.horizon, windows), F32),
            pltpu.VMEM((block, min(512, windows)), F32),
            pltpu.VMEM((block, min(512, windows)), F32),
            pltpu.VMEM((block, 1), F32),
            pltpu.SemaphoreType.DMA((4, 2)),
        ],
        compiler_params=pltpu.CompilerParams(vmem_limit_bytes=56 * MIB),
        cost_estimate=pl.CostEstimate(
            flops=2 * windows * hid * (2 * p.length + p.horizon), bytes_accessed=windows * p.length * 8, transcendentals=0
        ),
    )(packed, history, cotangent, theta, h3, gfine, pool, fine_bias, slices, bias_rows)


def pack(plan, arrays, biases):
    p = plan
    names = sorted(p.at, key=p.at.get)
    ends = [p.at[name] for name in names[1:]] + [p.columns]
    columns = []
    for name, end in zip(names, ends):
        piece = arrays[name] if name != "bias" else biases
        columns.append(jnp.pad(piece.astype(BF16), ((0, 0), (0, end - p.at[name] - piece.shape[1]))))
    return jnp.concatenate(columns, axis=1)


def unpack(plan, slices_ref, bias_rows_ref, grads):
    p = plan
    hid = p.hidden

    def joined(name, out, source, row=None):
        size, done = out.shape[1], 0
        for section in range(p.sections):
            first = p.start(name, section)
            last = min(first + p.rows(name), size)
            if row is not None:
                for at in range(done, last, LANES):
                    width = min(LANES, last - at)
                    out[:, at : at + width] = source[section, pl.ds(row + (at - first) // LANES, 1), :][:, :width]
            elif done < last:
                at = p.slice_at[name] + done - first
                out[:, done:last] = source[section, :, at : at + last - done].astype(F32)
            done = max(done, last)

    def ones_column(name, row):
        section = p.sections - 1
        at = p.slice_at[name] + row - p.start(name, section)
        block = slices_ref[section, :, at // LANES * LANES : at // LANES * LANES + LANES].astype(F32)
        return block.T[at % LANES : at % LANES + 1]

    def own_part(name, out):
        per = out.shape[1]
        width = min(per, LANES)
        share = p.part[name][0]
        for at in range(0, per, width):
            first = lax.axis_index("dp") * per + at
            block = first // LANES
            row = bias_rows_ref[block // share, pl.ds(p.bias_at[name] + block % share, 1), :]
            wide = jnp.broadcast_to(row, (8, LANES))
            out[:, at : at + width] = pltpu.roll(wide, (LANES - first % LANES) % LANES, 1)[:1, :width]

    for base, block in ((0, "coarse_"), (8, "fine_")):
        entry, head = block + "entry", block + "head"
        joined(entry, grads[base], slices_ref)
        grads[base + 1][...] = ones_column(entry, grads[base].shape[1])
        for i, name in enumerate((block + "middle", block + "upper")):
            joined(name, grads[base + 2 + 2 * i], slices_ref)
            own_part(name, grads[base + 3 + 2 * i])
        joined(head, grads[base + 6], slices_ref)
        joined(head, grads[base + 7], bias_rows_ref, p.bias_at[head])


def body(mesh_shape, history, targets, horizon, cotangent, *params):
    (c_entry, c_entry_b, c_middle, c_middle_b, c_upper, c_upper_b, c_head, c_head_b) = params[:8]
    (f_entry, f_entry_b, f_middle, f_middle_b, f_upper, f_upper_b, f_head, f_head_b) = params[8:]
    sections = mesh_shape["section"]
    length, hidden = f_entry.shape[0], c_middle.shape[1]
    p = Plan(
        length, f_head.shape[1] - length, hidden, c_entry.shape[0], c_head.shape[1], sections, history.shape[0]
    )
    pieces = (c_entry.T, c_middle, c_upper, c_head, f_entry.T, f_middle, f_upper, f_head)
    bias_pieces = (c_entry_b, c_middle_b, c_upper_b, f_entry_b, f_middle_b, f_upper_b)
    dp_count, per = mesh_shape["dp"], c_middle.shape[0]
    rows = (history.T, cotangent.T)
    fine_bias = f_head_b[None, :]
    rest = (targets.T, horizon[None, :], c_head_b[None, :], fine_bias)
    groups = dp_count // 2
    if sections == 4 and dp_count % 2 == 0 and per % 64 == 0 and groups > 1:
        theta, h3, gfine, pool, packed, slices, bias_rows = core(
            p, per, groups, *rows, *rest, pieces + tuple(b[None, :] for b in bias_pieces)
        )
    else:
        packed = pack(p, dict(zip(NAMES, pieces)), jnp.stack(bias_pieces, axis=1))
        packed = lax.all_gather(packed, "dp", axis=0, tiled=True)
        theta, h3, gfine, pool, part, head_bias = core(p, per, 0, *rows, *rest, (packed,))
        own = lax.psum_scatter(part.astype(F32), "dp", scatter_dimension=0, tiled=True)
        slices = lax.all_gather(own, "section", axis=0)
        bias_rows = lax.all_gather(lax.psum(head_bias, "dp"), "section", axis=0)
    residual, history_grad, prediction, *grads = outputs(
        p, packed, *rows, theta, h3, gfine, pool, fine_bias, slices, bias_rows
    )
    grads = [g.T if i in (0, 8) else g if g.shape[0] > 1 else g[0] for i, g in enumerate(grads)]
    return (prediction.T, residual.T, history_grad.T) + tuple(grads)


def solution(mesh):
    by_row, by_column, by_entry, copied = P("dp", None), P(None, "dp"), P("dp"), P()
    block = (by_column, by_entry, by_row, by_entry, by_row, by_entry, by_row, copied)
    in_specs = (by_row, by_row, by_entry, by_row) + block + block
    out_specs = (by_row, by_row, by_row) + block + block
    return jax.shard_map(
        functools.partial(body, dict(mesh.shape)), mesh=mesh, in_specs=in_specs, out_specs=out_specs, check_vma=False
    )
```

time: 1900 us -> 171 us (0.09)
  waiting for transfers between devices: 879 us -> 0 us
  local copies, waits for them, and re-layouts: 462 us -> 2.64 us
  other arithmetic: 195 us -> 1.37 us
  starting transfers between devices: 175 us -> 0 us
  Pallas kernels: 0 us -> 163 us
  matrix products: 84.6 us -> 0 us
  blocking collectives: 39.3 us -> 0 us
  loops' own time: 33.1 us -> 0 us
    unnamed x7 -> x0, waiting for transfers between devices: 522 us -> none
    all_gather x2 -> x0, waiting for transfers between devices: 186 us -> none  [the longest x1 185 us: body(): lax.all_gather(my_rows, 'section', axis=0, tiled=True)]
    ppermute x24 -> x0, starting transfers between devices: 175 us -> none  [from_behind(): return lax.ppermute(block, axis, route)]
    pallas_call x0 -> x2, Pallas kernels: none -> 163 us  [the longest x1 132 us: core(): pl.pallas_call(functools.partial(core_kernel, p, per, groups), out_shape=...]
    psum x1 -> x0, waiting for transfers between devices: 110 us -> none  [body(): lax.psum((jnp.where(first_block, own_grads, zero_flat), jnp.where(first_b...]
    unnamed x131 -> x0, local copies, waits for them, and re-layouts: 99.8 us -> none
    reshape x45 -> x0, local copies, waits for them, and re-layouts: 89.8 us -> none  [the longest x12 23.1 us: pack_rows(): gradient.reshape(row_count, -1)]
    dot_general x78 -> x0, matrix products: 84.6 us -> none  [the longest x24 40.7 us: contract_rows(): lax.dot_general(left_side, right_side, (((0,), (0,)), ((), ())), preferre...]
  transfers between devices with their start and end apart: 29 -> 0, of which waited for: 13 -> 0; matrix products, arithmetic and copies ran while one was open for 27% -> 0% of each run, Pallas kernels for 0% -> 0%
where the time goes in v1:
time: 171 us; the launch traced here: 168 us
  Pallas kernels  163 us (95%)
  local copies, waits for them, and re-layouts  2.64 us (2%)
    pallas_call x1, Pallas kernels, core(): pl.pallas_call(functools.partial(core_kernel, p, per, groups), out_shape=...  132 us
    pallas_call x1, Pallas kernels, outputs(): pl.pallas_call(functools.partial(outputs_kernel, p, block, steps), grid=(...  31.7 us

profile of v1, /device:TPU:8, one launch (start us, length us, event | category | flops | bytes accessed | tf_op | source)
XLA Modules:
  0.0 167.9 jit_solution(8297257148992531672)
XLA Ops:
  0.7 1.3 broadcast_in_dim.27.refs_3_
  2.0 1.3 broadcast_in_dim.29.refs_5_.fine_bias_ref
  3.3 131.5 %shard_map.339 = (f32[256,1536]{1,0:T(8,128)}, bf16[512,1536]{1,0:T(8,128)(2,1)}, bf16[512,1536]{1,0:T(8,128)(2,1)}, bf16[512,1536]{1,0:T(8,128)(2,1)}, bf16[512...) custom-call(bf16[3600,1536]{1,0:T(8,128)(2,1)} %bitcast.24, bf16[3600,1536]{1,0:T(8,128)(2,1)} %bitcast.26, ...), custom_call_target="tpu_custom_call" | custom-call | flops 30181687296 | bytes 22118400 | tf_op jit(solution)/shard_map/pallas_call | solution.py:908
  134.9 31.7 %shard_map.340 = (bf16[3600,1536]{1,0:T(8,128)(2,1)}, bf16[3600,1536]{1,0:T(8,128)(2,1)}, f32[720,1536]{1,0:T(8,128)}, f32[64,450]{1,0:T(8,128)}, f32[1,64]{1,0:...) custom-call(bf16[512,11008]{1,0:T(8,128)(2,1)} %get-tuple-element.45, ...), custom_call_target="tpu_custom_call" | custom-call | flops 12457082880 | bytes 44236800 | tf_op jit(solution)/shard_map/pallas_call | solution.py:1046
  166.5 1.4 reduce

commit v2 on v1

--- a/solution.py
+++ b/solution.py
@@ -47,7 +47,6 @@
             self.at[name] = place
             place += width
         self.columns = place
-        self.knots_wide = up(self.back, ONES)
         self.low = length // LANES * LANES
         self.skip = length - self.low
         self.square = hidden // sections
@@ -88,10 +87,9 @@
 
 def gelu_both(a):
     square = a * a
-    t = jnp.tanh(a * (GELU_A + GELU_B * square))
-    half = 0.5 * a
-    slope = 0.5 + 0.5 * t + half * (1.0 - t * t) * (GELU_A + (3.0 * GELU_B) * square)
-    return half + half * t, slope
+    v = 0.5 + 0.5 * jnp.tanh(a * (GELU_A + GELU_B * square))
+    h = a * v
+    return h, v + h * (1.0 - v) * (2.0 * GELU_A + (6.0 * GELU_B) * square)
 
 
 def dot(a, b):
@@ -118,14 +116,18 @@
     return jnp.concatenate(columns, axis=0)
 
 
-def hat_weights(first, count, plan, turned=False):
-    shape = (plan.knots_wide, count) if turned else (count, plan.theta_wide)
+def hat_weights(first, count, plan, turned=False, fore=False):
+    p = plan
+    shape = (p.knot_rows, count) if turned else (count, p.theta_wide)
     row = lax.broadcasted_iota(jnp.int32, shape, 1 if turned else 0) + first
     knot = lax.broadcasted_iota(jnp.int32, shape, 0 if turned else 1)
     away = row - KNOT * knot
     weight = jnp.maximum(KNOT - jnp.abs(away), 0)
-    weight = jnp.where((knot == plan.back - 1) & (away > 0), KNOT, weight)
-    return jnp.where((knot < plan.back) & (row < plan.length), weight, 0).astype(F32).astype(BF16)
+    last = (knot == p.back - 1) | (knot == p.back + p.fore - 1)
+    weight = jnp.where(last & (away > 0) & (away < KNOT), KNOT, weight)
+    own = (knot >= p.back) & (row >= p.length) if fore else (knot < p.back) & (row < p.length)
+    inside = own & (row < p.fine_out) & (knot < p.back + p.fore)
+    return jnp.where(inside, weight, 0).astype(F32).astype(BF16)
 
 
 def fractions(width):
@@ -269,11 +271,11 @@
             self.to_partner(k, j).start()
 
     def turn(self, t):
-        for depth, stage in enumerate((self.second, self.third, self.fourth)):
+        for depth, stage in ((2, self.fourth), (1, self.third), (0, self.second)):
             if 0 <= t - depth < self.chunks:
                 stage(t - depth)
-            if depth == 0 and t + self.ahead < self.chunks:
-                self.first(t + self.ahead)
+        if t + self.ahead < self.chunks:
+            self.first(t + self.ahead)
 
     def complete(self, k):
         for j in range(self.way.groups):
@@ -291,10 +293,10 @@
 
 
 class Reduce:
-    def __init__(self, plan, way, per, cuts, part_ref, core_in, far_in, far_out, out_ref, send, recv):
+    def __init__(self, plan, way, per, cuts, part_ref, core_in, far_in, far_out, stage_ref, out_ref, send, recv, local):
         self.p, self.way, self.per, self.cuts = plan, way, per, cuts
         self.part_ref, self.core_in, self.far_in, self.far_out = part_ref, core_in, far_in, far_out
-        self.out_ref, self.send, self.recv = out_ref, send, recv
+        self.stage_ref, self.out_ref, self.send, self.recv, self.local = stage_ref, out_ref, send, recv, local
         self.near = range(1, way.groups)
         self.chunks = len(cuts) - 1
 
@@ -319,7 +321,13 @@
         return remote(here, here, self.send.at[k, i, 2], self.recv.at[k, i, 2], to)
 
     def to_side(self, k, i):
-        return self.side(k, self.way.section, i, self.way.sides[i])
+        here = self.stage_ref.at[:, self.columns(k)]
+        there = self.out_ref.at[self.way.section, :, self.columns(k)]
+        return remote(here, there, self.send.at[k, i, 2], self.recv.at[k, i, 2], self.way.sides[i])
+
+    def keep(self, k):
+        there = self.out_ref.at[self.way.section, :, self.columns(k)]
+        return pltpu.make_async_copy(self.stage_ref.at[:, self.columns(k)], there, self.local.at[k])
 
     def to_across(self, k):
         i = k % 2
@@ -345,9 +353,10 @@
         for j in self.near:
             self.to_far(k, j).wait_recv()
             total += self.far_in(j - 1, k)[...].astype(F32)
-        self.out_ref[self.way.section, :, self.columns(k)] = total.astype(BF16)
+        self.stage_ref[:, self.columns(k)] = total.astype(BF16)
         for i in range(2):
             self.to_side(k, i).start()
+        self.keep(k).start()
 
     def fourth(self, k):
         i = k % 2
@@ -367,6 +376,7 @@
         for i in range(2):
             self.to_side(k, i).wait_send()
         self.to_across(k).wait_send()
+        self.keep(k).wait()
 
 
 class ReduceBias:
@@ -438,13 +448,16 @@
         kept_out, slices_out, bias_out = take(3)
     else:
         slice_out, bias_out = take(2)
-    w_ref, big_ref, h_ref, g_ref, r1_ref, pooled_ref, split_ref, theta_ref, gtheta_ref, gknot_ref = take(10)
-    pw_ref, pwt_ref, f32_ref, product_ref, bias_ref = take(5)
-    fore_bias_ref, horizon_buf, coarse_bias_buf, fine_bias_buf, sems = take(5)
+    w_ref, big_ref = take(2)
+    h_refs, g_refs = take(6), take(6)
+    r1_ref, pooled_ref, split_ref, theta_ref, gtheta_ref, gknot_ref = take(6)
+    pw_ref, pwt_ref, turned_ref, even_ref, odd_ref, bias_ref = take(6)
+    horizon_buf, coarse_bias_buf, fine_bias_buf, sems = take(4)
     if groups:
         shards = take(14)
         shard_sems, send, recv, partner_recv = take(4)
-        head_bias_ref, bias_in, bias_far, far_first, ready, reduce_send, reduce_recv, bias_send, bias_recv = take(9)
+        head_bias_ref, bias_in, bias_far, stage_ref, ready, reduce_send, reduce_recv, bias_send, bias_recv = take(9)
+        keep_sems = take(1)[0]
     else:
         head_bias_ref = bias_out
     hid, windows = p.hidden, p.windows
@@ -466,8 +479,8 @@
         load(fine_bias_ref, fine_bias_buf, 5),
     ]
     theta_copy = load(theta_ref, theta_out, 6)
-    h3_copy = load(h_ref.at[5, H], h3_out, 7)
-    gfine_copy = load(g_ref.at[3], gfine_out, 8)
+    h3_copy = load(h_refs[5].at[H], h3_out, 7)
+    gfine_copy = load(g_refs[3], gfine_out, 8)
     pool_copy = load(pooled_ref, pool_out, 9)
 
     if groups:
@@ -483,7 +496,7 @@
         entry_cut = place + up((middle - place) // 2, LANES)
         cuts = (0, 2 * hid, place, entry_cut, middle, middle + third, middle + 2 * third, p.columns)
         gather = Gather(p, way, per, cuts, w_ref, shards[:8], shards[8:], send, recv, partner_recv)
-        history_in.start()
+        cotangent_in.start()
         for copy in rows_in:
             copy.start()
         barrier = pltpu.get_barrier_semaphore()
@@ -499,7 +512,7 @@
     else:
         weights_in = load(packed_ref, w_ref, 10)
         weights_in.start()
-        history_in.start()
+        cotangent_in.start()
         for copy in rows_in:
             copy.start()
 
@@ -517,107 +530,136 @@
     big_ref[p.length :, :] = mark.astype(F32).astype(BF16)
     pooled_ref[...] = jnp.zeros_like(pooled_ref)
     for index in range(6):
-        h_ref[index, hid:, :] = jnp.ones((ONES, windows), BF16)
+        h_refs[index][hid:, :] = jnp.ones((ONES, windows), BF16)
     for copy in rows_in:
         copy.wait()
-    fore_bias_ref[...] = column_of(fine_bias_buf, p.low, p.wide_out - p.low)
+    step = 6 * LANES
+
+    def adjoint(low, high, fore):
+        for first in range(low, high, step):
+            count = min(step, high - first)
+            hats = hat_weights(first, count, p, True, fore)
+
+            @pl.loop(0, chunks)
+            def _(n):
+                lanes = lanes_of(n)
+                part = dot(hats, big_ref[first : first + count, lanes]) * (-1.0 / KNOT)
+                if first == 0:
+                    gtheta_ref[:, lanes] = part
+                else:
+                    gtheta_ref[:, lanes] += part
+
+    cotangent_in.wait()
+    adjoint(0, p.wide_in, False)
+    history_in.start()
+    turn(0)
+    turn(1)
     history_in.wait()
-    turn(0)
-
-    pool_unit = LANES
-    pool_count = p.wide_in // pool_unit
-
-    def pool(i):
-        rows = aligned(i * pool_unit, pool_unit, pool_unit)
-        for c in range(windows // LANES):
-            lanes = slice(c * LANES, (c + 1) * LANES)
-            f32_ref[c] = big_ref[rows, lanes].astype(F32)
-            total = f32_ref[c, pl.ds(0, pool_unit // POOL, stride=POOL), :]
-            for j in range(1, POOL):
-                total += f32_ref[c, pl.ds(j, pool_unit // POOL, stride=POOL), :]
-            pooled_ref[aligned(i * (pool_unit // POOL), pool_unit // POOL, ONES), lanes] = (total * (1.0 / POOL)).astype(BF16)
-
-    pieces = 4
-    for piece in range(pieces):
-        pl.loop(pool_count * piece // pieces, pool_count * (piece + 1) // pieces)(pool)
-        if piece + 1 < pieces:
-            turn(piece + 1)
+
+    unit = hid
+    shape = (unit // POOL, unit)
+    member = lax.broadcasted_iota(jnp.int32, shape, 1) - POOL * lax.broadcasted_iota(jnp.int32, shape, 0)
+    turned_ref[: unit // POOL, :] = ((member >= 0) & (member < POOL)).astype(F32).astype(BF16)
+    firsts = list(range(0, p.wide_in, unit))
+    for number, first in enumerate(firsts):
+        count = min(unit, p.wide_in - first)
+        rows = slice(first // POOL, (first + count) // POOL)
+
+        @pl.loop(0, chunks)
+        def _(n):
+            lanes = lanes_of(n)
+            total = dot(turned_ref[: count // POOL, :count], big_ref[first : first + count, lanes])
+            pooled_ref[rows, lanes] = (total * (1.0 / POOL)).astype(BF16)
+
+        if number in (len(firsts) // 2, len(firsts) - 1):
+            turn(2 + number // (len(firsts) - 1))
     complete(0, 1)
     if not groups:
         weights_in.wait()
-    bias_ref[...] = w_ref[:, p.at["bias"] : p.at["bias"] + LANES].astype(F32)
+    fore_parts = [(0, 8 * p.pair), (8 * p.pair, p.horizon)]
+    fore_bias = column_of(fine_bias_buf, p.low, p.wide_out - p.low)
+    placed = w_ref[:, p.at["bias"] : p.at["bias"] + LANES].astype(F32)
+    lane = lax.broadcasted_iota(jnp.int32, (hid, LANES), 1)
+    for number, (low, high) in enumerate(fore_parts):
+        column = fore_bias[p.skip + low : p.skip + high]
+        column = jnp.concatenate([column, jnp.zeros((hid - high + low, 1), F32)], axis=0)
+        placed = jnp.where(lane == 6 + number, column, placed)
+    bias_ref[...] = placed
+
+    def pipeline(*layers):
+        tile, pending = 0, nothing
+        for before, produce, finish, after in layers:
+            before()
+            for n in range(chunks):
+                lanes = slice(n * chunk, (n + 1) * chunk)
+                out = (even_ref, odd_ref)[tile % 2]
+                value = produce(lanes)
+                out[: value.shape[0], :] = value
+                pending()
+                pending = functools.partial(finish, out, lanes)
+                tile += 1
+            after()
+        pending()
+
+    def nothing():
+        pass
+
+    def turn_weight(first, count):
+        turned_ref[:count, :] = w_ref[:, first : first + count].T
 
     strip = ONES
 
-    def strips():
-        for r in range(0, hid, strip):
+    def activate(index):
+        def finish(source, lanes):
+            for r in range(0, hid, strip):
+                rows = slice(r, r + strip)
+                h, slope = gelu_both(source[rows, :] + bias_ref[rows, index : index + 1])
+                h_refs[index][rows, lanes] = h.astype(BF16)
+                g_refs[index][rows, lanes] = slope.astype(BF16)
+
+        return finish
+
+    def hidden(name, index, after=nothing):
+        return (
+            lambda: turn_weight(p.at[name], hid),
+            lambda lanes: dot(turned_ref[H, :], h_refs[index - 1][H, lanes]),
+            activate(index),
+            after,
+        )
+
+    at_entry = p.at["coarse_entry"]
+    at_head = p.at["coarse_head"]
+    theta_bias = column_of(coarse_bias_buf, 0, p.theta_wide)
+
+    def keep_theta(source, lanes):
+        for r in range(0, p.theta_wide, strip):
             rows = slice(r, r + strip)
-            yield product_ref[rows, :], rows
-
-    def activate(a, index, lanes):
-        product_ref[H, :] = a
-        for value, rows in strips():
-            h, slope = gelu_both(value + bias_ref[rows, index : index + 1])
-            h_ref[index, rows, lanes] = h.astype(BF16)
-            g_ref[index, rows, lanes] = slope.astype(BF16)
-
-    def tiles(body):
-        @pl.loop(0, chunks)
-        def _(n):
-            body(lanes_of(n))
-
-    def hidden_layer(name, index):
-        at = p.at[name]
-        turned = w_ref[:, at : at + hid].T
-        tiles(lambda lanes: activate(dot(turned, h_ref[index - 1, H, lanes]), index, lanes))
-
-    at_entry = p.at["coarse_entry"]
-    tiles(
-        lambda lanes: activate(dot(w_ref[:, at_entry : at_entry + p.pool_wide], pooled_ref[:, lanes]), 0, lanes)
+            theta = source[rows, :] + theta_bias[rows]
+            if r < p.knot_rows:
+                theta_ref[rows, lanes] = theta
+            knots = jnp.where(lax.broadcasted_iota(jnp.int32, theta.shape, 0) + r < p.back, theta, 0.0)
+            high = knots.astype(BF16)
+            split_ref[rows, lanes] = high
+            split_ref[p.theta_wide + r : p.theta_wide + r + strip, lanes] = (knots - high.astype(F32)).astype(BF16)
+
+    pipeline(
+        (
+            nothing,
+            lambda lanes: dot(w_ref[:, at_entry : at_entry + p.pool_wide], pooled_ref[:, lanes]),
+            activate(0),
+            lambda: turn(4),
+        ),
+        hidden("coarse_middle", 1, lambda: turn(5)),
+        hidden("coarse_upper", 2),
+        (
+            lambda: turn_weight(at_head, p.theta_wide),
+            lambda lanes: dot(turned_ref[: p.theta_wide, :], h_refs[2][H, lanes]),
+            keep_theta,
+            nothing,
+        ),
     )
-    turn(4)
-    hidden_layer("coarse_middle", 1)
-    turn(5)
-    hidden_layer("coarse_upper", 2)
-    at_head = p.at["coarse_head"]
-    turned_head = w_ref[:, at_head : at_head + p.theta_wide].T
-    theta_bias = column_of(coarse_bias_buf, 0, p.theta_wide)
-    used = lax.broadcasted_iota(jnp.int32, (p.theta_wide, chunk), 0) < p.back
-
-    @pl.loop(0, chunks)
-    def _(n):
-        lanes = lanes_of(n)
-        theta = dot(turned_head, h_ref[2, H, lanes]) + theta_bias
-        theta_ref[:, lanes] = theta
-        knots = jnp.where(used, theta, 0.0)
-        high = knots.astype(BF16)
-        split_ref[: p.theta_wide, lanes] = high
-        split_ref[p.theta_wide :, lanes] = (knots - high.astype(F32)).astype(BF16)
-
     theta_copy.start()
     turn(6)
-    complete(2, 3)
-
-    total = jnp.zeros((hid, p.theta_wide), F32)
-    step = 6 * LANES
-    for first in range(0, p.wide_in, step):
-        count = min(step, p.wide_in - first)
-        total += dot(w_ref[:, place + first : place + first + count], hat_weights(first, count, p))
-    product = (total * (1.0 / KNOT)).astype(BF16)
-    pwt_ref[:, : p.theta_wide] = product
-    pwt_ref[:, p.theta_wide :] = product
-    pw_ref[...] = product.T
-
-    def fine_entry(lanes):
-        a = dot(w_ref[:, place : place + p.wide_in], big_ref[: p.wide_in, lanes])
-        activate(a - dot(pwt_ref[...], split_ref[:, lanes]), 3, lanes)
-
-    for n in range(chunks):
-        fine_entry(slice(n * chunk, (n + 1) * chunk))
-        if n < 2:
-            turn(7 + n)
-    if chunks < 2:
-        turn(8)
 
     first_pair = p.start("fine_entry", section) // p.pair
 
@@ -639,16 +681,67 @@
         made = made * (pair < p.back // 2).astype(F32)
         r1_ref[aligned(i * p.pair, p.pair, ONES), :] = (big_ref[source, :].astype(F32) - made).astype(BF16)
 
-    cotangent_in.start()
-    target_in.start()
-    big_ref[p.fine_out :, :] = jnp.zeros((p.wide_out - p.fine_out, windows), BF16)
-    if groups:
-        signal(ready.at[0], way.all())
-    complete(4)
-    hidden_layer("fine_middle", 4)
-    hidden_layer("fine_upper", 5)
+    turn(7)
+    complete(2, 3)
+
+    total = jnp.zeros((hid, p.theta_wide), F32)
+    for first in range(0, p.wide_in, step):
+        count = min(step, p.wide_in - first)
+        total += dot(w_ref[:, place + first : place + first + count], hat_weights(first, count, p))
+    product = (total * (1.0 / KNOT)).astype(BF16)
+    pwt_ref[...] = product
+    pw_ref[...] = product.T
+    turn(8)
+
+    def fine_entry(lanes):
+        a = dot(w_ref[:, place : place + p.wide_in], big_ref[: p.wide_in, lanes])
+        for part in (0, p.theta_wide):
+            a -= dot(pwt_ref[...], split_ref[part : part + p.theta_wide, lanes])
+        return a
+
+    def entry_made():
+        cotangent_in.start()
+        target_in.start()
+        big_ref[p.fine_out :, :] = jnp.zeros((p.wide_out - p.fine_out, windows), BF16)
+        if groups:
+            signal(ready.at[0], way.all())
+        complete(4)
+
+    rest_c, later_c = fractions(chunk)
+
+    def fore(number):
+        low, high = fore_parts[number]
+
+        def before():
+            if number == 0:
+                complete(5, 6)
+                target_in.wait()
+            first = head_at + p.low
+            turned = w_ref[:, first : first + p.wide_out - p.low].T
+            turned_ref[: high - low, :] = turned[p.skip + low : p.skip + high]
+
+        def finish(source, lanes):
+            for k in range(low // KNOT, high // KNOT, 2):
+                here = slice(k * KNOT - low, (k + 2) * KNOT - low)
+                second = source[here, :] + bias_ref[here, 6 + number : 7 + number]
+                first = jnp.concatenate(
+                    [interpolate(p.back, p.fore, k + j, rest_c, later_c, lanes) for j in range(2)], axis=0
+                )
+                counts = (lax.broadcasted_iota(jnp.int32, (2 * KNOT, chunk), 0) + k * KNOT) < horizon_buf[:, lanes]
+                there = slice(p.length + k * KNOT, p.length + (k + 2) * KNOT)
+                error = first + second - big_ref[there, lanes].astype(F32)
+                big_ref[there, lanes] = jnp.where(counts, -error, 0.0).astype(BF16)
+
+        return before, lambda lanes: dot(turned_ref[: high - low, :], h_refs[5][H, lanes]), finish, nothing
+
+    pipeline(
+        (nothing, fine_entry, activate(3), entry_made),
+        hidden("fine_middle", 4),
+        hidden("fine_upper", 5),
+        fore(0),
+        fore(1),
+    )
     h3_copy.start()
-    complete(5, 6)
     if groups:
         kept = [
             load(w_ref.at[:, p.at[name] : p.at[name] + wide], kept_out.at[:, p.at[name] : p.at[name] + wide], 10 + n)
@@ -656,39 +749,10 @@
         ]
         for copy in kept:
             copy.start()
-
-    rest_c, later_c = fractions(chunk)
-    turned_fore = w_ref[:, head_at + p.low : head_at + p.wide_out].T
-    target_in.wait()
-
-    @pl.loop(0, chunks)
-    def _(n):
-        lanes = lanes_of(n)
-        before = jnp.zeros((1, chunk), F32)
-        product_ref[: p.horizon, :] = dot(turned_fore[p.skip : p.skip + p.horizon], h_ref[5, H, lanes])
-        for k in range(0, p.fore, 2):
-            here = slice(k * KNOT, (k + 2) * KNOT)
-            second = product_ref[here, :] + fore_bias_ref[p.skip + k * KNOT : p.skip + (k + 2) * KNOT, :]
-            first = jnp.concatenate(
-                [interpolate(p.back, p.fore, k + j, rest_c, later_c, lanes) for j in range(2)], axis=0
-            )
-            counts = (lax.broadcasted_iota(jnp.int32, (2 * KNOT, chunk), 0) + k * KNOT) < horizon_buf[:, lanes]
-            there = slice(p.length + k * KNOT, p.length + (k + 2) * KNOT)
-            error = first + second - big_ref[there, lanes].astype(F32)
-            gradient = jnp.where(counts, error, 0.0)
-            big_ref[there, lanes] = (-gradient).astype(BF16)
-            for j in range(2):
-                part = gradient[j * KNOT : (j + 1) * KNOT]
-                own = jnp.sum(part * rest_c, axis=0, keepdims=True)
-                after = jnp.sum(part * later_c, axis=0, keepdims=True)
-                last = after if k + j == p.fore - 1 else 0.0
-                gtheta_ref[p.back + k + j : p.back + k + j + 1, lanes] = own + before + last
-                before = after
-
     cotangent_in.wait()
 
     def gradient_slice(name, left, right_ref, first, step=LANES, sign=1.0):
-        left_side = left if name.endswith("entry") else h_ref[left]
+        left_side = left[...] if name.endswith("entry") else h_refs[left][...]
         for b in range(0, p.rows(name), step):
             width = min(step, p.rows(name) - b)
             value = sign * dot_rows(left_side, right_ref[aligned(first + b, width, ONES), :])
@@ -700,19 +764,19 @@
                     head_bias_ref[row : row + 1, :] = value[hid : hid + 1, c : c + LANES]
 
     def square_slice(name, index):
-        gradient_slice(name, index - 1, g_ref.at[index], p.start(name, section))
-
-    def back_layer(product, index):
-        def body(lanes):
-            product_ref[H, :] = product(lanes)
-            for value, rows in strips():
-                g_ref[index, rows, lanes] = (value * g_ref[index, rows, lanes].astype(F32)).astype(BF16)
-
-        tiles(body)
+        gradient_slice(name, index - 1, g_refs[index], p.start(name, section))
+
+    def back(index, product, after=nothing):
+        def finish(source, lanes):
+            for r in range(0, hid, strip):
+                rows = slice(r, r + strip)
+                g_refs[index][rows, lanes] = (source[rows, :] * g_refs[index][rows, lanes].astype(F32)).astype(BF16)
+
+        return nothing, product, finish, after
 
     def times(name, index):
         at = p.at[name]
-        return lambda lanes: dot(w_ref[:, at : at + hid], g_ref[index, :, lanes])
+        return lambda lanes: dot(w_ref[:, at : at + hid], g_refs[index][:, lanes])
 
     if groups:
         for copy in kept:
@@ -729,8 +793,6 @@
             return w_ref.at[rows, first : first + width(k)]
 
         def departures(j, k):
-            if k == 0:
-                return far_first.at[j * per : (j + 1) * per, :]
             first = (k * groups + j) * per
             return big_ref.at[first : first + per, : width(k)]
 
@@ -743,9 +805,11 @@
             arrivals,
             lambda j, k: arrivals(groups + j, k),
             departures,
+            stage_ref,
             slices_out,
             reduce_send,
             reduce_recv,
+            keep_sems,
         )
         reduce_bias = ReduceBias(way, head_bias_ref, bias_in, bias_far, bias_out, bias_send, bias_recv)
 
@@ -754,52 +818,45 @@
         pl.semaphore_wait(ready.at[0], len(way.all()))
         reduce.first(0)
 
-    back_layer(lambda lanes: -dot(w_ref[:, head_at : head_at + p.wide_out], big_ref[:, lanes]), 5)
-    if groups:
-        signal(ready.at[1], way.all())
-        reduce.second(0)
-
-    for first in range(0, p.wide_in, step):
-        count = min(step, p.wide_in - first)
-        hats = hat_weights(first, count, p, True)
-
-        @pl.loop(0, chunks)
-        def _(n):
-            lanes = lanes_of(n)
-            part = dot(hats, big_ref[first : first + count, lanes])[: p.back] * (-1.0 / KNOT)
-            if first == 0:
-                gtheta_ref[: p.back, lanes] = part
-            else:
-                gtheta_ref[: p.back, lanes] += part
-
-    back_layer(times("fine_upper", 5), 4)
-    back_layer(times("fine_middle", 4), 3)
+    adjoint(p.low, p.wide_out, True)
+
+    def head_used():
+        if groups:
+            signal(ready.at[1], way.all())
+            reduce.second(0)
+
+    pipeline(
+        back(5, lambda lanes: -dot(w_ref[:, head_at : head_at + p.wide_out], big_ref[:, lanes]), head_used),
+        back(4, times("fine_upper", 5)),
+        back(3, times("fine_middle", 4)),
+    )
     gfine_copy.start()
-    gradient_slice("fine_entry", g_ref[3], r1_ref, p.start("fine_entry", section) - first_pair * p.pair, 2 * LANES)
+    gradient_slice("fine_entry", g_refs[3], r1_ref, p.start("fine_entry", section) - first_pair * p.pair, 2 * LANES)
     square_slice("fine_middle", 4)
     square_slice("fine_upper", 5)
     if groups:
         pl.semaphore_wait(ready.at[1], len(way.all()))
         reduce.first(1)
         reduce.third(0)
-    row = lax.broadcasted_iota(jnp.int32, (p.knot_rows, chunk), 0)
     gknot_ref[p.knot_rows :, :] = jnp.zeros((p.theta_wide - p.knot_rows, windows), BF16)
 
-    @pl.loop(0, chunks)
-    def _(n):
-        lanes = lanes_of(n)
-        knots = jnp.where(row < p.coarse_out, gtheta_ref[:, lanes], 0.0)
-        gknot_ref[: p.knot_rows, lanes] = (knots - dot(pw_ref[: p.knot_rows, :], g_ref[3, :, lanes])).astype(BF16)
-
-    back_layer(lambda lanes: dot(w_ref[:, at_head : at_head + p.theta_wide], gknot_ref[:, lanes]), 2)
-    if groups:
-        reduce.second(1)
-    back_layer(times("coarse_upper", 2), 1)
-    if groups:
-        reduce.fourth(0)
-    back_layer(times("coarse_middle", 1), 0)
+    def knots_done(source, lanes):
+        for r in range(0, p.knot_rows, strip):
+            rows = slice(r, r + strip)
+            gknot_ref[rows, lanes] = (gtheta_ref[rows, lanes] - source[rows, :]).astype(BF16)
+
+    pipeline(
+        (nothing, lambda lanes: dot(pw_ref[: p.knot_rows, :], g_refs[3][:, lanes]), knots_done, nothing),
+        back(
+            2,
+            lambda lanes: dot(w_ref[:, at_head : at_head + p.theta_wide], gknot_ref[:, lanes]),
+            lambda: reduce.second(1) if groups else None,
+        ),
+        back(1, times("coarse_upper", 2), lambda: reduce.fourth(0) if groups else None),
+        back(0, times("coarse_middle", 1)),
+    )
     gradient_slice("coarse_head", 2, gknot_ref, p.start("coarse_head", section))
-    gradient_slice("coarse_entry", g_ref[0], pooled_ref, p.start("coarse_entry", section))
+    gradient_slice("coarse_entry", g_refs[0], pooled_ref, p.start("coarse_entry", section))
     square_slice("coarse_middle", 1)
     square_slice("coarse_upper", 2)
     if groups:
@@ -809,14 +866,18 @@
         reduce.second(2)
         reduce_bias.second()
 
-    turned_entry = w_ref[:, at_entry : at_entry + p.pool_wide].T
-
-    def pool_gradient(lanes):
-        product_ref[: p.pool_wide, :] = dot(turned_entry, g_ref[0, :, lanes])
+    def pool_gradient(source, lanes):
         for r in range(0, p.pool_wide, strip):
-            pooled_ref[r : r + strip, lanes] = (product_ref[r : r + strip, :] * (1.0 / POOL)).astype(BF16)
-
-    tiles(pool_gradient)
+            pooled_ref[r : r + strip, lanes] = (source[r : r + strip, :] * (1.0 / POOL)).astype(BF16)
+
+    pipeline(
+        (
+            lambda: turn_weight(at_entry, p.pool_wide),
+            lambda lanes: dot(turned_ref[: p.pool_wide, :], g_refs[0][:, lanes]),
+            pool_gradient,
+            nothing,
+        )
+    )
     pool_copy.start()
     if groups:
         reduce.fourth(1)
@@ -847,7 +908,7 @@
     hid, windows = p.hidden, p.windows
     flops = 2 * windows * hid * (2 * p.length + 2 * p.wide_out // 3 + 12 * hid + p.slice_columns)
     out_shape = [
-        jax.ShapeDtypeStruct((p.theta_wide, windows), F32),
+        jax.ShapeDtypeStruct((p.knot_rows, windows), F32),
         jax.ShapeDtypeStruct((hid, windows), BF16),
         jax.ShapeDtypeStruct((hid, windows), BF16),
         jax.ShapeDtypeStruct((p.pool_wide, windows), BF16),
@@ -856,20 +917,20 @@
     scratch = [
         pltpu.VMEM((hid, p.columns), BF16),
         pltpu.VMEM((p.wide_out, windows), BF16),
-        pltpu.VMEM((6, hid + ONES, windows), BF16),
-        pltpu.VMEM((6, hid, windows), BF16),
+        *[pltpu.VMEM((hid + ONES, windows), BF16)] * 6,
+        *[pltpu.VMEM((hid, windows), BF16)] * 6,
         pltpu.VMEM((p.r1_pairs * p.pair, windows), BF16),
         pltpu.VMEM((p.pool_wide, windows), BF16),
         pltpu.VMEM((2 * p.theta_wide, windows), BF16),
-        pltpu.VMEM((p.theta_wide, windows), F32),
+        pltpu.VMEM((p.knot_rows, windows), F32),
         pltpu.VMEM((p.knot_rows, windows), F32),
         pltpu.VMEM((p.theta_wide, windows), BF16),
         pltpu.VMEM((p.theta_wide, hid), BF16),
-        pltpu.VMEM((hid, 2 * p.theta_wide), BF16),
-        pltpu.VMEM((windows // LANES, LANES, LANES), F32),
-        pltpu.VMEM((max(hid, p.horizon), min(512, windows)), F32),
+        pltpu.VMEM((hid, p.theta_wide), BF16),
+        pltpu.VMEM((hid, hid), BF16),
+        pltpu.VMEM((hid, min(512, windows)), F32),
+        pltpu.VMEM((hid, min(512, windows)), F32),
         pltpu.VMEM((hid, LANES), F32),
-        pltpu.VMEM((p.wide_out - p.low, 1), F32),
         pltpu.VMEM(horizon.shape, jnp.int32),
         pltpu.VMEM(coarse_bias.shape, F32),
         pltpu.VMEM(fine_bias.shape, F32),
@@ -883,7 +944,7 @@
             jax.ShapeDtypeStruct((4, per, p.slice_columns), BF16),
             jax.ShapeDtypeStruct((4,) + bias, F32),
         ]
-        out_specs += [ANY, VMEM, VMEM]
+        out_specs += [ANY, ANY, VMEM]
         chunks, reduce_chunks = 7, 3
         scratch += [pltpu.VMEM(piece.shape, F32) for piece in weights]
         scratch += [
@@ -894,12 +955,13 @@
             pltpu.VMEM(bias, F32),
             pltpu.VMEM(bias, F32),
             pltpu.VMEM((groups,) + bias, F32),
-            pltpu.VMEM(((groups - 1) * per, p.rows("fine_head")), BF16),
+            pltpu.VMEM((per, p.slice_columns), BF16),
             pltpu.SemaphoreType.REGULAR((2,)),
             pltpu.SemaphoreType.DMA((reduce_chunks, max(groups, 3), 3)),
             pltpu.SemaphoreType.DMA((reduce_chunks, max(groups, 3), 3)),
             pltpu.SemaphoreType.DMA((groups + 3,)),
             pltpu.SemaphoreType.DMA((groups + 3,)),
+            pltpu.SemaphoreType.DMA((reduce_chunks,)),
         ]
         params = {"collective_id": 0, "has_side_effects": True}
     else:
@@ -936,13 +998,14 @@
     *refs,
 ):
     grads = refs[:16]
-    head_ref, entry_ref, side_ref, pool_grad, fore_ref, back_ref, fine_ref, bias_ref, sems = refs[16:]
+    head_ref, entry_ref, side_ref, pool_grad, fore_ref, *products, turned_head, turned_entry, bias_ref, sems = refs[16:]
+    back_refs, fine_refs = products[:2], products[2:]
     p = plan
     step = pl.program_id(0)
     windows = p.windows
-    chunk = min(512, p.windows)
+    chunk = min(512, windows)
     chunks = windows // chunk
-    lanes_of = lambda n: aligned(n * chunk, chunk, chunk)
+    lanes_of = lambda n: slice(n * chunk, (n + 1) * chunk) if isinstance(n, int) else aligned(n * chunk, chunk, chunk)
     knots = block // KNOT
     pooled = block // POOL
     rest, later = fractions(chunk)
@@ -978,10 +1041,10 @@
         @pl.loop(0, chunks)
         def _(n):
             lanes = lanes_of(n)
-            back_ref[: p.horizon, :] = dot(turned_fore[p.skip : p.skip + p.horizon], h3_ref[:, lanes])
+            back_refs[0][: p.horizon, :] = dot(turned_fore[p.skip : p.skip + p.horizon], h3_ref[:, lanes])
             for k in range(0, p.fore, 2):
                 rows = slice(k * KNOT, (k + 2) * KNOT)
-                second = back_ref[rows, :] + fore_bias[p.skip + k * KNOT : p.skip + (k + 2) * KNOT]
+                second = back_refs[0][rows, :] + fore_bias[p.skip + k * KNOT : p.skip + (k + 2) * KNOT]
                 first = jnp.concatenate([interpolate(k + j, p.fore, p.back, lanes) for j in range(2)], axis=0)
                 fore_ref[rows, lanes] = first.astype(BF16).astype(F32) + second.astype(BF16).astype(F32)
 
@@ -1000,31 +1063,38 @@
 
     fetch("fine_head", head_ref, step, slot, 0).wait()
     fetch("fine_entry", entry_ref, step, slot, 1).wait()
-    turned_head = head_ref[slot].T
-    turned_entry = entry_ref[slot].T
+    turned_head[...] = head_ref[slot].T
+    turned_entry[...] = entry_ref[slot].T
     row = jnp.broadcast_to(fine_bias_ref[:, aligned(step * block, block, LANES)], (8, block))
     bias_ref[...] = row.T[:, :1]
     pair = 2 * KNOT
 
-    @pl.loop(0, chunks)
-    def _(n):
+    def make(n, place):
         lanes = lanes_of(n)
-        back_ref[...] = dot(turned_head, h3_ref[:, lanes])
-        fine_ref[...] = dot(turned_entry, gfine_ref[:, lanes])
+        back_refs[place][...] = dot(turned_head[...], h3_ref[:, lanes])
+        fine_refs[place][...] = dot(turned_entry[...], gfine_ref[:, lanes])
+
+    def finish(n, place):
+        lanes = lanes_of(n)
         for at in range(0, block, pair):
             rows = slice(at, at + pair)
             k = step * knots + at // KNOT
             made = jnp.concatenate([interpolate(k + j, p.back, 0, lanes) for j in range(2)], axis=0)
-            back = back_ref[rows, :] + bias_ref[rows, :]
+            back = back_refs[place][rows, :] + bias_ref[rows, :]
             residual_ref[rows, lanes] = (history_ref[rows, lanes].astype(F32) - made - back).astype(BF16)
-        for at in range(0, block, pair):
-            rows = slice(at, at + pair)
             first = step * pooled + at // POOL
             spread = jnp.concatenate(
                 [jnp.broadcast_to(pool_grad[pl.ds(first + j, 1), lanes], (POOL, chunk)) for j in range(pair // POOL)],
                 axis=0,
             )
-            history_grad_ref[rows, lanes] = (cotangent_ref[rows, lanes].astype(F32) + fine_ref[rows, :] + spread).astype(BF16)
+            fine = fine_refs[place][rows, :] + spread
+            history_grad_ref[rows, lanes] = (cotangent_ref[rows, lanes].astype(F32) + fine).astype(BF16)
+
+    for n in range(chunks + 1):
+        if n < chunks:
+            make(n, n % 2)
+        if n > 0:
+            finish(n - 1, (n - 1) % 2)
 
     @pl.when(step == steps - 1)
     def _():
@@ -1060,8 +1130,9 @@
             pltpu.VMEM((hid, wide), BF16),
             pltpu.VMEM((p.pool_wide, windows), F32),
             pltpu.VMEM((p.horizon, windows), F32),
-            pltpu.VMEM((block, min(512, windows)), F32),
-            pltpu.VMEM((block, min(512, windows)), F32),
+            *[pltpu.VMEM((block, min(512, windows)), F32)] * 4,
+            pltpu.VMEM((block, hid), BF16),
+            pltpu.VMEM((block, hid), BF16),
             pltpu.VMEM((block, 1), F32),
             pltpu.SemaphoreType.DMA((4, 2)),
         ],

time: 171 us -> 177 us (1.035)
  Pallas kernels: 163 us -> 170 us
    pallas_call x1, Pallas kernels: 132 us -> 141 us  [core(): pl.pallas_call(functools.partial(core_kernel, p, per, groups), out_shape=...]
    pallas_call x1, Pallas kernels: 31.7 us -> 29 us  [outputs(): pl.pallas_call(functools.partial(outputs_kernel, p, block, steps), grid=(...]
where the time goes in v2:
time: 177 us; the launch traced here: 175 us
  Pallas kernels  170 us (96%)
  local copies, waits for them, and re-layouts  2.64 us (1%)
    pallas_call x1, Pallas kernels, core(): pl.pallas_call(functools.partial(core_kernel, p, per, groups), out_shape=...  141 us
    pallas_call x1, Pallas kernels, outputs(): pl.pallas_call(functools.partial(outputs_kernel, p, block, steps), grid=(...  29 us

profile of v2, /device:TPU:8, one launch (start us, length us, event | category | flops | bytes accessed | tf_op | source)
XLA Modules:
  0.0 174.7 jit_solution(3276665693617690236)
XLA Ops:
  0.7 1.3 broadcast_in_dim.27.refs_3_
  2.0 1.3 broadcast_in_dim.29.refs_5_.fine_bias_ref
  3.3 140.8 %shard_map.339 = (f32[192,1536]{1,0:T(8,128)}, bf16[512,1536]{1,0:T(8,128)(2,1)}, bf16[512,1536]{1,0:T(8,128)(2,1)}, bf16[512,1536]{1,0:T(8,128)(2,1)}, bf16[512...) custom-call(bf16[3600,1536]{1,0:T(8,128)(2,1)} %bitcast.24, bf16[3600,1536]{1,0:T(8,128)(2,1)} %bitcast.26, ...), custom_call_target="tpu_custom_call" | custom-call | flops 30181687296 | bytes 22118400 | tf_op jit(solution)/shard_map/pallas_call | solution.py:970
  144.1 29.0 %shard_map.340 = (bf16[3600,1536]{1,0:T(8,128)(2,1)}, bf16[3600,1536]{1,0:T(8,128)(2,1)}, f32[720,1536]{1,0:T(8,128)}, f32[64,450]{1,0:T(8,128)}, f32[1,64]{1,0:...) custom-call(bf16[512,11008]{1,0:T(8,128)(2,1)} %get-tuple-element.45, ...), custom_call_target="tpu_custom_call" | custom-call | flops 12457082880 | bytes 44236800 | tf_op jit(solution)/shard_map/pallas_call | solution.py:1116
  173.1 1.4 reduce

commit v3 on v2

--- a/solution.py
+++ b/solution.py
@@ -52,10 +52,11 @@
         self.square = hidden // sections
         self.slice_at, self.part, place = {}, {}, 0
         for name, width in (
-            ("fine_head", self.wide_out),
+            ("head_back", self.wide_in),
+            ("head_fore", self.wide_out - self.low),
+            ("fine_upper", hidden),
+            ("fine_middle", hidden),
             ("fine_entry", self.wide_in),
-            ("fine_middle", hidden),
-            ("fine_upper", hidden),
             ("coarse_middle", hidden),
             ("coarse_upper", hidden),
             ("coarse_head", self.theta_wide),
@@ -68,7 +69,7 @@
             place += share * LANES
         self.slice_columns = place
         self.bias_at, place = {}, 0
-        for name in ("fine_head", "coarse_head", "coarse_middle", "coarse_upper", "fine_middle", "fine_upper"):
+        for name in ("head_back", "head_fore", "coarse_head", "coarse_middle", "coarse_upper", "fine_middle", "fine_upper"):
             self.bias_at[name] = place
             place += self.part[name][0]
         self.bias_rows = up(place, 8)
@@ -270,26 +271,18 @@
             self.arrived(k, j, 3)
             self.to_partner(k, j).start()
 
-    def turn(self, t):
-        for depth, stage in ((2, self.fourth), (1, self.third), (0, self.second)):
-            if 0 <= t - depth < self.chunks:
-                stage(t - depth)
-        if t + self.ahead < self.chunks:
-            self.first(t + self.ahead)
-
     def complete(self, k):
         for j in range(self.way.groups):
             there = (self.way.from_far(j) * 2 + 1 - self.way.core) if j else self.way.partner[1]
             here = self.at(k, there)
             remote(here, here, self.send.at[k, 0, 5], self.partner_recv.at[k, j], self.way.partner).wait_recv()
 
-    def sent(self):
-        for k in range(self.chunks):
-            for j in self.near:
-                for copy in (self.to_far(k, j), self.to_side(k, j, 0), self.to_side(k, j, 1), self.to_across(k, j)):
-                    copy.wait_send()
-                self.to_partner(k, j).wait_send()
-            self.to_partner(k, 0).wait_send()
+    def sent(self, k):
+        for j in self.near:
+            for copy in (self.to_far(k, j), self.to_side(k, j, 0), self.to_side(k, j, 1), self.to_across(k, j)):
+                copy.wait_send()
+            self.to_partner(k, j).wait_send()
+        self.to_partner(k, 0).wait_send()
 
 
 class Reduce:
@@ -368,11 +361,13 @@
     def complete(self, k):
         self.side(k, self.way.across, 2, self.way.partner).wait_recv()
 
+    def sent_far(self, k):
+        for j in self.near:
+            self.to_far(k, j).wait_send()
+
     def sent(self, k):
         for g in range(self.way.groups):
             self.to_partner(k, g).wait_send()
-        for j in self.near:
-            self.to_far(k, j).wait_send()
         for i in range(2):
             self.to_side(k, i).wait_send()
         self.to_across(k).wait_send()
@@ -462,7 +457,7 @@
         head_bias_ref = bias_out
     hid, windows = p.hidden, p.windows
     section = lax.axis_index("section")
-    chunk = min(512, windows)
+    chunk = min(512, windows // 2)
     chunks = windows // chunk
     H = slice(0, hid)
     lanes_of = lambda n: aligned(n * chunk, chunk, chunk)
@@ -516,9 +511,12 @@
         for copy in rows_in:
             copy.start()
 
-    def turn(t):
+    def move(*steps):
         if groups:
-            gather.turn(t)
+            for stage, k in steps:
+                {2: gather.second, 3: gather.third, 4: gather.fourth}[stage](k)
+                if stage == 2 and k + gather.ahead < gather.chunks:
+                    gather.first(k + gather.ahead)
 
     def complete(*ks):
         if groups:
@@ -535,25 +533,21 @@
         copy.wait()
     step = 6 * LANES
 
-    def adjoint(low, high, fore):
-        for first in range(low, high, step):
-            count = min(step, high - first)
-            hats = hat_weights(first, count, p, True, fore)
-
-            @pl.loop(0, chunks)
-            def _(n):
-                lanes = lanes_of(n)
-                part = dot(hats, big_ref[first : first + count, lanes]) * (-1.0 / KNOT)
-                if first == 0:
-                    gtheta_ref[:, lanes] = part
-                else:
-                    gtheta_ref[:, lanes] += part
+    def adjoint(first, count, fore):
+        hats = hat_weights(first, count, p, True, fore)
+
+        @pl.loop(0, chunks)
+        def _(n):
+            lanes = lanes_of(n)
+            rows = slice(first, first + count) if isinstance(first, int) else aligned(first, count, ONES)
+            gtheta_ref[:, lanes] += dot(hats, big_ref[rows, lanes]) * (-1.0 / KNOT)
 
     cotangent_in.wait()
-    adjoint(0, p.wide_in, False)
+    gtheta_ref[...] = jnp.zeros_like(gtheta_ref)
+    quarter = p.wide_in // 4
+    pl.loop(0, 4)(lambda i: adjoint(i * quarter, quarter, False))
     history_in.start()
-    turn(0)
-    turn(1)
+    move((2, 0), (2, 1), (3, 0))
     history_in.wait()
 
     unit = hid
@@ -571,8 +565,9 @@
             total = dot(turned_ref[: count // POOL, :count], big_ref[first : first + count, lanes])
             pooled_ref[rows, lanes] = (total * (1.0 / POOL)).astype(BF16)
 
-        if number in (len(firsts) // 2, len(firsts) - 1):
-            turn(2 + number // (len(firsts) - 1))
+        if number == len(firsts) // 2:
+            move((4, 0), (3, 1), (2, 2))
+    move((4, 1), (3, 2), (2, 3))
     complete(0, 1)
     if not groups:
         weights_in.wait()
@@ -604,6 +599,18 @@
     def nothing():
         pass
 
+    def looped(*layers):
+        for before, produce, finish, after in layers:
+            before()
+
+            @pl.loop(0, chunks)
+            def _(n, produce=produce, finish=finish):
+                value = produce(lanes_of(n))
+                even_ref[: value.shape[0], :] = value
+                finish(even_ref, lanes_of(n))
+
+            after()
+
     def turn_weight(first, count):
         turned_ref[:count, :] = w_ref[:, first : first + count].T
 
@@ -642,15 +649,16 @@
             split_ref[rows, lanes] = high
             split_ref[p.theta_wide + r : p.theta_wide + r + strip, lanes] = (knots - high.astype(F32)).astype(BF16)
 
-    pipeline(
+    forward = pipeline if groups else looped
+    forward(
         (
             nothing,
             lambda lanes: dot(w_ref[:, at_entry : at_entry + p.pool_wide], pooled_ref[:, lanes]),
             activate(0),
-            lambda: turn(4),
+            nothing,
         ),
-        hidden("coarse_middle", 1, lambda: turn(5)),
-        hidden("coarse_upper", 2),
+        hidden("coarse_middle", 1, lambda: move((4, 2), (2, 4))),
+        hidden("coarse_upper", 2, lambda: move((3, 3))),
         (
             lambda: turn_weight(at_head, p.theta_wide),
             lambda lanes: dot(turned_ref[: p.theta_wide, :], h_refs[2][H, lanes]),
@@ -659,7 +667,10 @@
         ),
     )
     theta_copy.start()
-    turn(6)
+
+    def keep(name, wide, sem):
+        columns = slice(p.at[name], p.at[name] + wide)
+        return load(w_ref.at[:, columns], kept_out.at[:, columns], sem)
 
     first_pair = p.start("fine_entry", section) // p.pair
 
@@ -681,8 +692,12 @@
         made = made * (pair < p.back // 2).astype(F32)
         r1_ref[aligned(i * p.pair, p.pair, ONES), :] = (big_ref[source, :].astype(F32) - made).astype(BF16)
 
-    turn(7)
+    move((4, 3), (2, 5), (3, 4))
     complete(2, 3)
+    kept = []
+    if groups:
+        kept.append(keep("fine_entry", p.wide_in, 10))
+        kept[0].start()
 
     total = jnp.zeros((hid, p.theta_wide), F32)
     for first in range(0, p.wide_in, step):
@@ -691,7 +706,7 @@
     product = (total * (1.0 / KNOT)).astype(BF16)
     pwt_ref[...] = product
     pw_ref[...] = product.T
-    turn(8)
+    move((4, 4), (2, 6), (3, 5))
 
     def fine_entry(lanes):
         a = dot(w_ref[:, place : place + p.wide_in], big_ref[: p.wide_in, lanes])
@@ -705,6 +720,7 @@
         big_ref[p.fine_out :, :] = jnp.zeros((p.wide_out - p.fine_out, windows), BF16)
         if groups:
             signal(ready.at[0], way.all())
+        move((4, 5), (3, 6))
         complete(4)
 
     rest_c, later_c = fractions(chunk)
@@ -713,12 +729,9 @@
         low, high = fore_parts[number]
 
         def before():
-            if number == 0:
-                complete(5, 6)
-                target_in.wait()
-            first = head_at + p.low
-            turned = w_ref[:, first : first + p.wide_out - p.low].T
-            turned_ref[: high - low, :] = turned[p.skip + low : p.skip + high]
+            first = head_at + p.low + low
+            turned = w_ref[:, first : first + up(high - low + p.skip, LANES)].T
+            turned_ref[: high - low, :] = turned[p.skip : p.skip + high - low]
 
         def finish(source, lanes):
             for k in range(low // KNOT, high // KNOT, 2):
@@ -734,34 +747,28 @@
 
         return before, lambda lanes: dot(turned_ref[: high - low, :], h_refs[5][H, lanes]), finish, nothing
 
-    pipeline(
-        (nothing, fine_entry, activate(3), entry_made),
-        hidden("fine_middle", 4),
-        hidden("fine_upper", 5),
-        fore(0),
-        fore(1),
-    )
+    looped((nothing, fine_entry, activate(3), entry_made))
+    forward(hidden("fine_middle", 4, lambda: move((4, 6))), hidden("fine_upper", 5))
     h3_copy.start()
-    if groups:
-        kept = [
-            load(w_ref.at[:, p.at[name] : p.at[name] + wide], kept_out.at[:, p.at[name] : p.at[name] + wide], 10 + n)
-            for n, (name, wide) in enumerate(zip(KEPT, (p.wide_in, p.wide_out)))
-        ]
-        for copy in kept:
-            copy.start()
     cotangent_in.wait()
+    target_in.wait()
 
     def gradient_slice(name, left, right_ref, first, step=LANES, sign=1.0):
-        left_side = left[...] if name.endswith("entry") else h_refs[left][...]
-        for b in range(0, p.rows(name), step):
-            width = min(step, p.rows(name) - b)
-            value = sign * dot_rows(left_side, right_ref[aligned(first + b, width, ONES), :])
-            to = place + p.slice_at[name] + b
-            w_ref[:, to : to + width] = value[:hid].astype(BF16)
+        left_ref = left if name.endswith("entry") else h_refs[left]
+
+        def part(b):
+            value = sign * dot_rows(left_ref[...], right_ref[aligned(first + b * step, step, ONES), :])
+            w_ref[:, aligned(place + p.slice_at[name] + b * step, step, LANES)] = value[:hid].astype(BF16)
             if name in p.bias_at:
-                for c in range(0, width, LANES):
-                    row = p.bias_at[name] + (b + c) // LANES
-                    head_bias_ref[row : row + 1, :] = value[hid : hid + 1, c : c + LANES]
+                for c in range(step // LANES):
+                    row = p.bias_at[name] + b * (step // LANES) + c
+                    head_bias_ref[pl.ds(row, 1), :] = value[hid : hid + 1, c * LANES : (c + 1) * LANES]
+
+        count = p.rows(name) // step
+        if count > 1:
+            pl.loop(0, count)(part)
+        else:
+            part(0)
 
     def square_slice(name, index):
         gradient_slice(name, index - 1, g_refs[index], p.start(name, section))
@@ -779,10 +786,7 @@
         return lambda lanes: dot(w_ref[:, at : at + hid], g_refs[index][:, lanes])
 
     if groups:
-        for copy in kept:
-            copy.wait()
-        gather.sent()
-        cuts = (0, p.slice_at["fine_entry"], p.slice_at["coarse_middle"], p.slice_columns)
+        cuts = (0, p.slice_at["head_fore"], p.slice_at["fine_entry"], p.slice_at["coarse_middle"], p.slice_columns)
         width = lambda k: cuts[k + 1] - cuts[k]
 
         def arrivals(row, k):
@@ -793,6 +797,8 @@
             return w_ref.at[rows, first : first + width(k)]
 
         def departures(j, k):
+            if k == 0:
+                return gknot_ref.at[j * per : (j + 1) * per, : width(0)]
             first = (k * groups + j) * per
             return big_ref.at[first : first + per, : width(k)]
 
@@ -812,32 +818,43 @@
             keep_sems,
         )
         reduce_bias = ReduceBias(way, head_bias_ref, bias_in, bias_far, bias_out, bias_send, bias_recv)
-
-    gradient_slice("fine_head", 5, big_ref, p.start("fine_head", section), 3 * LANES, -1.0)
+        kept[0].wait()
+        gather.sent(2)
+        gather.sent(3)
+
+    gradient_slice("head_back", 5, big_ref, p.start("head_back", section), 2 * LANES, -1.0)
     if groups:
         pl.semaphore_wait(ready.at[0], len(way.all()))
         reduce.first(0)
-
-    adjoint(p.low, p.wide_out, True)
-
-    def head_used():
-        if groups:
-            signal(ready.at[1], way.all())
-            reduce.second(0)
-
-    pipeline(
-        back(5, lambda lanes: -dot(w_ref[:, head_at : head_at + p.wide_out], big_ref[:, lanes]), head_used),
-        back(4, times("fine_upper", 5)),
-        back(3, times("fine_middle", 4)),
-    )
+    complete(5, 6)
+    looped(fore(0), fore(1))
+    if groups:
+        kept.append(keep("fine_head", p.wide_out, 11))
+        kept[1].start()
+        reduce.second(0)
+
+    adjoint(p.low, p.wide_out - p.low, True)
+    looped(back(5, lambda lanes: -dot(w_ref[:, head_at : head_at + p.wide_out], big_ref[:, lanes])))
+    if groups:
+        kept[1].wait()
+        for k in (0, 1, 4, 5, 6):
+            gather.sent(k)
+        signal(ready.at[1], way.all())
+    looped(back(4, times("fine_upper", 5)))
+    gradient_slice("head_fore", 5, big_ref, p.start("head_fore", section) + p.low, LANES, -1.0)
+    square_slice("fine_upper", 5)
+    square_slice("fine_middle", 4)
+    if groups:
+        pl.semaphore_wait(ready.at[1], len(way.all()))
+        reduce.first(1)
+    looped(back(3, times("fine_middle", 4)))
     gfine_copy.start()
     gradient_slice("fine_entry", g_refs[3], r1_ref, p.start("fine_entry", section) - first_pair * p.pair, 2 * LANES)
-    square_slice("fine_middle", 4)
-    square_slice("fine_upper", 5)
-    if groups:
-        pl.semaphore_wait(ready.at[1], len(way.all()))
-        reduce.first(1)
+    if groups:
+        reduce.first(2)
+        reduce.second(1)
         reduce.third(0)
+        reduce.sent_far(0)
     gknot_ref[p.knot_rows :, :] = jnp.zeros((p.theta_wide - p.knot_rows, windows), BF16)
 
     def knots_done(source, lanes):
@@ -845,32 +862,32 @@
             rows = slice(r, r + strip)
             gknot_ref[rows, lanes] = (gtheta_ref[rows, lanes] - source[rows, :]).astype(BF16)
 
-    pipeline(
+    looped(
         (nothing, lambda lanes: dot(pw_ref[: p.knot_rows, :], g_refs[3][:, lanes]), knots_done, nothing),
-        back(
-            2,
-            lambda lanes: dot(w_ref[:, at_head : at_head + p.theta_wide], gknot_ref[:, lanes]),
-            lambda: reduce.second(1) if groups else None,
-        ),
-        back(1, times("coarse_upper", 2), lambda: reduce.fourth(0) if groups else None),
-        back(0, times("coarse_middle", 1)),
+        back(2, lambda lanes: dot(w_ref[:, at_head : at_head + p.theta_wide], gknot_ref[:, lanes])),
     )
+    if groups:
+        reduce.second(2)
+    looped(back(1, times("coarse_upper", 2)))
+    if groups:
+        reduce.fourth(0)
+    looped(back(0, times("coarse_middle", 1)))
     gradient_slice("coarse_head", 2, gknot_ref, p.start("coarse_head", section))
     gradient_slice("coarse_entry", g_refs[0], pooled_ref, p.start("coarse_entry", section))
     square_slice("coarse_middle", 1)
     square_slice("coarse_upper", 2)
     if groups:
-        reduce.first(2)
+        reduce.first(3)
         reduce_bias.to_partner().start()
         reduce.third(1)
-        reduce.second(2)
+        reduce.second(3)
         reduce_bias.second()
 
     def pool_gradient(source, lanes):
         for r in range(0, p.pool_wide, strip):
             pooled_ref[r : r + strip, lanes] = (source[r : r + strip, :] * (1.0 / POOL)).astype(BF16)
 
-    pipeline(
+    looped(
         (
             lambda: turn_weight(at_entry, p.pool_wide),
             lambda lanes: dot(turned_ref[: p.pool_wide, :], g_refs[0][:, lanes]),
@@ -884,10 +901,14 @@
         reduce_bias.third()
         reduce.third(2)
         reduce_bias.fourth()
+        reduce.third(3)
         reduce.fourth(2)
+        reduce.fourth(3)
         for k in range(reduce.chunks):
             reduce.complete(k)
             reduce.sent(k)
+            if k > 0:
+                reduce.sent_far(k)
         reduce_bias.complete()
     else:
         out = load(w_ref.at[:, place : place + p.slice_columns], slice_out, 10)
@@ -928,8 +949,8 @@
         pltpu.VMEM((p.theta_wide, hid), BF16),
         pltpu.VMEM((hid, p.theta_wide), BF16),
         pltpu.VMEM((hid, hid), BF16),
-        pltpu.VMEM((hid, min(512, windows)), F32),
-        pltpu.VMEM((hid, min(512, windows)), F32),
+        pltpu.VMEM((hid, min(512, windows // 2)), F32),
+        pltpu.VMEM((hid, min(512, windows // 2)), F32),
         pltpu.VMEM((hid, LANES), F32),
         pltpu.VMEM(horizon.shape, jnp.int32),
         pltpu.VMEM(coarse_bias.shape, F32),
@@ -945,7 +966,7 @@
             jax.ShapeDtypeStruct((4,) + bias, F32),
         ]
         out_specs += [ANY, ANY, VMEM]
-        chunks, reduce_chunks = 7, 3
+        chunks, reduce_chunks = 7, 4
         scratch += [pltpu.VMEM(piece.shape, F32) for piece in weights]
         scratch += [
             pltpu.SemaphoreType.DMA((len(weights),)),
@@ -1158,15 +1179,17 @@
     p = plan
     hid = p.hidden
 
-    def joined(name, out, source, row=None):
-        size, done = out.shape[1], 0
+    def joined(name, out, source, row=None, base=0, low=0, high=None):
+        high, done = out.shape[1] if high is None else high, low
         for section in range(p.sections):
-            first = p.start(name, section)
-            last = min(first + p.rows(name), size)
+            first = base + p.start(name, section)
+            last = min(first + p.rows(name), high)
             if row is not None:
-                for at in range(done, last, LANES):
-                    width = min(LANES, last - at)
-                    out[:, at : at + width] = source[section, pl.ds(row + (at - first) // LANES, 1), :][:, :width]
+                for at in range(max(done // LANES * LANES, first), last, LANES):
+                    begin, end = max(at, done), min(at + LANES, last)
+                    if begin < end:
+                        here = source[section, pl.ds(row + (at - first) // LANES, 1), :]
+                        out[:, begin:end] = here[:, begin - at : end - at]
             elif done < last:
                 at = p.slice_at[name] + done - first
                 out[:, done:last] = source[section, :, at : at + last - done].astype(F32)
@@ -1196,8 +1219,13 @@
         for i, name in enumerate((block + "middle", block + "upper")):
             joined(name, grads[base + 2 + 2 * i], slices_ref)
             own_part(name, grads[base + 3 + 2 * i])
-        joined(head, grads[base + 6], slices_ref)
-        joined(head, grads[base + 7], bias_rows_ref, p.bias_at[head])
+        for number, source in ((6, slices_ref), (7, bias_rows_ref)):
+            row = lambda name: p.bias_at[name] if number == 7 else None
+            if base == 0:
+                joined(head, grads[number], source, row(head))
+            else:
+                joined("head_back", grads[8 + number], source, row("head_back"), 0, 0, p.length)
+                joined("head_fore", grads[8 + number], source, row("head_fore"), p.low, p.length)
 
 
 def body(mesh_shape, history, targets, horizon, cotangent, *params):

time: 177 us -> 157 us (0.89)
  Pallas kernels: 170 us -> 150 us
    pallas_call x1, Pallas kernels: 141 us -> 121 us  [core(): pl.pallas_call(functools.partial(core_kernel, p, per, groups), out_shape=...]
where the time goes in v3:
time: 157 us; the launch traced here: 154 us
  Pallas kernels  150 us (96%)
  local copies, waits for them, and re-layouts  2.64 us (2%)
    pallas_call x1, Pallas kernels, core(): pl.pallas_call(functools.partial(core_kernel, p, per, groups), out_shape=...  121 us
    pallas_call x1, Pallas kernels, outputs(): pl.pallas_call(functools.partial(outputs_kernel, p, block, steps), grid=(...  29 us

profile of v3, /device:TPU:8, one launch (start us, length us, event | category | flops | bytes accessed | tf_op | source)
XLA Modules:
  0.0 154.4 jit_solution(11970934709970931722)
XLA Ops:
  0.7 1.3 broadcast_in_dim.27.refs_3_
  2.0 1.3 broadcast_in_dim.29.refs_5_.fine_bias_ref
  3.3 120.8 %shard_map.339 = (f32[192,1536]{1,0:T(8,128)}, bf16[512,1536]{1,0:T(8,128)(2,1)}, bf16[512,1536]{1,0:T(8,128)(2,1)}, bf16[512,1536]{1,0:T(8,128)(2,1)}, bf16[512...) custom-call(bf16[3600,1536]{1,0:T(8,128)(2,1)} %bitcast.24, bf16[3600,1536]{1,0:T(8,128)(2,1)} %bitcast.26, ...), custom_call_target="tpu_custom_call" | custom-call | flops 30383013888 | bytes 22118400 | tf_op jit(solution)/shard_map/pallas_call | solution.py:991
  124.1 29.0 %shard_map.340 = (bf16[3600,1536]{1,0:T(8,128)(2,1)}, bf16[3600,1536]{1,0:T(8,128)(2,1)}, f32[720,1536]{1,0:T(8,128)}, f32[64,450]{1,0:T(8,128)}, f32[1,64]{1,0:...) custom-call(bf16[512,11008]{1,0:T(8,128)(2,1)} %get-tuple-element.45, ...), custom_call_target="tpu_custom_call" | custom-call | flops 12457082880 | bytes 44236800 | tf_op jit(solution)/shard_map/pallas_call | solution.py:1137
  153.1 1.4 reduce

commit v4 on v3

--- a/solution.py
+++ b/solution.py
@@ -33,10 +33,10 @@
         self.pool_wide, self.theta_wide = up(pooled + 1, LANES), up(coarse_out + 1, LANES)
         widths = [
             ("coarse_entry", self.pool_wide),
+            ("bias", LANES),
             ("coarse_middle", hidden),
             ("coarse_upper", hidden),
             ("coarse_head", self.theta_wide),
-            ("bias", LANES),
             ("fine_entry", self.wide_in),
             ("fine_middle", hidden),
             ("fine_upper", hidden),
@@ -57,9 +57,9 @@
             ("fine_upper", hidden),
             ("fine_middle", hidden),
             ("fine_entry", self.wide_in),
+            ("coarse_head", self.theta_wide),
+            ("coarse_upper", hidden),
             ("coarse_middle", hidden),
-            ("coarse_upper", hidden),
-            ("coarse_head", self.theta_wide),
             ("coarse_entry", self.pool_wide),
         ):
             self.slice_at[name] = place
@@ -175,6 +175,7 @@
         self.side = [s + 1 - 2 * (s % 2), (s + 2) % 4]
         self.sides = [(t, self.dp) for t in self.side]
         self.across = 3 - s
+        self.corner = (self.across, self.dp)
 
     def far(self, j):
         group = (self.group + j) % self.groups
@@ -184,7 +185,7 @@
         return (self.group + self.groups - j) % self.groups
 
     def all(self):
-        return [self.partner] + self.sides + [self.far(j)[1] for j in range(1, self.groups)]
+        return [self.partner, self.corner] + self.sides + [self.far(j)[1] for j in range(1, self.groups)]
 
 
 class Gather:
@@ -215,6 +216,8 @@
         return self.copy(self.at(k, self.source(j), self.way.section), k, j, 1 + i, self.way.sides[i])
 
     def to_across(self, k, j):
+        if k == 0:
+            return self.copy(self.at(k, self.source(j), self.way.section), k, j, 3, self.way.corner)
         i = (k + j) % 2
         return self.copy(self.at(k, self.source(j), self.way.side[i]), k, j, 3, self.way.sides[1 - i])
 
@@ -259,12 +262,15 @@
             self.arrived(k, j, 0)
             for i in range(2):
                 self.to_side(k, j, i).start()
+            if k == 0:
+                self.to_across(k, j).start()
 
     def third(self, k):
         for j in self.near:
             self.arrived(k, j, 1)
             self.arrived(k, j, 2)
-            self.to_across(k, j).start()
+            if k > 0:
+                self.to_across(k, j).start()
 
     def fourth(self, k):
         for j in self.near:
@@ -316,15 +322,12 @@
     def to_side(self, k, i):
         here = self.stage_ref.at[:, self.columns(k)]
         there = self.out_ref.at[self.way.section, :, self.columns(k)]
-        return remote(here, there, self.send.at[k, i, 2], self.recv.at[k, i, 2], self.way.sides[i])
+        place = (self.way.sides + [self.way.corner])[i]
+        return remote(here, there, self.send.at[k, i, 2], self.recv.at[k, i, 2], place)
 
     def keep(self, k):
         there = self.out_ref.at[self.way.section, :, self.columns(k)]
         return pltpu.make_async_copy(self.stage_ref.at[:, self.columns(k)], there, self.local.at[k])
-
-    def to_across(self, k):
-        i = k % 2
-        return self.side(k, self.way.side[i], 2, self.way.sides[1 - i])
 
     def summed(self, k, group):
         own = self.part_ref(group * 2 + self.way.core, k)[...].astype(F32)
@@ -347,19 +350,13 @@
             self.to_far(k, j).wait_recv()
             total += self.far_in(j - 1, k)[...].astype(F32)
         self.stage_ref[:, self.columns(k)] = total.astype(BF16)
-        for i in range(2):
+        for i in range(3):
             self.to_side(k, i).start()
         self.keep(k).start()
 
-    def fourth(self, k):
-        i = k % 2
-        for turn in (i, 1 - i):
-            self.side(k, self.way.side[turn], turn, self.way.sides[turn]).wait_recv()
-            if turn == i:
-                self.to_across(k).start()
-
     def complete(self, k):
-        self.side(k, self.way.across, 2, self.way.partner).wait_recv()
+        for i, source in enumerate(self.way.side + [self.way.across]):
+            self.side(k, source, i, self.way.partner).wait_recv()
 
     def sent_far(self, k):
         for j in self.near:
@@ -368,9 +365,8 @@
     def sent(self, k):
         for g in range(self.way.groups):
             self.to_partner(k, g).wait_send()
-        for i in range(2):
+        for i in range(3):
             self.to_side(k, i).wait_send()
-        self.to_across(k).wait_send()
         self.keep(k).wait()
 
 
@@ -394,8 +390,8 @@
         here = self.out_ref.at[source]
         return self.copy(here, here, self.way.groups + n, to)
 
-    def to_across(self):
-        return self.side(self.way.side[0], 2, self.way.sides[1])
+    def to_side(self, i):
+        return self.side(self.way.section, i, (self.way.sides + [self.way.corner])[i])
 
     def second(self):
         self.to_partner().wait_recv()
@@ -411,22 +407,17 @@
         for g in range(1, self.way.groups):
             total += self.far_ref[g]
         self.out_ref[self.way.section] = total
-        for i in range(2):
-            self.side(self.way.section, i, self.way.sides[i]).start()
-
-    def fourth(self):
-        self.side(self.way.side[0], 0, self.way.partner).wait_recv()
-        self.to_across().start()
-        self.side(self.way.side[1], 1, self.way.partner).wait_recv()
+        for i in range(3):
+            self.to_side(i).start()
 
     def complete(self):
-        self.side(self.way.across, 2, self.way.partner).wait_recv()
+        for i, source in enumerate(self.way.side + [self.way.across]):
+            self.side(source, i, self.way.partner).wait_recv()
         self.to_partner().wait_send()
         for j in self.near:
             self.to_far(j).wait_send()
-        for i in range(2):
-            self.side(self.way.section, i, self.way.sides[i]).wait_send()
-        self.to_across().wait_send()
+        for i in range(3):
+            self.to_side(i).wait_send()
 
 
 def core_kernel(plan, per, groups, *refs):
@@ -447,7 +438,7 @@
     h_refs, g_refs = take(6), take(6)
     r1_ref, pooled_ref, split_ref, theta_ref, gtheta_ref, gknot_ref = take(6)
     pw_ref, pwt_ref, turned_ref, even_ref, odd_ref, bias_ref = take(6)
-    horizon_buf, coarse_bias_buf, fine_bias_buf, sems = take(4)
+    horizon_rows, horizon_buf, coarse_bias_buf, fine_bias_buf, sems = take(5)
     if groups:
         shards = take(14)
         shard_sems, send, recv, partner_recv = take(4)
@@ -469,7 +460,7 @@
     cotangent_in = load(cotangent_ref, big_ref.at[: p.length], 2)
     target_in = load(target_ref, big_ref.at[p.length : p.fine_out], 0)
     rows_in = [
-        load(horizon_ref, horizon_buf, 3),
+        load(horizon_ref, horizon_rows, 3),
         load(coarse_bias_ref, coarse_bias_buf, 4),
         load(fine_bias_ref, fine_bias_buf, 5),
     ]
@@ -489,7 +480,7 @@
         middle = p.at["fine_middle"]
         third = (p.columns - middle) // 3 // LANES * LANES
         entry_cut = place + up((middle - place) // 2, LANES)
-        cuts = (0, 2 * hid, place, entry_cut, middle, middle + third, middle + 2 * third, p.columns)
+        cuts = (0, p.at["coarse_middle"], place, entry_cut, middle, middle + third, middle + 2 * third, p.columns)
         gather = Gather(p, way, per, cuts, w_ref, shards[:8], shards[8:], send, recv, partner_recv)
         cotangent_in.start()
         for copy in rows_in:
@@ -531,6 +522,8 @@
         h_refs[index][hid:, :] = jnp.ones((ONES, windows), BF16)
     for copy in rows_in:
         copy.wait()
+    for n in range(windows // LANES):
+        horizon_buf[:, n * LANES : (n + 1) * LANES] = horizon_rows[n : n + 1, :]
     step = 6 * LANES
 
     def adjoint(first, count, fore):
@@ -566,9 +559,9 @@
             pooled_ref[rows, lanes] = (total * (1.0 / POOL)).astype(BF16)
 
         if number == len(firsts) // 2:
-            move((4, 0), (3, 1), (2, 2))
-    move((4, 1), (3, 2), (2, 3))
-    complete(0, 1)
+            move((4, 0))
+    move((3, 1), (2, 2))
+    complete(0)
     if not groups:
         weights_in.wait()
     fore_parts = [(0, 8 * p.pair), (8 * p.pair, p.horizon)]
@@ -649,13 +642,17 @@
             split_ref[rows, lanes] = high
             split_ref[p.theta_wide + r : p.theta_wide + r + strip, lanes] = (knots - high.astype(F32)).astype(BF16)
 
+    def coarse_rest():
+        move((4, 1), (3, 2), (2, 3))
+        complete(1)
+
     forward = pipeline if groups else looped
     forward(
         (
             nothing,
             lambda lanes: dot(w_ref[:, at_entry : at_entry + p.pool_wide], pooled_ref[:, lanes]),
             activate(0),
-            nothing,
+            coarse_rest,
         ),
         hidden("coarse_middle", 1, lambda: move((4, 2), (2, 4))),
         hidden("coarse_upper", 2, lambda: move((3, 3))),
@@ -786,7 +783,8 @@
         return lambda lanes: dot(w_ref[:, at : at + hid], g_refs[index][:, lanes])
 
     if groups:
-        cuts = (0, p.slice_at["head_fore"], p.slice_at["fine_entry"], p.slice_at["coarse_middle"], p.slice_columns)
+        cuts = (0, p.slice_at["head_fore"], p.slice_at["fine_entry"])
+        cuts += (p.slice_at["coarse_head"], p.slice_at["coarse_middle"], p.slice_columns)
         width = lambda k: cuts[k + 1] - cuts[k]
 
         def arrivals(row, k):
@@ -866,21 +864,22 @@
         (nothing, lambda lanes: dot(pw_ref[: p.knot_rows, :], g_refs[3][:, lanes]), knots_done, nothing),
         back(2, lambda lanes: dot(w_ref[:, at_head : at_head + p.theta_wide], gknot_ref[:, lanes])),
     )
-    if groups:
+    gradient_slice("coarse_head", 2, gknot_ref, p.start("coarse_head", section))
+    square_slice("coarse_upper", 2)
+    if groups:
+        reduce.first(3)
         reduce.second(2)
     looped(back(1, times("coarse_upper", 2)))
     if groups:
-        reduce.fourth(0)
-    looped(back(0, times("coarse_middle", 1)))
-    gradient_slice("coarse_head", 2, gknot_ref, p.start("coarse_head", section))
-    gradient_slice("coarse_entry", g_refs[0], pooled_ref, p.start("coarse_entry", section))
-    square_slice("coarse_middle", 1)
-    square_slice("coarse_upper", 2)
-    if groups:
-        reduce.first(3)
-        reduce_bias.to_partner().start()
         reduce.third(1)
         reduce.second(3)
+    square_slice("coarse_middle", 1)
+    looped(back(0, times("coarse_middle", 1)))
+    gradient_slice("coarse_entry", g_refs[0], pooled_ref, p.start("coarse_entry", section))
+    if groups:
+        reduce.first(4)
+        reduce_bias.to_partner().start()
+        reduce.second(4)
         reduce_bias.second()
 
     def pool_gradient(source, lanes):
@@ -897,13 +896,10 @@
     )
     pool_copy.start()
     if groups:
-        reduce.fourth(1)
+        reduce.third(2)
         reduce_bias.third()
-        reduce.third(2)
-        reduce_bias.fourth()
         reduce.third(3)
-        reduce.fourth(2)
-        reduce.fourth(3)
+        reduce.third(4)
         for k in range(reduce.chunks):
             reduce.complete(k)
             reduce.sent(k)
@@ -953,6 +949,7 @@
         pltpu.VMEM((hid, min(512, windows // 2)), F32),
         pltpu.VMEM((hid, LANES), F32),
         pltpu.VMEM(horizon.shape, jnp.int32),
+        pltpu.VMEM((1, windows), jnp.int32),
         pltpu.VMEM(coarse_bias.shape, F32),
         pltpu.VMEM(fine_bias.shape, F32),
         pltpu.SemaphoreType.DMA((13,)),
@@ -966,7 +963,7 @@
             jax.ShapeDtypeStruct((4,) + bias, F32),
         ]
         out_specs += [ANY, ANY, VMEM]
-        chunks, reduce_chunks = 7, 4
+        chunks, reduce_chunks = 7, 5
         scratch += [pltpu.VMEM(piece.shape, F32) for piece in weights]
         scratch += [
             pltpu.SemaphoreType.DMA((len(weights),)),
@@ -1241,7 +1238,7 @@
     dp_count, per = mesh_shape["dp"], c_middle.shape[0]
     rows = (history.T, cotangent.T)
     fine_bias = f_head_b[None, :]
-    rest = (targets.T, horizon[None, :], c_head_b[None, :], fine_bias)
+    rest = (targets.T, horizon.reshape(-1, LANES), c_head_b[None, :], fine_bias)
     groups = dp_count // 2
     if sections == 4 and dp_count % 2 == 0 and per % 64 == 0 and groups > 1:
         theta, h3, gfine, pool, packed, slices, bias_rows = core(

time: 157 us -> 152 us (0.968); the launches traced: 154 us -> 152 us
  no operation moved by 1% of the time
where the time goes in v4:
time: 152 us
  Pallas kernels  149 us (98%)
    pallas_call x1, Pallas kernels, core(): pl.pallas_call(functools.partial(core_kernel, p, per, groups), out_shape=...  120 us
    pallas_call x1, Pallas kernels, outputs(): pl.pallas_call(functools.partial(outputs_kernel, p, block, steps), grid=(...  29 us

profile of v4, /device:TPU:8, one launch (start us, length us, event | category | flops | bytes accessed | tf_op | source)
XLA Modules:
  0.0 152.2 jit_solution(7410410751129222248)
XLA Ops:
  0.7 1.3 broadcast_in_dim.25.refs_5_.fine_bias_ref
  2.0 119.8 %shard_map.339 = (f32[192,1536]{1,0:T(8,128)}, bf16[512,1536]{1,0:T(8,128)(2,1)}, bf16[512,1536]{1,0:T(8,128)(2,1)}, bf16[512,1536]{1,0:T(8,128)(2,1)}, bf16[512...) custom-call(bf16[3600,1536]{1,0:T(8,128)(2,1)} %bitcast.25, bf16[3600,1536]{1,0:T(8,128)(2,1)} %bitcast.27, ...), custom_call_target="tpu_custom_call" | custom-call | flops 30383013888 | bytes 22118400 | tf_op jit(solution)/shard_map/pallas_call | solution.py:988
  121.8 29.0 %shard_map.340 = (bf16[3600,1536]{1,0:T(8,128)(2,1)}, bf16[3600,1536]{1,0:T(8,128)(2,1)}, f32[720,1536]{1,0:T(8,128)}, f32[64,450]{1,0:T(8,128)}, f32[1,64]{1,0:...) custom-call(bf16[512,11008]{1,0:T(8,128)(2,1)} %get-tuple-element.45, ...), custom_call_target="tpu_custom_call" | custom-call | flops 12457082880 | bytes 44236800 | tf_op jit(solution)/shard_map/pallas_call | solution.py:1134
  150.8 1.4 reduce

commit v5 on v4

--- a/solution.py
+++ b/solution.py
@@ -429,7 +429,7 @@
         shards_in = take(14)
     else:
         (packed_ref,) = take(1)
-    theta_out, h3_out, gfine_out, pool_out = take(4)
+    theta_out, h3_out, gfine_out, pool_out, row_out = take(5)
     if groups:
         kept_out, slices_out, bias_out = take(3)
     else:
@@ -522,6 +522,9 @@
         h_refs[index][hid:, :] = jnp.ones((ONES, windows), BF16)
     for copy in rows_in:
         copy.wait()
+    for at in range(0, p.fine_out, LANES):
+        part = slice(at, min(at + LANES, p.fine_out))
+        row_out[:, part] = fine_bias_buf[part].reshape(1, part.stop - at)
     for n in range(windows // LANES):
         horizon_buf[:, n * LANES : (n + 1) * LANES] = horizon_rows[n : n + 1, :]
     step = 6 * LANES
@@ -565,7 +568,7 @@
     if not groups:
         weights_in.wait()
     fore_parts = [(0, 8 * p.pair), (8 * p.pair, p.horizon)]
-    fore_bias = column_of(fine_bias_buf, p.low, p.wide_out - p.low)
+    fore_bias = column_of(row_out, p.low, p.wide_out - p.low)
     placed = w_ref[:, p.at["bias"] : p.at["bias"] + LANES].astype(F32)
     lane = lax.broadcasted_iota(jnp.int32, (hid, LANES), 1)
     for number, (low, high) in enumerate(fore_parts):
@@ -929,8 +932,9 @@
         jax.ShapeDtypeStruct((hid, windows), BF16),
         jax.ShapeDtypeStruct((hid, windows), BF16),
         jax.ShapeDtypeStruct((p.pool_wide, windows), BF16),
+        jax.ShapeDtypeStruct((1, p.fine_out), F32),
     ]
-    out_specs = [ANY] * 4
+    out_specs = [ANY] * 4 + [VMEM]
     scratch = [
         pltpu.VMEM((hid, p.columns), BF16),
         pltpu.VMEM((p.wide_out, windows), BF16),
@@ -1059,10 +1063,13 @@
         @pl.loop(0, chunks)
         def _(n):
             lanes = lanes_of(n)
-            back_refs[0][: p.horizon, :] = dot(turned_fore[p.skip : p.skip + p.horizon], h3_ref[:, lanes])
+            for part in range(0, p.horizon, block):
+                size = min(block, p.horizon - part)
+                back_refs[part // block][:size, :] = dot(turned_fore[p.skip + part : p.skip + part + size], h3_ref[:, lanes])
             for k in range(0, p.fore, 2):
                 rows = slice(k * KNOT, (k + 2) * KNOT)
-                second = back_refs[0][rows, :] + fore_bias[p.skip + k * KNOT : p.skip + (k + 2) * KNOT]
+                here = slice(k * KNOT % block, k * KNOT % block + 2 * KNOT)
+                second = back_refs[k * KNOT // block][here, :] + fore_bias[p.skip + k * KNOT : p.skip + (k + 2) * KNOT]
                 first = jnp.concatenate([interpolate(k + j, p.fore, p.back, lanes) for j in range(2)], axis=0)
                 fore_ref[rows, lanes] = first.astype(BF16).astype(F32) + second.astype(BF16).astype(F32)
 
@@ -1122,7 +1129,7 @@
 def outputs(plan, packed, history, cotangent, theta, h3, gfine, pool, fine_bias, slices, bias_rows):
     p = plan
     hid, windows = p.hidden, p.windows
-    block = 6 * LANES
+    block = 3 * LANES
     steps = -(-p.length // block)
     rows = pl.BlockSpec((block, windows), lambda i: (i, 0))
     wide = p.wide_out - p.low
@@ -1131,6 +1138,7 @@
     grads = []
     for entry, out in ((p.pooled, p.coarse_out), (p.length, p.fine_out)):
         grads += [(per, entry), vector, square, vector, square, vector, (per, out), (1, out)]
+    grads[-1] = (p.fine_out,)
     return pl.pallas_call(
         functools.partial(outputs_kernel, p, block, steps),
         grid=(steps,),
@@ -1177,7 +1185,7 @@
     hid = p.hidden
 
     def joined(name, out, source, row=None, base=0, low=0, high=None):
-        high, done = out.shape[1] if high is None else high, low
+        high, done = out.shape[-1] if high is None else high, low
         for section in range(p.sections):
             first = base + p.start(name, section)
             last = min(first + p.rows(name), high)
@@ -1186,7 +1194,11 @@
                     begin, end = max(at, done), min(at + LANES, last)
                     if begin < end:
                         here = source[section, pl.ds(row + (at - first) // LANES, 1), :]
-                        out[:, begin:end] = here[:, begin - at : end - at]
+                        here = here[:, begin - at : end - at]
+                        if len(out.shape) == 1:
+                            out[begin:end] = here.reshape(end - begin)
+                        else:
+                            out[:, begin:end] = here
             elif done < last:
                 at = p.slice_at[name] + done - first
                 out[:, done:last] = source[section, :, at : at + last - done].astype(F32)
@@ -1222,7 +1234,7 @@
                 joined(head, grads[number], source, row(head))
             else:
                 joined("head_back", grads[8 + number], source, row("head_back"), 0, 0, p.length)
-                joined("head_fore", grads[8 + number], source, row("head_fore"), p.low, p.length)
+                joined("head_fore", grads[8 + number], source, row("head_fore"), p.low, p.length, p.fine_out)
 
 
 def body(mesh_shape, history, targets, horizon, cotangent, *params):
@@ -1237,24 +1249,23 @@
     bias_pieces = (c_entry_b, c_middle_b, c_upper_b, f_entry_b, f_middle_b, f_upper_b)
     dp_count, per = mesh_shape["dp"], c_middle.shape[0]
     rows = (history.T, cotangent.T)
-    fine_bias = f_head_b[None, :]
-    rest = (targets.T, horizon.reshape(-1, LANES), c_head_b[None, :], fine_bias)
+    rest = (targets.T, horizon.reshape(-1, LANES), c_head_b[None, :], f_head_b)
     groups = dp_count // 2
     if sections == 4 and dp_count % 2 == 0 and per % 64 == 0 and groups > 1:
-        theta, h3, gfine, pool, packed, slices, bias_rows = core(
+        theta, h3, gfine, pool, fine_bias, packed, slices, bias_rows = core(
             p, per, groups, *rows, *rest, pieces + tuple(b[None, :] for b in bias_pieces)
         )
     else:
         packed = pack(p, dict(zip(NAMES, pieces)), jnp.stack(bias_pieces, axis=1))
         packed = lax.all_gather(packed, "dp", axis=0, tiled=True)
-        theta, h3, gfine, pool, part, head_bias = core(p, per, 0, *rows, *rest, (packed,))
+        theta, h3, gfine, pool, fine_bias, part, head_bias = core(p, per, 0, *rows, *rest, (packed,))
         own = lax.psum_scatter(part.astype(F32), "dp", scatter_dimension=0, tiled=True)
         slices = lax.all_gather(own, "section", axis=0)
         bias_rows = lax.all_gather(lax.psum(head_bias, "dp"), "section", axis=0)
     residual, history_grad, prediction, *grads = outputs(
         p, packed, *rows, theta, h3, gfine, pool, fine_bias, slices, bias_rows
     )
-    grads = [g.T if i in (0, 8) else g if g.shape[0] > 1 else g[0] for i, g in enumerate(grads)]
+    grads = [g.T if i in (0, 8) else g[0] if g.shape[0] == 1 else g for i, g in enumerate(grads)]
     return (prediction.T, residual.T, history_grad.T) + tuple(grads)
 
 

time: 152 us -> 151 us (level)
  no operation moved by 1% of the time
where the time goes in v5:
time: 151 us
  Pallas kernels  150 us (99%)
    pallas_call x1, Pallas kernels, core(): pl.pallas_call(functools.partial(core_kernel, p, per, groups), out_shape=...  120 us
    pallas_call x1, Pallas kernels, outputs(): pl.pallas_call(functools.partial(outputs_kernel, p, block, steps), grid=(...  30.2 us

profile of v5, /device:TPU:8, one launch (start us, length us, event | category | flops | bytes accessed | tf_op | source)
XLA Modules:
  0.0 150.9 jit_solution(13670862489222296072)
XLA Ops:
  0.7 119.9 %shard_map.339 = (f32[192,1536]{1,0:T(8,128)}, bf16[512,1536]{1,0:T(8,128)(2,1)}, bf16[512,1536]{1,0:T(8,128)(2,1)}, bf16[512,1536]{1,0:T(8,128)(2,1)}, f32[1,43...) custom-call(bf16[3600,1536]{1,0:T(8,128)(2,1)} %bitcast.25, ...), custom_call_target="tpu_custom_call" | custom-call | flops 30383013888 | bytes 22118400 | tf_op jit(solution)/shard_map/pallas_call | solution.py:992
  120.5 30.2 %shard_map.340 = (bf16[3600,1536]{1,0:T(8,128)(2,1)}, bf16[3600,1536]{1,0:T(8,128)(2,1)}, f32[720,1536]{1,0:T(8,128)}, f32[64,450]{1,0:T(8,128)}, f32[1,64]{1,0:...) custom-call(bf16[512,11008]{1,0:T(8,128)(2,1)} %get-tuple-element.46, ...), custom_call_target="tpu_custom_call" | custom-call | flops 12457082880 | bytes 44236800 | tf_op jit(solution)/shard_map/pallas_call | solution.py:1142

commit v6 on v5

--- a/solution.py
+++ b/solution.py
@@ -1020,7 +1020,7 @@
     *refs,
 ):
     grads = refs[:16]
-    head_ref, entry_ref, side_ref, pool_grad, fore_ref, *products, turned_head, turned_entry, bias_ref, sems = refs[16:]
+    head_ref, entry_ref, side_ref, pool_in, slices_in, pool_grad, fore_ref, *products, turned_head, turned_entry, bias_ref, sems = refs[16:]
     back_refs, fine_refs = products[:2], products[2:]
     p = plan
     step = pl.program_id(0)
@@ -1046,13 +1046,16 @@
     wide = p.wide_out - p.low
     first_fore = p.at["fine_head"] + p.low
     side = pltpu.make_async_copy(packed_ref.at[:, first_fore : first_fore + wide], side_ref, sems.at[2, 0])
+    pool_copy = pltpu.make_async_copy(pool_ref, pool_in, sems.at[2, 1])
+    slices_copy = pltpu.make_async_copy(slices_ref, slices_in, sems.at[3, 1])
 
     @pl.when(step == 0)
     def _():
         fetch("fine_head", head_ref, 0, 0, 0).start()
         fetch("fine_entry", entry_ref, 0, 0, 1).start()
+        pool_copy.start()
         side.start()
-        pool_grad[...] = pool_ref[...].astype(F32)
+        slices_copy.start()
 
     @pl.when(step == 2)
     def _():
@@ -1077,7 +1080,8 @@
 
     @pl.when(step == 1)
     def _():
-        unpack(p, slices_ref, bias_rows_ref, grads)
+        slices_copy.wait()
+        unpack(p, slices_in, bias_rows_ref, grads)
 
     slot = step % 2
 
@@ -1090,6 +1094,12 @@
     fetch("fine_entry", entry_ref, step, slot, 1).wait()
     turned_head[...] = head_ref[slot].T
     turned_entry[...] = entry_ref[slot].T
+
+    @pl.when(step == 0)
+    def _():
+        pool_copy.wait()
+        pool_grad[...] = pool_in[...].astype(F32)
+
     row = jnp.broadcast_to(fine_bias_ref[:, aligned(step * block, block, LANES)], (8, block))
     bias_ref[...] = row.T[:, :1]
     pair = 2 * KNOT
@@ -1129,7 +1139,7 @@
 def outputs(plan, packed, history, cotangent, theta, h3, gfine, pool, fine_bias, slices, bias_rows):
     p = plan
     hid, windows = p.hidden, p.windows
-    block = 3 * LANES
+    block = 6 * LANES
     steps = -(-p.length // block)
     rows = pl.BlockSpec((block, windows), lambda i: (i, 0))
     wide = p.wide_out - p.low
@@ -1148,12 +1158,14 @@
             jax.ShapeDtypeStruct((p.horizon, windows), F32),
         )
         + tuple(jax.ShapeDtypeStruct(shape, F32) for shape in grads),
-        in_specs=[ANY, rows, rows, VMEM, VMEM, VMEM, VMEM, VMEM, VMEM, VMEM],
+        in_specs=[ANY, rows, rows, VMEM, VMEM, VMEM, ANY, VMEM, ANY, VMEM],
         out_specs=(rows, rows, ANY) + (VMEM,) * len(grads),
         scratch_shapes=[
             pltpu.VMEM((2, hid, block), BF16),
             pltpu.VMEM((2, hid, block), BF16),
             pltpu.VMEM((hid, wide), BF16),
+            pltpu.VMEM(pool.shape, BF16),
+            pltpu.VMEM(slices.shape, slices.dtype),
             pltpu.VMEM((p.pool_wide, windows), F32),
             pltpu.VMEM((p.horizon, windows), F32),
             *[pltpu.VMEM((block, min(512, windows)), F32)] * 4,

time: 151 us -> 150 us (level)
  no operation moved by 1% of the time
where the time goes in v6:
time: 150 us
  Pallas kernels  149 us (99%)
    pallas_call x1, Pallas kernels, core(): pl.pallas_call(functools.partial(core_kernel, p, per, groups), out_shape=...  120 us
    pallas_call x1, Pallas kernels, outputs(): pl.pallas_call(functools.partial(outputs_kernel, p, block, steps), grid=(...  29.4 us

profile of v6, /device:TPU:8, one launch (start us, length us, event | category | flops | bytes accessed | tf_op | source)
XLA Modules:
  0.0 150.1 jit_solution(7822366518312684855)
XLA Ops:
  0.7 119.9 %shard_map.339 = (f32[192,1536]{1,0:T(8,128)}, bf16[512,1536]{1,0:T(8,128)(2,1)}, bf16[512,1536]{1,0:T(8,128)(2,1)}, bf16[512,1536]{1,0:T(8,128)(2,1)}, f32[1,43...) custom-call(bf16[3600,1536]{1,0:T(8,128)(2,1)} %bitcast.25, ...), custom_call_target="tpu_custom_call" | custom-call | flops 30383013888 | bytes 22118400 | tf_op jit(solution)/shard_map/pallas_call | solution.py:992
  120.5 29.4 %shard_map.340 = (bf16[3600,1536]{1,0:T(8,128)(2,1)}, bf16[3600,1536]{1,0:T(8,128)(2,1)}, f32[720,1536]{1,0:T(8,128)}, f32[64,450]{1,0:T(8,128)}, f32[1,64]{1,0:...) custom-call(bf16[512,11008]{1,0:T(8,128)(2,1)} %get-tuple-element.46, ...), custom_call_target="tpu_custom_call" | custom-call | flops 12457082880 | bytes 44236800 | tf_op jit(solution)/shard_map/pallas_call | solution.py:1152
